TPU v7x, 32 devices: a whole 2x2x4 slice. The times are simulated.
32 devices in a mesh: expert: 8 (over y, x, core), edata: 4 (over z).
Axes of the slice: x: 2, y: 2, z: 4, core: 2. Of those that a mesh axis runs over, the one named last changes fastest.
Arguments:
- out_grad: bfloat16 [16384, 4096], P(('expert', 'edata')), may hold values from -0.8984375 to 0.8984375
- hidden_saved: bfloat16 [16384, 768], P(('expert', 'edata')), may hold values from -6 to 6
- recv_counts: int32 [256], P(('expert', 'edata')), may hold values from 1 to 64, as said below
- master_weight: float32 [32768, 768], P(('expert', 'edata'))
- moment_one: bfloat16 [32768, 768], P(('expert', 'edata')), may hold values from -4 to 4
- moment_two: bfloat16 [32768, 768], P(('expert', 'edata')), may hold values from 0.049804688 to 0.5
Outputs:
- new_master: float32 [32768, 768], P(('expert', 'edata'))
- new_moment_one: bfloat16 [32768, 768], P(('expert', 'edata'))
- new_moment_two: bfloat16 [32768, 768], P(('expert', 'edata'))
- scaled_weight: bfloat16 [32768, 768], P('expert')
- expert_peak: float32 [8], P('expert')
Inputs may be any that keep to these rules, and one draw needn't show every extreme that they name: `recv_counts`: counts are skewed over experts; in every draw some pair fills all 64 slots.
All inputs are finite; a program needn't handle non-finite values. Where the computation divides by a largest or mean magnitude, that divisor is 1e-20 or more.
Results may differ from a plain program's by a relative error of at most 0.001.
Values may be sent and summed in bfloat16 or wider, within the bound.
No kernel may reach another device: no remote copies, remote signals or barrier semaphores. Data moves between devices by JAX's collectives and lax.ppermute only.
A program may use at most 128 MiB of HBM per device.

v0:
```python
import jax
import jax.numpy as jnp
from jax import lax
from jax.sharding import PartitionSpec as P

beta_one = 0.9
beta_two = 0.999
correct_one = 1.0 - 0.9**5
correct_two = 1.0 - 0.999**5
adam_eps = 1e-08
learn_rate = 0.05
weight_decay = 1.0
peak_eps = 1e-06


def local(out_grad, hidden_saved, recv_counts, master_weight, moment_one, moment_two):
    experts = lax.axis_size("expert")
    capacity = out_grad.shape[0] // experts
    arrived = lax.all_to_all(out_grad, "expert", split_axis=0, concat_axis=0, tiled=True)
    slots = jnp.arange(capacity)
    live = (slots[None, :] < recv_counts[:, None]).reshape(-1)
    masked = jnp.where(live[:, None], arrived, jnp.zeros((), jnp.bfloat16))
    grad = lax.psum_scatter(
        lax.dot_general(
            masked, hidden_saved, (((0,), (0,)), ((), ())), preferred_element_type=jnp.float32
        ),
        "edata",
        scatter_dimension=0,
        tiled=True,
    )
    first = beta_one * moment_one.astype(jnp.float32) + (1.0 - beta_one) * grad
    second = beta_two * moment_two.astype(jnp.float32) + (1.0 - beta_two) * grad * grad
    update = first / correct_one / (jnp.sqrt(second / correct_two) + adam_eps)
    new_master = master_weight - learn_rate * (update + weight_decay * master_weight)
    local_peak = jnp.max(jnp.abs(new_master))
    peak = lax.pmax(local_peak, "edata")
    scaled_shard = (new_master / (peak + peak_eps)).astype(jnp.bfloat16)
    scaled = lax.all_gather(scaled_shard, "edata", axis=0, tiled=True)
    return (
        new_master,
        first.astype(jnp.bfloat16),
        second.astype(jnp.bfloat16),
        scaled,
        peak.reshape(1),
    )


def solution(mesh):
    placed = (
        P(("expert", "edata"), None),
        P(("expert", "edata"), None),
        P(("expert", "edata")),
        P(("expert", "edata"), None),
        P(("expert", "edata"), None),
        P(("expert", "edata"), None),
    )
    return jax.shard_map(
        local,
        mesh=mesh,
        in_specs=placed,
        out_specs=(
            P(("expert", "edata"), None),
            P(("expert", "edata"), None),
            P(("expert", "edata"), None),
            P("expert", None),
            P("expert"),
        ),
        check_vma=False,
    )
```

profile of v0, /device:TPU:0, one launch (start us, length us, event | category | flops | bytes accessed | tf_op | source)
XLA Modules:
  0.0 432.7 jit_solution(14772641992098723860)
XLA Ops:
  7.2 0.0 copy-start
  7.2 0.0 copy-start.2
  7.2 5.3 %all-to-all-start = ((bf16[8,64,4096]{2,1,0:T(8,128)(2,1)}), bf16[8,64,4096]{2,1,0:T(8,128)(2,1)}, u32[]{:S(2)}, u32[]{:S(2)}) async-start(bf16[8,64,4096]{2,1,0:T(8,128)(2,1)} %bitcast.6), calls=%async_computation | async-start | bytes 8388608 | tf_op jit(solution)/shard_map/all_to_all | solution.py:19
  12.5 0.0 reduce-scatter.2.cloned.1.call-start
  12.5 0.0 copy-done.2
  12.6 0.1 iota_compare_fusion
  12.6 0.1 lt.23
  12.7 49.0 %all-to-all-done = bf16[8,64,4096]{2,1,0:T(8,128)(2,1)} async-done(((bf16[8,64,4096]{2,1,0:T(8,128)(2,1)}), bf16[8,64,4096]{2,1,0:T(8,128)(2,1)}, u32[]{:S(2)}, u32[]{:S(2)}) %all-to-all-start) | async-done | bytes 4194336 | tf_op jit(solution)/shard_map/all_to_all | solution.py:19
  61.7 2.5 bitcast_select_fusion
  64.3 0.0 copy-done
  64.3 6.4 %fusion.3 = f32[4096,768]{1,0:T(8,128)} fusion(bf16[512,4096]{1,0:T(8,128)(2,1)S(1)} %bitcast_select_fusion, bf16[512,768]{1,0:T(8,128)(2,1)S(1)} %copy-done), kind=kOutput, calls=%fused_computation.10 | convolution fusion | flops 3221225472 | bytes 17563648 | tf_op jit(solution)/shard_map/dot_general | solution.py:24
  70.7 0.0 copy-start.1
  70.7 0.0 reduce-scatter.2.cloned.1.call-update
  70.7 0.0 all-gather.2.cloned.1.call-start
  70.8 212.1 %reduce-scatter.2.cloned.1.call-done = f32[1024,768]{1,0:T(8,128)} async-done(((f32[4096,768]{1,0:T(8,128)}), f32[1024,768]{1,0:T(8,128)}) %reduce-scatter.2.cloned.1.call-update) | async-done | bytes 3145744 | tf_op jit(solution)/shard_map/reduce_scatter | solution.py:23
  282.9 0.0 copy-done.1
  282.9 7.2 %abs_reduce_fusion = (f32[]{:T(128)}, f32[1024,768]{1,0:T(8,128)}, bf16[1024,768]{1,0:T(8,128)(2,1)}, bf16[1024,768]{1,0:T(8,128)(2,1)}) fusion(f32[1024,768]{1,0:T(8,128)} %param.9, f32[1024,768]{1,0:T(8,128)} %reduce-scatter.2.cloned.1.call-done, bf16[1024,768]{1,0:T(8,128)(2,1)S(1)} %copy-done.1, bf16[1024,768]{1,0:T(8,128)(2,1)} %param.10), kind=kLoop, calls=%fused_computation.4 | loop fusion | flops 15728639 | bytes 15728644 | tf_op jit(solution)/shard_map/reduce_max | solution.py:35
  290.1 12.1 %pmax.7 = f32[]{:T(128)} all-reduce(f32[]{:T(128)} %get-tuple-element.5), channel_id=1, replica_groups=mesh['expert'=8,'edata'=4] {'edata'}, use_global_device_ids=true, to_apply=%region_2.3 | all-reduce | flops 1 | bytes 8 | tf_op jit(solution)/shard_map/pmax | solution.py:36
  302.8 3.3 divide_convert_fusion
  306.0 0.0 all-gather.2.cloned.1.call-update
  306.1 113.9 %all-gather.2.cloned.1.call-done = bf16[4096,768]{1,0:T(8,128)(2,1)} async-done(((bf16[1024,768]{1,0:T(8,128)(2,1)}), bf16[4096,768]{1,0:T(8,128)(2,1)}) %all-gather.2.cloned.1.call-update) | async-done | bytes 6291472 | tf_op jit(solution)/shard_map/all_gather | solution.py:38
  419.9 5.9 %copy.12 = bf16[4096,768]{1,0:T(8,128)(2,1)} copy(bf16[4096,768]{1,0:T(8,128)(2,1)} %all-gather.2.cloned.1.call-done) | data formatting | bytes 12582912
Async XLA Ops:
  7.2 57.1 %copy-start = (bf16[512,768]{1,0:T(8,128)(2,1)S(1)}, bf16[512,768]{1,0:T(8,128)(2,1)}, u32[]{:S(2)}) copy-start(bf16[512,768]{1,0:T(8,128)(2,1)} %param.7) | copy-start | bytes 2359300
  7.2 5.4 %copy-start.2 = (s32[8]{0:T(128)S(1)}, s32[8]{0:T(128)}, u32[]{:S(2)}) copy-start(s32[8]{0:T(128)} %param.8) | copy-start | bytes 100
  7.2 54.5 %all-to-all-start = ((bf16[8,64,4096]{2,1,0:T(8,128)(2,1)}), bf16[8,64,4096]{2,1,0:T(8,128)(2,1)}, u32[]{:S(2)}, u32[]{:S(2)}) async-start(bf16[8,64,4096]{2,1,0:T(8,128)(2,1)} %bitcast.6), calls=%async_computation | async-start | bytes 8388608 | tf_op jit(solution)/shard_map/all_to_all | solution.py:19
  12.5 270.4 %reduce-scatter.2.cloned.1.call-start = ((), (), s32[]{:S(2)}) async-start(), calls=%async_computation.2 | async-start | bytes 15728640 | tf_op jit(solution)/shard_map/reduce_scatter | solution.py:23
  70.7 212.2 %copy-start.1 = (bf16[1024,768]{1,0:T(8,128)(2,1)S(1)}, bf16[1024,768]{1,0:T(8,128)(2,1)}, u32[]{:S(2)}) copy-start(bf16[1024,768]{1,0:T(8,128)(2,1)} %param.11) | copy-start | bytes 4718596
  70.7 349.2 %all-gather.2.cloned.1.call-start = ((), (), s32[]{:S(2)}) async-start(), calls=%async_computation.3 | async-start | bytes 7864320 | tf_op jit(solution)/shard_map/all_gather | solution.py:38
Sparse Core Ops, SparseCore 0:
  70.9 211.9 reduce-scatter.1
  306.2 113.7 all-gather.1
where the time goes:
time: 433 us
  waiting for transfers between devices  375 us (87%)
  between operations  14.7 us (3%)
  other arithmetic  13 us (3%)
  blocking collectives  12.1 us (3%)
  matrix products  6.44 us (1%)
  local copies, waits for them, and re-layouts  6 us (1%)
  starting transfers between devices  5.39 us (1%)
    reduce_scatter x1, waiting for transfers between devices, local(): lax.psum_scatter(lax.dot_general(masked, hidden_saved, (((0,), (0,)), (()...  212 us
    all_gather x1, waiting for transfers between devices, local(): scaled = lax.all_gather(scaled_shard, 'edata', axis=0, tiled=True)  114 us
    all_to_all x1, waiting for transfers between devices, local(): lax.all_to_all(out_grad, 'expert', split_axis=0, concat_axis=0, tiled=True)  49 us
    pmax x1, blocking collectives, local(): peak = lax.pmax(local_peak, 'edata')  12.1 us
  transfers between devices with their start and end apart: 3, of which 3 were waited for; matrix products, arithmetic and copies ran while one was open for 0% of the time, Pallas kernels for 0%

commit v1 on v0

v1 whole, which is shorter than its diff:
```python
import functools
import jax
import jax.numpy as jnp
from jax import lax
from jax.experimental import pallas as pl
from jax.experimental.pallas import tpu as pltpu
from jax.sharding import PartitionSpec as P

beta_one = 0.9
beta_two = 0.999
correct_one = 1.0 - 0.9**5
correct_two = 1.0 - 0.999**5
adam_eps = 1e-08
learn_rate = 0.05
weight_decay = 1.0
peak_eps = 1e-06

VMEM_LIMIT = 40 * 1024 * 1024
LEVELS = 32000.0
TAIL = 16


def params():
    return pltpu.CompilerParams(vmem_limit_bytes=VMEM_LIMIT)


def pick_kernel(table_ref, x_ref, o_ref):
    o_ref[...] = x_ref[...]


def pick_columns(x, starts, width):
    rows = x.shape[0]
    count = starts.shape[0]
    return pl.pallas_call(
        pick_kernel,
        out_shape=jax.ShapeDtypeStruct((rows, count * width), x.dtype),
        grid_spec=pltpu.PrefetchScalarGridSpec(
            num_scalar_prefetch=1,
            grid=(count, 2),
            in_specs=[pl.BlockSpec((rows // 2, width), lambda i, j, table: (j, table[i]))],
            out_specs=pl.BlockSpec((rows // 2, width), lambda i, j, table: (j, i)),
        ),
        compiler_params=params(),
        cost_estimate=pl.CostEstimate(
            flops=0, bytes_accessed=4 * rows * count * width, transcendentals=0
        ),
        name="pick_columns",
    )(starts, x)


def contract(rows_ref, hidden_ref):
    return lax.dot_general(
        rows_ref[...],
        hidden_ref[...],
        (((0,), (0,)), ((), ())),
        preferred_element_type=jnp.float32,
    )


def code_kernel(count, *refs):
    rows, hidden, out = refs[:count], refs[count : 2 * count], refs[2 * count]
    total = contract(rows[0], hidden[0])
    for k in range(1, count):
        total = total + contract(rows[k], hidden[k])
    block = total.shape[0]
    top = jnp.maximum(jnp.max(jnp.abs(total), axis=0, keepdims=True), 1e-30)
    exponent = jnp.floor(jnp.log2(top)) + 1.0
    step = jnp.exp2(exponent) * (1.0 / LEVELS)
    codes = jnp.round(total * (1.0 / step))
    out[0, :block, :] = codes.astype(jnp.int32).astype(jnp.int16)
    out[0, block:, :] = jnp.broadcast_to(
        exponent.astype(jnp.int32), (TAIL, total.shape[1])
    ).astype(jnp.int16)


def coded_sum(rows, offsets, hidden, width, block):
    count = len(rows)
    depth, ffn = hidden[0].shape
    blocks = width // block
    specs = [
        pl.BlockSpec((depth, block), functools.partial(lambda o, i: (0, o + i), off // block))
        for off in offsets
    ]
    return pl.pallas_call(
        functools.partial(code_kernel, count),
        out_shape=jax.ShapeDtypeStruct((blocks, block + TAIL, ffn), jnp.int16),
        grid=(blocks,),
        in_specs=specs + [pl.BlockSpec((depth, ffn), lambda i: (0, 0))] * count,
        out_specs=pl.BlockSpec((1, block + TAIL, ffn), lambda i: (i, 0, 0)),
        compiler_params=params(),
        cost_estimate=pl.CostEstimate(
            flops=2 * count * depth * width * ffn,
            bytes_accessed=2 * (count * depth * (width + ffn) + width * ffn),
            transcendentals=0,
        ),
        name="coded_sum",
    )(*rows, *hidden)


def adam_kernel(count, aliased, *refs):
    rows, hidden = refs[:count], refs[count : 2 * count]
    coded, master, one, two = refs[2 * count : 2 * count + 4]
    outs = refs[2 * count + 4 + aliased :]
    new_master_ref, new_one_ref, new_two_ref, top_ref = outs
    block = master.shape[0]
    step = jnp.exp2(coded[0, block : block + 1, :].astype(jnp.int32).astype(jnp.float32)) * (
        1.0 / LEVELS
    )
    grad = coded[0, :block, :].astype(jnp.int32).astype(jnp.float32) * step
    for k in range(count):
        grad = grad + contract(rows[k], hidden[k])
    first = beta_one * one[...].astype(jnp.float32) + (1.0 - beta_one) * grad
    second = beta_two * two[...].astype(jnp.float32) + (1.0 - beta_two) * grad * grad
    update = first / correct_one / (jnp.sqrt(second / correct_two) + adam_eps)
    weight = master[...]
    new_master = weight - learn_rate * (update + weight_decay * weight)
    new_master_ref[...] = new_master
    new_one_ref[...] = first.astype(jnp.bfloat16)
    new_two_ref[...] = second.astype(jnp.bfloat16)
    top = jnp.max(jnp.abs(new_master), axis=0, keepdims=True)

    @pl.when(pl.program_id(0) == 0)
    def _():
        top_ref[...] = top

    @pl.when(pl.program_id(0) > 0)
    def _():
        top_ref[...] = jnp.maximum(top_ref[...], top)


def adam(rows, offsets, hidden, coded, master, one, two, at, block, earlier=()):
    count = len(rows)
    depth, ffn = hidden[0].shape
    blocks = coded.shape[0]
    shard = master.shape[0]
    first_block = at // block
    specs = [
        pl.BlockSpec((depth, block), functools.partial(lambda o, i: (0, o + i), off // block))
        for off in offsets
    ]
    here = pl.BlockSpec((block, ffn), lambda i: (first_block + i, 0))
    whole = pl.BlockSpec(memory_space=pl.ANY)
    operands = 2 * count + 4
    return pl.pallas_call(
        functools.partial(adam_kernel, count, len(earlier)),
        out_shape=(
            jax.ShapeDtypeStruct((shard, ffn), jnp.float32),
            jax.ShapeDtypeStruct((shard, ffn), jnp.bfloat16),
            jax.ShapeDtypeStruct((shard, ffn), jnp.bfloat16),
            jax.ShapeDtypeStruct((1, ffn), jnp.float32),
        ),
        grid=(blocks,),
        in_specs=specs
        + [pl.BlockSpec((depth, ffn), lambda i: (0, 0))] * count
        + [pl.BlockSpec((1, block + TAIL, ffn), lambda i: (i, 0, 0)), here, here, here]
        + [whole] * len(earlier),
        out_specs=(here, here, here, pl.BlockSpec((1, ffn), lambda i: (0, 0))),
        input_output_aliases={operands + k: k for k in range(len(earlier))},
        compiler_params=params(),
        cost_estimate=pl.CostEstimate(
            flops=2 * count * depth * blocks * block * ffn,
            bytes_accessed=blocks * block * ffn * 18,
            transcendentals=0,
        ),
        name="adam",
    )(*rows, *hidden, coded, master, one, two, *earlier)


def local(out_grad, hidden_saved, recv_counts, master_weight, moment_one, moment_two):
    experts = lax.axis_size("expert")
    replicas = lax.axis_size("edata")
    me = lax.axis_index("edata")
    half = replicas // 2
    group = range(1, half)
    capacity = out_grad.shape[0] // experts
    shard = master_weight.shape[0]
    parts = 2
    width = shard // parts
    block = min(256, width)

    def swap(x, k):
        return lax.ppermute(x, "edata", [(i, i ^ k) for i in range(replicas)])

    live = (jnp.arange(capacity)[None, :] < recv_counts[:, None]).reshape(-1)
    hidden = jnp.where(live[:, None], hidden_saved, jnp.zeros((), jnp.bfloat16))
    hiddens = [hidden] + [swap(hidden, k) for k in group]

    def arrive(targets):
        starts = jnp.stack([d * parts + p for d, p in targets]).astype(jnp.int32)
        picked = pick_columns(out_grad, starts, width)
        return lax.all_to_all(picked, "expert", split_axis=0, concat_axis=0, tiled=True)

    coded = []
    for p in range(parts):
        got = arrive([(me ^ half ^ k, p) for k in range(half)])
        rows = [got] + [swap(got[:, k * width : (k + 1) * width], k) for k in group]
        coded.append(swap(coded_sum(rows, [0] * half, hiddens, width, block), half))

    results, tops = (), []
    got = arrive([(me ^ k, p) for k in range(half) for p in range(parts)])
    rows = [got] + [swap(got[:, k * shard : (k + 1) * shard], k) for k in group]
    for p in range(parts):
        *results, top = adam(
            rows,
            [p * width] * half,
            hiddens,
            coded[p],
            master_weight,
            moment_one,
            moment_two,
            p * width,
            block,
            tuple(results),
        )
        tops.append(top)
    new_master, new_one, new_two = results

    peak = functools.reduce(jnp.maximum, [jnp.max(top) for top in tops]).reshape(1)
    step = 1
    while step < replicas:
        peak = jnp.maximum(peak, swap(peak, step))
        step *= 2

    pieces = 2
    rows_of = shard // pieces
    own = [
        (new_master[i * rows_of : (i + 1) * rows_of] / (peak + peak_eps)).astype(jnp.bfloat16)
        for i in range(pieces)
    ]
    scaled = jnp.zeros((replicas * shard, new_master.shape[1]), jnp.bfloat16)

    def place(scaled, piece, source, i, valid=None):
        at = (source * shard + i * rows_of, 0)
        if valid is not None:
            piece = jnp.where(valid, piece, lax.dynamic_slice(scaled, at, piece.shape))
        return lax.dynamic_update_slice(scaled, piece, at)

    for i in range(pieces):
        scaled = place(scaled, own[i], me, i)
    down, up = list(own), list(own)
    for s in range(1, replicas):
        for i in range(pieces):
            down[i] = lax.ppermute(down[i], "edata", [(j, j - 1) for j in range(1, replicas)])
            up[i] = lax.ppermute(up[i], "edata", [(j, j + 1) for j in range(replicas - 1)])
        for i in range(pieces):
            scaled = place(scaled, down[i], jnp.minimum(me + s, replicas - 1), i, me + s < replicas)
            scaled = place(scaled, up[i], jnp.maximum(me - s, 0), i, me - s >= 0)
    return new_master, new_one, new_two, scaled, peak


def solution(mesh):
    placed = (
        P(("expert", "edata"), None),
        P(("expert", "edata"), None),
        P(("expert", "edata")),
        P(("expert", "edata"), None),
        P(("expert", "edata"), None),
        P(("expert", "edata"), None),
    )
    return jax.shard_map(
        local,
        mesh=mesh,
        in_specs=placed,
        out_specs=(
            P(("expert", "edata"), None),
            P(("expert", "edata"), None),
            P(("expert", "edata"), None),
            P("expert", None),
            P("expert"),
        ),
        check_vma=False,
    )
```

time: 433 us -> 308 us (0.71)
  waiting for transfers between devices: 375 us -> 159 us
  starting transfers between devices: 5.39 us -> 60.1 us
  Pallas kernels: 0 us -> 22.6 us
  local copies, waits for them, and re-layouts: 6 us -> 27.5 us
  other arithmetic: 13 us -> 31.8 us
  blocking collectives: 12.1 us -> 0 us
  between operations: 14.7 us -> 4.88 us
  matrix products: 6.44 us -> 0 us
    reduce_scatter x1 -> x0, waiting for transfers between devices: 212 us -> none  [local(): lax.psum_scatter(lax.dot_general(masked, hidden_saved, (((0,), (0,)), (()...]
    ppermute x0 -> x20, waiting for transfers between devices: none -> 120 us  [the longest x8 75.4 us: swap(): return lax.ppermute(x, 'edata', [(i, i ^ k) for i in range(replicas)])]
    all_gather x1 -> x0, waiting for transfers between devices: 114 us -> none  [local(): scaled = lax.all_gather(scaled_shard, 'edata', axis=0, tiled=True)]
    ppermute x0 -> x20, starting transfers between devices: none -> 47.7 us  [the longest x6 27.6 us: local(): lax.ppermute(up[i], 'edata', [(j, j + 1) for j in range(replicas - 1)])]
    dynamic_update_slice x0 -> x14, other arithmetic: none -> 29.1 us  [place(): return lax.dynamic_update_slice(scaled, piece, at)]
    pallas_call x0 -> x7, Pallas kernels: none -> 22.6 us  [the longest x2 10.3 us: adam(): pl.pallas_call(functools.partial(adam_kernel, count, len(earlier)), out_s...]
    unnamed x7 -> x32, local copies, waits for them, and re-layouts: 5.91 us -> 19.5 us
    pmax x1 -> x0, blocking collectives: 12.1 us -> none  [local(): peak = lax.pmax(local_peak, 'edata')]
  transfers between devices with their start and end apart: 3 -> 23, of which waited for: 3 -> 20; matrix products, arithmetic and copies ran while one was open for 0% -> 11% of each run, Pallas kernels for 0% -> 5%
where the time goes in v1:
time: 308 us; the launch traced here: 306 us
  waiting for transfers between devices  159 us (52%)
  starting transfers between devices  60.1 us (20%)
  other arithmetic  31.8 us (10%)
  local copies, waits for them, and re-layouts  27.5 us (9%)
  Pallas kernels  22.6 us (7%)
  between operations  4.88 us (2%)
    ppermute x8, waiting for transfers between devices, swap(): return lax.ppermute(x, 'edata', [(i, i ^ k) for i in range(replicas)])  75.4 us
    ppermute x6, waiting for transfers between devices, local(): lax.ppermute(down[i], 'edata', [(j, j - 1) for j in range(1, replicas)])  43.3 us
    all_to_all x3, waiting for transfers between devices, arrive(): lax.all_to_all(picked, 'expert', split_axis=0, concat_axis=0, tiled=True)  39.3 us
    dynamic_update_slice x14, other arithmetic, place(): return lax.dynamic_update_slice(scaled, piece, at)  29.1 us
    ppermute x6, starting transfers between devices, local(): lax.ppermute(up[i], 'edata', [(j, j + 1) for j in range(replicas - 1)])  27.6 us
    unnamed x32, local copies, waits for them, and re-layouts  19.5 us
    all_to_all x3, starting transfers between devices, arrive(): lax.all_to_all(picked, 'expert', split_axis=0, concat_axis=0, tiled=True)  12.5 us
    ppermute x8, starting transfers between devices, swap(): return lax.ppermute(x, 'edata', [(i, i ^ k) for i in range(replicas)])  12.4 us
  transfers between devices with their start and end apart: 23, of which 20 were waited for; matrix products, arithmetic and copies ran while one was open for 11% of the time, Pallas kernels for 5%

profile of v1, /device:TPU:0, one launch (start us, length us, event | category | flops | bytes accessed | tf_op | source)
XLA Modules:
  0.0 305.9 jit_solution(11947893429887843570)
XLA Ops:
  5.1 5.2 %all-to-all-start.1 = ((bf16[8,64,1024]{2,1,0:T(8,128)(2,1)}), bf16[8,64,1024]{2,1,0:T(8,128)(2,1)S(1)}, u32[]{:S(2)}, u32[]{:S(2)}) async-start(bf16[8,64,1024]{2,1,0:T(8,128)(2,1)} %bitcast.8), calls=%async_computation.1 | async-start | bytes 2097152 | tf_op jit(solution)/shard_map/all_to_all | solution.py:191
  14.6 11.1 %all-to-all-done.1 = bf16[8,64,1024]{2,1,0:T(8,128)(2,1)S(1)} async-done(((bf16[8,64,1024]{2,1,0:T(8,128)(2,1)}), bf16[8,64,1024]{2,1,0:T(8,128)(2,1)S(1)}, u32[]{:S(2)}, u32[]{:S(2)}) %all-to-all-start.1) | async-done | bytes 1048608 | tf_op jit(solution)/shard_map/all_to_all | solution.py:191
  25.7 3.7 %all-to-all-start.2 = ((bf16[8,64,1024]{2,1,0:T(8,128)(2,1)}), bf16[8,64,1024]{2,1,0:T(8,128)(2,1)S(1)}, u32[]{:S(2)}, u32[]{:S(2)}) async-start(bf16[8,64,1024]{2,1,0:T(8,128)(2,1)} %bitcast.12), calls=%async_computation.2 | async-start | bytes 2097152 | tf_op jit(solution)/shard_map/all_to_all | solution.py:191
  34.2 10.5 %all-to-all-done.2 = bf16[8,64,1024]{2,1,0:T(8,128)(2,1)S(1)} async-done(((bf16[8,64,1024]{2,1,0:T(8,128)(2,1)}), bf16[8,64,1024]{2,1,0:T(8,128)(2,1)S(1)}, u32[]{:S(2)}, u32[]{:S(2)}) %all-to-all-start.2) | async-done | bytes 1048608 | tf_op jit(solution)/shard_map/all_to_all | solution.py:191
  45.7 3.6 %all-to-all-start = ((bf16[8,64,2048]{2,1,0:T(8,128)(2,1)}), bf16[8,64,2048]{2,1,0:T(8,128)(2,1)S(1)}, u32[]{:S(2)}, u32[]{:S(2)}) async-start(bf16[8,64,2048]{2,1,0:T(8,128)(2,1)} %bitcast.19), calls=%async_computation | async-start | bytes 4194304 | tf_op jit(solution)/shard_map/all_to_all | solution.py:191
  58.1 17.7 %all-to-all-done = bf16[8,64,2048]{2,1,0:T(8,128)(2,1)S(1)} async-done(((bf16[8,64,2048]{2,1,0:T(8,128)(2,1)}), bf16[8,64,2048]{2,1,0:T(8,128)(2,1)S(1)}, u32[]{:S(2)}, u32[]{:S(2)}) %all-to-all-start) | async-done | bytes 2097184 | tf_op jit(solution)/shard_map/all_to_all | solution.py:191
  78.5 4.0 %collective-permute-done.4.refs_1_ = bf16[512,512]{1,0:T(8,128)(2,1)} collective-permute-done((bf16[512,512]{1,0:T(8,128)(2,1)}, bf16[512,512]{1,0:T(8,128)(2,1)}, u32[]{:S(2)}, u32[]{:S(2)}) %collective-permute-start.4) | collective-permute-done | bytes 524320 | tf_op jit(solution)/shard_map/ppermute | solution.py:182
  83.7 3.4 %coded_sum.3 = s16[2,272,768]{2,1,0:T(8,128)(2,1)} custom-call(bf16[512,1024]{1,0:T(8,128)(2,1)S(1)} %bitcast.23, bf16[512,512]{1,0:T(8,128)(2,1)} %collective-permute-done.4.refs_1_, bf16[512,768]{1,0:T(8,128)(2,1)S(1)} %broadcast_select_fusion.refs_2_, bf16[512,768]{1,0:T(8,128)(2,1)} %collective-permute-done.1.refs_3_), custom_call_target="tpu_custom_call" | custom-call | flops 805306368 | bytes 3407872 | tf_op jit(solution)/shard_map/coded_sum/pallas_call | solution.py:84
  87.1 2.6 collective-permute-start.5
  89.7 21.8 %collective-permute-done.2.refs_1_ = bf16[512,512]{1,0:T(8,128)(2,1)S(1)} collective-permute-done((bf16[512,512]{1,0:T(8,128)(2,1)}, bf16[512,512]{1,0:T(8,128)(2,1)S(1)}, u32[]{:S(2)}, u32[]{:S(2)}) %collective-permute-start.2) | collective-permute-done | bytes 524320 | tf_op jit(solution)/shard_map/ppermute | solution.py:182
  111.5 3.3 %coded_sum.2 = s16[2,272,768]{2,1,0:T(8,128)(2,1)} custom-call(bf16[512,1024]{1,0:T(8,128)(2,1)S(1)} %bitcast.21, bf16[512,512]{1,0:T(8,128)(2,1)S(1)} %collective-permute-done.2.refs_1_, bf16[512,768]{1,0:T(8,128)(2,1)S(1)} %broadcast_select_fusion.refs_2_, bf16[512,768]{1,0:T(8,128)(2,1)} %collective-permute-done.1.refs_3_), custom_call_target="tpu_custom_call" | custom-call | flops 805306368 | bytes 3407872 | tf_op jit(solution)/shard_map/coded_sum/pallas_call | solution.py:84
  116.7 16.6 %collective-permute-done.5.refs_4_ = s16[2,272,768]{2,1,0:T(8,128)(2,1)} collective-permute-done((s16[2,272,768]{2,1,0:T(8,128)(2,1)}, s16[2,272,768]{2,1,0:T(8,128)(2,1)}, u32[]{:S(2)}, u32[]{:S(2)}) %collective-permute-start.5) | collective-permute-done | bytes 835616 | tf_op jit(solution)/shard_map/ppermute | solution.py:182
  138.6 5.2 %adam.2 = (f32[1024,768]{1,0:T(8,128)}, bf16[1024,768]{1,0:T(8,128)(2,1)}, bf16[1024,768]{1,0:T(8,128)(2,1)}, f32[1,768]{1,0:T(1,128)S(1)}) custom-call(bf16[512,2048]{1,0:T(8,128)(2,1)S(1)} %bitcast.17, bf16[512,1024]{1,0:T(8,128)(2,1)} %collective-permute-done.refs_1_, bf16[512,768]{1,0:T(8,128)(2,1)S(1)} %broadcast_select_fusion.refs_2_, ...), custom_call_target="tpu_custom_call" | custom-call | flops 805306368 | bytes 7077888 | tf_op jit(solution)/shard_map/adam/pallas_call | solution.py:144
  144.4 26.9 %collective-permute-done.3.refs_4_ = s16[2,272,768]{2,1,0:T(8,128)(2,1)} collective-permute-done((s16[2,272,768]{2,1,0:T(8,128)(2,1)}, s16[2,272,768]{2,1,0:T(8,128)(2,1)}, u32[]{:S(2)}, u32[]{:S(2)}) %collective-permute-start.3) | collective-permute-done | bytes 835616 | tf_op jit(solution)/shard_map/ppermute | solution.py:182
  176.0 5.2 %adam.3 = (f32[1024,768]{1,0:T(8,128)}, bf16[1024,768]{1,0:T(8,128)(2,1)}, bf16[1024,768]{1,0:T(8,128)(2,1)}, f32[1,768]{1,0:T(1,128)S(1)}) custom-call(bf16[512,2048]{1,0:T(8,128)(2,1)S(1)} %bitcast.18, bf16[512,1024]{1,0:T(8,128)(2,1)} %collective-permute-done.refs_1_, ...), custom_call_target="tpu_custom_call", output_to_operand_aliasing={{0}: (8, {}), {1}: (9, {}), {2}: (10, {})} | custom-call | flops 805306368 | bytes 7077888 | tf_op jit(solution)/shard_map/adam/pallas_call | solution.py:144
  184.7 2.3 collective-permute-done.6
  189.2 3.2 %collective-permute-done.7 = f32[1]{0:T(128)} collective-permute-done((f32[1]{0:T(128)}, f32[1]{0:T(128)}, u32[]{:S(2)}, u32[]{:S(2)}) %collective-permute-start.7) | collective-permute-done | bytes 36 | tf_op jit(solution)/shard_map/ppermute | solution.py:182
  193.0 3.1 %broadcast_in_dim.21 = bf16[4096,768]{1,0:T(8,128)(2,1)} broadcast(bf16[]{:T(256)} %constant.28.clone.1), dimensions={} | broadcast | bytes 6291458 | tf_op jit(solution)/shard_map/broadcast_in_dim | solution.py:230
  198.6 5.5 %collective-permute-start.9 = (bf16[512,768]{1,0:T(8,128)(2,1)}, bf16[512,768]{1,0:T(8,128)(2,1)}, u32[]{:S(2)}, u32[]{:S(2)}) collective-permute-start(bf16[512,768]{1,0:T(8,128)(2,1)} %get-tuple-element.24), channel_id=1, source_target_pairs={{0,1},{1,2},{2,3},{4,5},{5,6},{6,7},{8,9},{9,10},{10,11},{12,13},{... | collective-permute-start | bytes 2359304 | tf_op jit(solution)/shard_map/ppermute | solution.py:244
  206.6 4.6 %collective-permute-start.11 = (bf16[512,768]{1,0:T(8,128)(2,1)}, bf16[512,768]{1,0:T(8,128)(2,1)S(1)}, u32[]{:S(2)}, u32[]{:S(2)}) collective-permute-start(bf16[512,768]{1,0:T(8,128)(2,1)} %get-tuple-element.22), channel_id=1, source_target_pairs={{0,1},{1,2},{2,3},{4,5},{5,6},{6,7},{8,9},{9,10},{10,11},{12,13},{... | collective-permute-start | bytes 2359304 | tf_op jit(solution)/shard_map/ppermute | solution.py:244
  211.3 8.7 %collective-permute-done.8 = bf16[512,768]{1,0:T(8,128)(2,1)} collective-permute-done((bf16[512,768]{1,0:T(8,128)(2,1)}, bf16[512,768]{1,0:T(8,128)(2,1)}, u32[]{:S(2)}, u32[]{:S(2)}) %collective-permute-start.8) | collective-permute-done | bytes 786464 | tf_op jit(solution)/shard_map/ppermute | solution.py:243
  221.5 4.4 %collective-permute-start.13 = (bf16[512,768]{1,0:T(8,128)(2,1)}, bf16[512,768]{1,0:T(8,128)(2,1)S(1)}, u32[]{:S(2)}, u32[]{:S(2)}) collective-permute-start(bf16[512,768]{1,0:T(8,128)(2,1)} %collective-permute-done.9), channel_id=1, source_target_pairs={{0,1},{1,2},{2,3},{4,5},{5,6},{6,7},{8,9},{9,10},{10,11},{12,13},{... | collective-permute-start | bytes 2359304 | tf_op jit(solution)/shard_map/ppermute | solution.py:244
  225.9 10.8 %collective-permute-done.10 = bf16[512,768]{1,0:T(8,128)(2,1)S(1)} collective-permute-done((bf16[512,768]{1,0:T(8,128)(2,1)}, bf16[512,768]{1,0:T(8,128)(2,1)S(1)}, u32[]{:S(2)}, u32[]{:S(2)}) %collective-permute-start.10) | collective-permute-done | bytes 786464 | tf_op jit(solution)/shard_map/ppermute | solution.py:243
  238.3 4.3 %collective-permute-start.15 = (bf16[512,768]{1,0:T(8,128)(2,1)S(1)}, bf16[512,768]{1,0:T(8,128)(2,1)S(1)}, u32[]{:S(2)}, u32[]{:S(2)}) collective-permute-start(bf16[512,768]{1,0:T(8,128)(2,1)S(1)} %collective-permute-done.11), channel_id=1, source_target_pairs={{0,1},{1,2},{2,3},{4,5},{5,6},{6,7},{8,9},{9,10},{10,11},{12,13},{... | collective-permute-start | bytes 2359304 | tf_op jit(solution)/shard_map/ppermute | solution.py:244
  242.7 2.4 select_dynamic-update-slice_fusion.11
  245.1 2.2 select_dynamic-update-slice_fusion.10
  255.2 4.3 %collective-permute-start.17 = (bf16[512,768]{1,0:T(8,128)(2,1)S(1)}, bf16[512,768]{1,0:T(8,128)(2,1)S(1)}, u32[]{:S(2)}, u32[]{:S(2)}) collective-permute-start(bf16[512,768]{1,0:T(8,128)(2,1)S(1)} %collective-permute-done.13), channel_id=1, source_target_pairs={{0,1},{1,2},{2,3},{4,5},{5,6},{6,7},{8,9},{9,10},{10,11},{12,13},{... | collective-permute-start | bytes 2359304 | tf_op jit(solution)/shard_map/ppermute | solution.py:244
  259.5 10.9 %collective-permute-done.14 = bf16[512,768]{1,0:T(8,128)(2,1)S(1)} collective-permute-done((bf16[512,768]{1,0:T(8,128)(2,1)S(1)}, bf16[512,768]{1,0:T(8,128)(2,1)S(1)}, u32[]{:S(2)}, u32[]{:S(2)}) %collective-permute-start.14) | collective-permute-done | bytes 786464 | tf_op jit(solution)/shard_map/ppermute | solution.py:243
  271.9 4.4 %collective-permute-start.19 = (bf16[512,768]{1,0:T(8,128)(2,1)S(1)}, bf16[512,768]{1,0:T(8,128)(2,1)S(1)}, u32[]{:S(2)}, u32[]{:S(2)}) collective-permute-start(bf16[512,768]{1,0:T(8,128)(2,1)S(1)} %collective-permute-done.15), channel_id=1, source_target_pairs={{0,1},{1,2},{2,3},{4,5},{5,6},{6,7},{8,9},{9,10},{10,11},{12,13},{... | collective-permute-start | bytes 2359304 | tf_op jit(solution)/shard_map/ppermute | solution.py:244
  276.4 2.2 select_dynamic-update-slice_fusion.7
  291.7 8.6 %collective-permute-done.18 = bf16[512,768]{1,0:T(8,128)(2,1)S(1)} collective-permute-done((bf16[512,768]{1,0:T(8,128)(2,1)S(1)}, bf16[512,768]{1,0:T(8,128)(2,1)S(1)}, u32[]{:S(2)}, u32[]{:S(2)}) %collective-permute-start.18) | collective-permute-done | bytes 786464 | tf_op jit(solution)/shard_map/ppermute | solution.py:243
  302.6 2.2 select_dynamic-update-slice_fusion
  (78 shorter events, 75.9 us)
Async XLA Ops:
  0.7 2.2 copy-start
  5.1 20.6 %all-to-all-start.1 = ((bf16[8,64,1024]{2,1,0:T(8,128)(2,1)}), bf16[8,64,1024]{2,1,0:T(8,128)(2,1)S(1)}, u32[]{:S(2)}, u32[]{:S(2)}) async-start(bf16[8,64,1024]{2,1,0:T(8,128)(2,1)} %bitcast.8), calls=%async_computation.1 | async-start | bytes 2097152 | tf_op jit(solution)/shard_map/all_to_all | solution.py:191
  10.2 2.2 copy-start.1
  25.7 19.0 %copy-start.6 = (bf16[8,64,1024]{2,1,0:T(8,128)(2,1)}, bf16[8,64,1024]{2,1,0:T(8,128)(2,1)S(1)}, u32[]{:S(2)}) copy-start(bf16[8,64,1024]{2,1,0:T(8,128)(2,1)S(1)} %all-to-all-done.1) | copy-start | bytes 3145732
  25.7 23.6 %copy-start.15 = (s32[8]{0:T(128)S(1)}, s32[8]{0:T(128)}, u32[]{:S(2)}) copy-start(s32[8]{0:T(128)} %param.8) | copy-start | bytes 100
  25.7 19.0 %all-to-all-start.2 = ((bf16[8,64,1024]{2,1,0:T(8,128)(2,1)}), bf16[8,64,1024]{2,1,0:T(8,128)(2,1)S(1)}, u32[]{:S(2)}, u32[]{:S(2)}) async-start(bf16[8,64,1024]{2,1,0:T(8,128)(2,1)} %bitcast.12), calls=%async_computation.2 | async-start | bytes 2097152 | tf_op jit(solution)/shard_map/all_to_all | solution.py:191
  29.4 2.2 copy-start.2
  45.7 30.2 %all-to-all-start = ((bf16[8,64,2048]{2,1,0:T(8,128)(2,1)}), bf16[8,64,2048]{2,1,0:T(8,128)(2,1)S(1)}, u32[]{:S(2)}, u32[]{:S(2)}) async-start(bf16[8,64,2048]{2,1,0:T(8,128)(2,1)} %bitcast.19), calls=%async_computation | async-start | bytes 4194304 | tf_op jit(solution)/shard_map/all_to_all | solution.py:191
  50.7 27.8 %collective-permute-start.1 = (bf16[512,768]{1,0:T(8,128)(2,1)S(1)}, bf16[512,768]{1,0:T(8,128)(2,1)}, u32[]{:S(2)}, u32[]{:S(2)}) collective-permute-start(bf16[512,768]{1,0:T(8,128)(2,1)S(1)} %broadcast_select_fusion.refs_2_), channel_id=1, source_target_pairs={{0,1},{1,0},{2,3},{3,2},{4,5},{5,4},{6,7},{7,6},{8,9},{9,8},{10,11... | collective-permute-start | bytes 2359304 | tf_op jit(solution)/shard_map/ppermute | solution.py:182
  54.3 28.2 %collective-permute-start.4 = (bf16[512,512]{1,0:T(8,128)(2,1)}, bf16[512,512]{1,0:T(8,128)(2,1)}, u32[]{:S(2)}, u32[]{:S(2)}) collective-permute-start(bf16[512,512]{1,0:T(8,128)(2,1)} %slice.22), channel_id=1, source_target_pairs={{0,1},{1,0},{2,3},{3,2},{4,5},{5,4},{6,7},{7,6},{8,9},{9,8},{10,11... | collective-permute-start | bytes 1572872 | tf_op jit(solution)/shard_map/ppermute | solution.py:182
  56.6 55.0 %collective-permute-start.2 = (bf16[512,512]{1,0:T(8,128)(2,1)}, bf16[512,512]{1,0:T(8,128)(2,1)S(1)}, u32[]{:S(2)}, u32[]{:S(2)}) collective-permute-start(bf16[512,512]{1,0:T(8,128)(2,1)} %slice.21), channel_id=1, source_target_pairs={{0,1},{1,0},{2,3},{3,2},{4,5},{5,4},{6,7},{7,6},{8,9},{9,8},{10,11... | collective-permute-start | bytes 1572872 | tf_op jit(solution)/shard_map/ppermute | solution.py:182
  75.9 35.7 %copy-start.7 = (bf16[8,64,1024]{2,1,0:T(8,128)(2,1)S(1)}, bf16[8,64,1024]{2,1,0:T(8,128)(2,1)}, u32[]{:S(2)}) copy-start(bf16[8,64,1024]{2,1,0:T(8,128)(2,1)} %copy-done.6) | copy-start | bytes 3145732
  76.9 57.0 %collective-permute-start = (bf16[512,1024]{1,0:T(8,128)(2,1)}, bf16[512,1024]{1,0:T(8,128)(2,1)}, u32[]{:S(2)}, u32[]{:S(2)}) collective-permute-start(bf16[512,1024]{1,0:T(8,128)(2,1)} %slice.20), channel_id=1, source_target_pairs={{0,1},{1,0},{2,3},{3,2},{4,5},{5,4},{6,7},{7,6},{8,9},{9,8},{10,11... | collective-permute-start | bytes 3145736 | tf_op jit(solution)/shard_map/ppermute | solution.py:182
  87.1 46.1 %collective-permute-start.5 = (s16[2,272,768]{2,1,0:T(8,128)(2,1)}, s16[2,272,768]{2,1,0:T(8,128)(2,1)}, u32[]{:S(2)}, u32[]{:S(2)}) collective-permute-start(s16[2,272,768]{2,1,0:T(8,128)(2,1)} %coded_sum.3), channel_id=1, source_target_pairs={{0,2},{1,3},{2,0},{3,1},{4,6},{5,7},{6,4},{7,5},{8,10},{9,11},{10,... | collective-permute-start | bytes 2506760 | tf_op jit(solution)/shard_map/ppermute | solution.py:182
  114.9 56.4 %collective-permute-start.3 = (s16[2,272,768]{2,1,0:T(8,128)(2,1)}, s16[2,272,768]{2,1,0:T(8,128)(2,1)}, u32[]{:S(2)}, u32[]{:S(2)}) collective-permute-start(s16[2,272,768]{2,1,0:T(8,128)(2,1)} %coded_sum.2), channel_id=1, source_target_pairs={{0,2},{1,3},{2,0},{3,1},{4,6},{5,7},{6,4},{7,5},{8,10},{9,11},{10,... | collective-permute-start | bytes 2506760 | tf_op jit(solution)/shard_map/ppermute | solution.py:182
  133.9 1.9 copy-start.3
  171.3 1.9 copy-start.4
  181.8 14.3 %copy-start.14 = (f32[1024,768]{1,0:T(8,128)S(1)}, f32[1024,768]{1,0:T(8,128)}, u32[]{:S(2)}) copy-start(f32[1024,768]{1,0:T(8,128)} %get-tuple-element.8) | copy-start | bytes 9437188
  183.4 3.7 %collective-permute-start.6 = (f32[1]{0:T(128)}, f32[1]{0:T(128)}, u32[]{:S(2)}, u32[]{:S(2)}) collective-permute-start(f32[1]{0:T(128)} %bitcast.14), channel_id=1, source_target_pairs={{0,1},{1,0},{2,3},{3,2},{4,5},{5,4},{6,7},{7,6},{8,9},{9,8},{10,11... | collective-permute-start | bytes 20 | tf_op jit(solution)/shard_map/ppermute | solution.py:182
  187.7 4.6 %collective-permute-start.7 = (f32[1]{0:T(128)}, f32[1]{0:T(128)}, u32[]{:S(2)}, u32[]{:S(2)}) collective-permute-start(f32[1]{0:T(128)} %max.22), channel_id=1, source_target_pairs={{0,2},{1,3},{2,0},{3,1},{4,6},{5,7},{6,4},{7,5},{8,10},{9,11},{10,... | collective-permute-start | bytes 20 | tf_op jit(solution)/shard_map/ppermute | solution.py:182
  197.4 22.7 %collective-permute-start.8 = (bf16[512,768]{1,0:T(8,128)(2,1)}, bf16[512,768]{1,0:T(8,128)(2,1)}, u32[]{:S(2)}, u32[]{:S(2)}) collective-permute-start(bf16[512,768]{1,0:T(8,128)(2,1)} %get-tuple-element.24), channel_id=1, source_target_pairs={{1,0},{2,1},{3,2},{5,4},{6,5},{7,6},{9,8},{10,9},{11,10},{13,12},{... | collective-permute-start | bytes 2359304 | tf_op jit(solution)/shard_map/ppermute | solution.py:243
  198.6 22.8 %collective-permute-start.9 = (bf16[512,768]{1,0:T(8,128)(2,1)}, bf16[512,768]{1,0:T(8,128)(2,1)}, u32[]{:S(2)}, u32[]{:S(2)}) collective-permute-start(bf16[512,768]{1,0:T(8,128)(2,1)} %get-tuple-element.24), channel_id=1, source_target_pairs={{0,1},{1,2},{2,3},{4,5},{5,6},{6,7},{8,9},{9,10},{10,11},{12,13},{... | collective-permute-start | bytes 2359304 | tf_op jit(solution)/shard_map/ppermute | solution.py:244
  205.4 31.4 %collective-permute-start.10 = (bf16[512,768]{1,0:T(8,128)(2,1)}, bf16[512,768]{1,0:T(8,128)(2,1)S(1)}, u32[]{:S(2)}, u32[]{:S(2)}) collective-permute-start(bf16[512,768]{1,0:T(8,128)(2,1)} %get-tuple-element.22), channel_id=1, source_target_pairs={{1,0},{2,1},{3,2},{5,4},{6,5},{7,6},{9,8},{10,9},{11,10},{13,12},{... | collective-permute-start | bytes 2359304 | tf_op jit(solution)/shard_map/ppermute | solution.py:243
  206.6 31.7 %collective-permute-start.11 = (bf16[512,768]{1,0:T(8,128)(2,1)}, bf16[512,768]{1,0:T(8,128)(2,1)S(1)}, u32[]{:S(2)}, u32[]{:S(2)}) collective-permute-start(bf16[512,768]{1,0:T(8,128)(2,1)} %get-tuple-element.22), channel_id=1, source_target_pairs={{0,1},{1,2},{2,3},{4,5},{5,6},{6,7},{8,9},{9,10},{10,11},{12,13},{... | collective-permute-start | bytes 2359304 | tf_op jit(solution)/shard_map/ppermute | solution.py:244
  220.0 33.6 %collective-permute-start.12 = (bf16[512,768]{1,0:T(8,128)(2,1)}, bf16[512,768]{1,0:T(8,128)(2,1)S(1)}, u32[]{:S(2)}, u32[]{:S(2)}) collective-permute-start(bf16[512,768]{1,0:T(8,128)(2,1)} %collective-permute-done.8), channel_id=1, source_target_pairs={{1,0},{2,1},{3,2},{5,4},{6,5},{7,6},{9,8},{10,9},{11,10},{13,12},{... | collective-permute-start | bytes 2359304 | tf_op jit(solution)/shard_map/ppermute | solution.py:243
  221.5 33.7 %collective-permute-start.13 = (bf16[512,768]{1,0:T(8,128)(2,1)}, bf16[512,768]{1,0:T(8,128)(2,1)S(1)}, u32[]{:S(2)}, u32[]{:S(2)}) collective-permute-start(bf16[512,768]{1,0:T(8,128)(2,1)} %collective-permute-done.9), channel_id=1, source_target_pairs={{0,1},{1,2},{2,3},{4,5},{5,6},{6,7},{8,9},{9,10},{10,11},{12,13},{... | collective-permute-start | bytes 2359304 | tf_op jit(solution)/shard_map/ppermute | solution.py:244
  236.8 33.7 %collective-permute-start.14 = (bf16[512,768]{1,0:T(8,128)(2,1)S(1)}, bf16[512,768]{1,0:T(8,128)(2,1)S(1)}, u32[]{:S(2)}, u32[]{:S(2)}) collective-permute-start(bf16[512,768]{1,0:T(8,128)(2,1)S(1)} %collective-permute-done.10), channel_id=1, source_target_pairs={{1,0},{2,1},{3,2},{5,4},{6,5},{7,6},{9,8},{10,9},{11,10},{13,12},{... | collective-permute-start | bytes 2359304 | tf_op jit(solution)/shard_map/ppermute | solution.py:243
  238.3 33.6 %collective-permute-start.15 = (bf16[512,768]{1,0:T(8,128)(2,1)S(1)}, bf16[512,768]{1,0:T(8,128)(2,1)S(1)}, u32[]{:S(2)}, u32[]{:S(2)}) collective-permute-start(bf16[512,768]{1,0:T(8,128)(2,1)S(1)} %collective-permute-done.11), channel_id=1, source_target_pairs={{0,1},{1,2},{2,3},{4,5},{5,6},{6,7},{8,9},{9,10},{10,11},{12,13},{... | collective-permute-start | bytes 2359304 | tf_op jit(solution)/shard_map/ppermute | solution.py:244
  253.6 33.7 %collective-permute-start.16 = (bf16[512,768]{1,0:T(8,128)(2,1)S(1)}, bf16[512,768]{1,0:T(8,128)(2,1)S(1)}, u32[]{:S(2)}, u32[]{:S(2)}) collective-permute-start(bf16[512,768]{1,0:T(8,128)(2,1)S(1)} %collective-permute-done.12), channel_id=1, source_target_pairs={{1,0},{2,1},{3,2},{5,4},{6,5},{7,6},{9,8},{10,9},{11,10},{13,12},{... | collective-permute-start | bytes 2359304 | tf_op jit(solution)/shard_map/ppermute | solution.py:243
  255.2 34.3 %collective-permute-start.17 = (bf16[512,768]{1,0:T(8,128)(2,1)S(1)}, bf16[512,768]{1,0:T(8,128)(2,1)S(1)}, u32[]{:S(2)}, u32[]{:S(2)}) collective-permute-start(bf16[512,768]{1,0:T(8,128)(2,1)S(1)} %collective-permute-done.13), channel_id=1, source_target_pairs={{0,1},{1,2},{2,3},{4,5},{5,6},{6,7},{8,9},{9,10},{10,11},{12,13},{... | collective-permute-start | bytes 2359304 | tf_op jit(solution)/shard_map/ppermute | solution.py:244
  270.5 29.9 %collective-permute-start.18 = (bf16[512,768]{1,0:T(8,128)(2,1)S(1)}, bf16[512,768]{1,0:T(8,128)(2,1)S(1)}, u32[]{:S(2)}, u32[]{:S(2)}) collective-permute-start(bf16[512,768]{1,0:T(8,128)(2,1)S(1)} %collective-permute-done.14), channel_id=1, source_target_pairs={{1,0},{2,1},{3,2},{5,4},{6,5},{7,6},{9,8},{10,9},{11,10},{13,12},{... | collective-permute-start | bytes 2359304 | tf_op jit(solution)/shard_map/ppermute | solution.py:243
  271.9 30.6 %collective-permute-start.19 = (bf16[512,768]{1,0:T(8,128)(2,1)S(1)}, bf16[512,768]{1,0:T(8,128)(2,1)S(1)}, u32[]{:S(2)}, u32[]{:S(2)}) collective-permute-start(bf16[512,768]{1,0:T(8,128)(2,1)S(1)} %collective-permute-done.15), channel_id=1, source_target_pairs={{0,1},{1,2},{2,3},{4,5},{5,6},{6,7},{8,9},{9,10},{10,11},{12,13},{... | collective-permute-start | bytes 2359304 | tf_op jit(solution)/shard_map/ppermute | solution.py:244
  (7 other events, 9.1 us)

commit v2 on v0

v2 whole, which is shorter than its diff:
```python
import functools
import jax
import jax.numpy as jnp
from jax import lax
from jax.experimental import pallas as pl
from jax.experimental.pallas import tpu as pltpu
from jax.sharding import PartitionSpec as P

beta_one = 0.9
beta_two = 0.999
correct_one = 1.0 - 0.9**5
correct_two = 1.0 - 0.999**5
adam_eps = 1e-08
learn_rate = 0.05
weight_decay = 1.0
peak_eps = 1e-06

VMEM_LIMIT = 60 * 1024 * 1024
LEVELS = 32000.0
PLACE_HINT = 1 << 36
TAIL = 16


def params():
    return pltpu.CompilerParams(vmem_limit_bytes=VMEM_LIMIT)


def hint(amount):
    return pl.CostEstimate(flops=amount, bytes_accessed=amount, transcendentals=0)


def pick_kernel(strips, table_ref, x_ref, out_ref, buffer, sems_in, sems_out):
    rows = x_ref.shape[0]
    width = out_ref.shape[1]
    size = rows // strips
    moves = []
    for k in range(out_ref.shape[0] // size):
        i, j = divmod(k, strips)
        start = pl.multiple_of(table_ref[i] * width, width)
        there = pl.ds(k * size, size)
        moves.append(
            (
                pltpu.make_async_copy(
                    x_ref.at[pl.ds(j * size, size), pl.ds(start, width)],
                    buffer.at[there, :],
                    sems_in.at[k],
                ),
                pltpu.make_async_copy(buffer.at[there, :], out_ref.at[there, :], sems_out.at[k]),
            )
        )
    for come, _ in moves:
        come.start()
    for come, go in moves:
        come.wait()
        go.start()
    for _, go in moves:
        go.wait()


def pick_columns(x, chunks, width):
    rows, count, strips = x.shape[0], chunks.shape[0], 4
    anywhere = pl.BlockSpec(memory_space=pl.ANY)
    return pl.pallas_call(
        functools.partial(pick_kernel, strips),
        out_shape=jax.ShapeDtypeStruct((count * rows, width), x.dtype),
        in_specs=[pl.BlockSpec(memory_space=pltpu.SMEM), anywhere],
        out_specs=anywhere,
        scratch_shapes=[
            pltpu.VMEM((count * rows, width), x.dtype),
            pltpu.SemaphoreType.DMA((strips * count,)),
            pltpu.SemaphoreType.DMA((strips * count,)),
        ],
        compiler_params=params(),
        cost_estimate=hint(1024),
        name="pick_columns",
    )(chunks, x)


def gate_kernel(*refs):
    pass


def gate(x, after):
    if not after:
        return x
    anywhere = pl.BlockSpec(memory_space=pl.ANY)
    return pl.pallas_call(
        gate_kernel,
        out_shape=jax.ShapeDtypeStruct(x.shape, x.dtype),
        in_specs=[anywhere] * (1 + len(after)),
        out_specs=anywhere,
        input_output_aliases={0: 0},
        cost_estimate=hint(1024),
        name="gate",
    )(x, *after)


def contract(rows_ref, hidden_ref):
    return lax.dot_general(
        rows_ref[...],
        hidden_ref[...],
        (((0,), (0,)), ((), ())),
        preferred_element_type=jnp.float32,
    )


def group_sum(count, refs):
    rows, hidden = refs[1 : count + 1], refs[count + 1 : 2 * count + 1]
    total = contract(rows[0], hidden[0])
    for k in range(1, count):
        total = total + contract(rows[k], hidden[k])
    return total


def code_kernel(count, *refs):
    out = refs[-1]
    total = group_sum(count, refs)
    block = total.shape[0]
    top = jnp.maximum(jnp.max(jnp.abs(total), axis=0, keepdims=True), 1e-30)
    exponent = jnp.floor(jnp.log2(top)) + 1.0
    step = jnp.exp2(exponent) * (1.0 / LEVELS)
    codes = jnp.round(total * (1.0 / step))
    out[0, :block, :] = codes.astype(jnp.int32).astype(jnp.int16)
    out[0, block:, :] = jnp.broadcast_to(
        exponent.astype(jnp.int32), (TAIL, total.shape[1])
    ).astype(jnp.int16)


def sum_kernel(count, *refs):
    refs[-1][...] = group_sum(count, refs)


def summed(kernel, rows, order, hidden, at, width, block, out_shape, out_spec, name):
    count = len(hidden)
    depth, ffn = hidden[0].shape
    first = at // block
    return pl.pallas_call(
        functools.partial(kernel, count),
        out_shape=out_shape,
        grid_spec=pltpu.PrefetchScalarGridSpec(
            num_scalar_prefetch=1,
            grid=(width // block,),
            in_specs=[
                pl.BlockSpec(
                    (depth, block), functools.partial(lambda k, i, table: (table[k], first + i), k)
                )
                for k in range(count)
            ]
            + [pl.BlockSpec((depth, ffn), lambda i, table: (0, 0))] * count,
            out_specs=out_spec,
        ),
        compiler_params=params(),
        cost_estimate=hint(1024),
        name=name,
    )(order, *[rows] * count, *hidden)


def coded_sum(rows, order, hidden, at, width, block):
    ffn = hidden[0].shape[1]
    shape = jax.ShapeDtypeStruct((width // block, block + TAIL, ffn), jnp.int16)
    spec = pl.BlockSpec((1, block + TAIL, ffn), lambda i, table: (i, 0, 0))
    return summed(
        code_kernel, rows, order, hidden, at, width, block, shape, spec, "coded_sum"
    )


def own_sum(rows, order, hidden, block):
    ffn, width = hidden[0].shape[1], rows.shape[1]
    shape = jax.ShapeDtypeStruct((width, ffn), jnp.float32)
    spec = pl.BlockSpec((block, ffn), lambda i, table: (i, 0))
    return summed(sum_kernel, rows, order, hidden, 0, width, block, shape, spec, "own_sum")


def adam_kernel(arrays, at, block, size, *refs):
    streams = refs[:5]
    outs, top_ref = refs[-14:-11], refs[-11]
    buffers, results = refs[-10:-5], refs[-5:-2]
    arrived, left = refs[-2:]
    own, coded, master, one, two = buffers
    steps = coded.shape[0] * block // size
    comes, leaves = [], []
    for i in range(steps):
        here, there = pl.ds(i * size, size), pl.ds(at + i * size, size)
        pairs = [(x.at[there, :], y.at[here, :]) for x, y in zip(streams[2:], buffers[2:])]
        pairs.append((streams[0].at[there, :], own.at[here, :]))
        if i * size % block == 0:
            b = i * size // block
            pairs.append((streams[1].at[b], coded.at[b]))
        comes.append(
            [pltpu.make_async_copy(x, y, arrived.at[i, k]) for k, (x, y) in enumerate(pairs)]
        )
        leaves.append(
            [
                pltpu.make_async_copy(y.at[here, :], x.at[there, :], left.at[i, k])
                for k, (x, y) in enumerate(zip(outs, results))
            ]
        )
    for copies in comes:
        for copy in copies:
            copy.start()
    highest = None
    for i in range(steps):
        for copy in comes[i]:
            copy.wait()
        here = pl.ds(i * size, size)
        b, off = i * size // block, i * size % block
        exponent = coded[b, block : block + 1, :].astype(jnp.int32).astype(jnp.float32)
        codes = coded[b, off : off + size, :].astype(jnp.int32).astype(jnp.float32)
        grad = own[here, :] + codes * (jnp.exp2(exponent) * (1.0 / LEVELS))
        first = beta_one * one[here, :].astype(jnp.float32) + (1.0 - beta_one) * grad
        second = beta_two * two[here, :].astype(jnp.float32) + (1.0 - beta_two) * grad * grad
        update = (first * (1.0 / correct_one)) / (
            jnp.sqrt(second * (1.0 / correct_two)) + adam_eps
        )
        weight = master[here, :]
        new_master = weight - learn_rate * (update + weight_decay * weight)
        results[0][here, :] = new_master
        results[1][here, :] = first.astype(jnp.bfloat16)
        results[2][here, :] = second.astype(jnp.bfloat16)
        for copy in leaves[i]:
            copy.start()
        top = jnp.max(jnp.abs(new_master), axis=0, keepdims=True)
        highest = top if highest is None else jnp.maximum(highest, top)
    peak = jnp.max(highest)
    if arrays:
        peak = jnp.maximum(peak, refs[5 + arrays][0])
    top_ref[0] = peak
    for copies in leaves:
        for copy in copies:
            copy.wait()


def adam(own, coded, master, one, two, at, block, earlier=()):
    shard, ffn = master.shape
    size = min(128, block)
    width = coded.shape[0] * block
    steps = width // size
    anywhere = pl.BlockSpec(memory_space=pl.ANY)
    scalar = pl.BlockSpec(memory_space=pltpu.SMEM)
    arrays = max(len(earlier) - 1, 0)
    types = (jnp.float32, jnp.bfloat16, jnp.bfloat16)
    return pl.pallas_call(
        functools.partial(adam_kernel, arrays, at, block, size),
        out_shape=tuple(jax.ShapeDtypeStruct((shard, ffn), t) for t in types)
        + (jax.ShapeDtypeStruct((1,), jnp.float32),),
        in_specs=[anywhere] * (5 + arrays) + [scalar] * (arrays > 0),
        out_specs=(anywhere, anywhere, anywhere, scalar),
        scratch_shapes=[pltpu.VMEM((width, ffn), jnp.float32), pltpu.VMEM(coded.shape, jnp.int16)]
        + [pltpu.VMEM((width, ffn), t) for t in types * 2]
        + [pltpu.SemaphoreType.DMA((steps, 5)), pltpu.SemaphoreType.DMA((steps, 3))],
        input_output_aliases={5 + k: k for k in range(arrays)},
        compiler_params=params(),
        cost_estimate=hint(1024),
        name="adam",
    )(own, coded, master, one, two, *earlier)


def place_kernel(count, strips, table_ref, *refs):
    pieces = refs[:count]
    whole, buffer, sems_in, sems_out = refs[-4:]
    rows = pieces[0].shape[0]
    size = rows // strips

    def come(k, j):
        strip = pl.ds(j * size, size)
        return pltpu.make_async_copy(
            pieces[k].at[strip, :], buffer.at[k, strip, :], sems_in.at[k, j]
        )

    def leave(k, j):
        at = pl.multiple_of(table_ref[2 * k] * rows + j * size, size)
        return pltpu.make_async_copy(
            buffer.at[k, pl.ds(j * size, size), :], whole.at[pl.ds(at, size), :], sems_out.at[k, j]
        )

    for k in range(count):

        @pl.when(table_ref[2 * k + 1] > 0)
        def _():
            for j in range(strips):
                come(k, j).start()

    for k in range(count):

        @pl.when(table_ref[2 * k + 1] > 0)
        def _():
            for j in range(strips):
                come(k, j).wait()
                leave(k, j).start()

    for k in range(count):

        @pl.when(table_ref[2 * k + 1] > 0)
        def _():
            for j in range(strips):
                leave(k, j).wait()


def place(whole, shape, pieces, spots):
    count, strips = len(pieces), 4
    table = jnp.stack([jnp.asarray(v).astype(jnp.int32) for spot in spots for v in spot])
    anywhere = pl.BlockSpec(memory_space=pl.ANY)
    earlier = () if whole is None else (whole,)
    return pl.pallas_call(
        functools.partial(place_kernel, count, strips),
        out_shape=jax.ShapeDtypeStruct(shape, jnp.bfloat16),
        in_specs=[pl.BlockSpec(memory_space=pltpu.SMEM)] + [anywhere] * (count + len(earlier)),
        out_specs=anywhere,
        scratch_shapes=[
            pltpu.VMEM((count,) + pieces[0].shape, jnp.bfloat16),
            pltpu.SemaphoreType.DMA((count, strips)),
            pltpu.SemaphoreType.DMA((count, strips)),
        ],
        input_output_aliases={1 + count: 0} if earlier else {},
        compiler_params=params(),
        cost_estimate=hint(PLACE_HINT),
        name="place",
    )(table, *pieces, *earlier)


def local(out_grad, hidden_saved, recv_counts, master_weight, moment_one, moment_two):
    experts = lax.axis_size("expert")
    half = lax.axis_size("near")
    replicas = lax.axis_size("far") * half
    near, far = lax.axis_index("near"), lax.axis_index("far")
    me = far * half + near
    capacity = out_grad.shape[0] // experts
    shard, ffn = master_weight.shape
    block = min(256, shard // 2)
    chain = ("far", "near")

    def swap(x, k):
        return lax.ppermute(x, chain, [(i, i ^ k) for i in range(replicas)])

    live = (jnp.arange(capacity)[None, :] < recv_counts[:, None]).reshape(-1)
    hidden = jnp.where(live[:, None], hidden_saved, jnp.zeros((), jnp.bfloat16))
    hiddens = [hidden] + [swap(hidden, k) for k in range(1, half)]
    order = jnp.stack([near ^ k for k in range(half)]).astype(jnp.int32)

    def arrive(side, after):
        chunks = (side * half + jnp.arange(half)).astype(jnp.int32)
        picked = gate(pick_columns(out_grad, chunks, shard), after)
        return lax.all_to_all(picked, ("near", "expert"), 0, 0, tiled=True)

    part = shard // 2
    got = arrive(1 - far, ())
    partials = [coded_sum(got, order, hiddens, p * part, part, block) for p in range(2)]
    coded = [swap(partial, half) for partial in partials]

    got = arrive(far, (partials[0],))
    own = own_sum(got, order, hiddens, block)
    results = ()
    for p in range(2):
        results = adam(
            own, coded[p], master_weight, moment_one, moment_two, p * part, block, tuple(results)
        )
    new_master, new_one, new_two, peak = results

    step = 1
    while step < replicas:
        peak = jnp.maximum(peak, swap(peak, step))
        step *= 2

    pieces = 2
    size = shard // pieces
    whole_shape = (replicas * shard, ffn)
    inverse = 1.0 / (peak + peak_eps)
    down = [
        (new_master[i * size : (i + 1) * size] * inverse).astype(jnp.bfloat16)
        for i in range(pieces)
    ]
    up = list(down)
    scaled = place(None, whole_shape, down, [(me * pieces + i, 1) for i in range(pieces)])
    for s in range(1, replicas):
        for i in range(pieces):
            down[i] = lax.ppermute(down[i], chain, [(j, j - 1) for j in range(1, replicas)])
            up[i] = lax.ppermute(up[i], chain, [(j, j + 1) for j in range(replicas - 1)])
        for i in range(pieces):
            scaled = place(
                scaled,
                whole_shape,
                [down[i], up[i]],
                [
                    (jnp.minimum(me + s, replicas - 1) * pieces + i, me + s < replicas),
                    (jnp.maximum(me - s, 0) * pieces + i, me >= s),
                ],
            )
    return new_master, new_one, new_two, scaled, peak


def solution(mesh):
    experts, replicas = mesh.devices.shape
    cut = jax.sharding.Mesh(
        mesh.devices.reshape(experts, 2, replicas // 2), ("expert", "far", "near")
    )
    everything = ("expert", "far", "near")
    placed = P(everything, None)
    return jax.shard_map(
        local,
        mesh=cut,
        in_specs=(placed, placed, P(everything), placed, placed, placed),
        out_specs=(placed, placed, placed, P("expert", None), P("expert")),
        check_vma=False,
    )
```

time: 433 us -> 270 us (0.62)
  waiting for transfers between devices: 375 us -> 142 us
  starting transfers between devices: 5.39 us -> 58.7 us
  Pallas kernels: 0 us -> 50.6 us
  blocking collectives: 12.1 us -> 0 us
  between operations: 14.7 us -> 3.99 us
  matrix products: 6.44 us -> 0 us
    reduce_scatter x1 -> x0, waiting for transfers between devices: 212 us -> none  [local(): lax.psum_scatter(lax.dot_general(masked, hidden_saved, (((0,), (0,)), (()...]
    all_gather x1 -> x0, waiting for transfers between devices: 114 us -> none  [local(): scaled = lax.all_gather(scaled_shard, 'edata', axis=0, tiled=True)]
    ppermute x0 -> x17, waiting for transfers between devices: none -> 101 us  [the longest x5 51.7 us: swap(): return lax.ppermute(x, chain, [(i, i ^ k) for i in range(replicas)])]
    pallas_call x0 -> x15, Pallas kernels: none -> 50.6 us  [the longest x7 19.2 us: place(): pl.pallas_call(functools.partial(place_kernel, count, strips), out_shape=...]
    ppermute x0 -> x17, starting transfers between devices: none -> 46.9 us  [the longest x6 29.7 us: local(): lax.ppermute(up[i], chain, [(j, j + 1) for j in range(replicas - 1)])]
    pmax x1 -> x0, blocking collectives: 12.1 us -> none  [local(): peak = lax.pmax(local_peak, 'edata')]
    all_to_all x1 -> x2, waiting for transfers between devices: 49 us -> 41.2 us  [arrive(): return lax.all_to_all(picked, ('near', 'expert'), 0, 0, tiled=True)]
    reduce_max x1 -> x0, other arithmetic: 7.17 us -> none  [local(): local_peak = jnp.max(jnp.abs(new_master))]
  transfers between devices with their start and end apart: 3 -> 19, of which waited for: 3 -> 15; matrix products, arithmetic and copies ran while one was open for 0% -> 3% of each run, Pallas kernels for 0% -> 13%
where the time goes in v2:
time: 270 us; the launch traced here: 268 us
  waiting for transfers between devices  142 us (53%)
  starting transfers between devices  58.7 us (22%)
  Pallas kernels  50.6 us (19%)
  other arithmetic  9.47 us (4%)
  between operations  3.99 us (1%)
  local copies, waits for them, and re-layouts  3.66 us (1%)
    ppermute x5, waiting for transfers between devices, swap(): return lax.ppermute(x, chain, [(i, i ^ k) for i in range(replicas)])  51.7 us
    all_to_all x2, waiting for transfers between devices, arrive(): return lax.all_to_all(picked, ('near', 'expert'), 0, 0, tiled=True)  41.2 us
    ppermute x6, starting transfers between devices, local(): lax.ppermute(up[i], chain, [(j, j + 1) for j in range(replicas - 1)])  29.7 us
    ppermute x6, waiting for transfers between devices, local(): lax.ppermute(down[i], chain, [(j, j - 1) for j in range(1, replicas)])  25.6 us
    ppermute x6, waiting for transfers between devices, local(): lax.ppermute(up[i], chain, [(j, j + 1) for j in range(replicas - 1)])  23.6 us
    pallas_call x7, Pallas kernels, place(): pl.pallas_call(functools.partial(place_kernel, count, strips), out_shape=...  19.2 us
    pallas_call x3, Pallas kernels, summed(): pl.pallas_call(functools.partial(kernel, count), out_shape=out_shape, gri...  15.1 us
    all_to_all x2, starting transfers between devices, arrive(): return lax.all_to_all(picked, ('near', 'expert'), 0, 0, tiled=True)  11.8 us
  transfers between devices with their start and end apart: 19, of which 15 were waited for; matrix products, arithmetic and copies ran while one was open for 3% of the time, Pallas kernels for 13%

profile of v2, /device:TPU:0, one launch (start us, length us, event | category | flops | bytes accessed | tf_op | source)
XLA Modules:
  0.0 268.4 jit_solution(9468270097224640605)
XLA Ops:
  1.2 3.1 %pick_columns.3 = bf16[1024,1024]{1,0:T(8,128)(2,1)} custom-call(s32[2]{0:T(128)} %iota_add_fusion.table_ref, bf16[512,4096]{1,0:T(8,128)(2,1)} %x_ref.3), custom_call_target="tpu_custom_call" | custom-call | flops 1024 | bytes 1024 | tf_op jit(solution)/shard_map/pick_columns/pallas_call | solution.py:63
  4.2 6.3 %all-to-all-start = ((bf16[16,64,1024]{2,1,0:T(8,128)(2,1)}), bf16[16,64,1024]{2,1,0:T(8,128)(2,1)S(1)}, u32[]{:S(2)}, u32[]{:S(2)}) async-start(bf16[16,64,1024]{2,1,0:T(8,128)(2,1)} %bitcast.34), calls=%async_computation | async-start | bytes 4194304 | tf_op jit(solution)/shard_map/all_to_all | solution.py:343
  14.5 3.1 %pick_columns.2.refs_0_ = bf16[1024,1024]{1,0:T(8,128)(2,1)} custom-call(s32[2]{0:T(128)} %iota_add_fusion.1.table_ref, bf16[512,4096]{1,0:T(8,128)(2,1)} %x_ref.3), custom_call_target="tpu_custom_call" | custom-call | flops 1024 | bytes 1024 | tf_op jit(solution)/shard_map/pick_columns/pallas_call | solution.py:63
  18.2 37.3 %collective-permute-done.refs_4_ = bf16[512,768]{1,0:T(8,128)(2,1)} collective-permute-done((bf16[512,768]{1,0:T(8,128)(2,1)S(1)}, bf16[512,768]{1,0:T(8,128)(2,1)}, u32[]{:S(2)}, u32[]{:S(2)}) %collective-permute-start) | collective-permute-done | bytes 786464 | tf_op jit(solution)/shard_map/ppermute | solution.py:333
  56.9 4.4 %coded_sum.2.refs_1_ = s16[2,272,768]{2,1,0:T(8,128)(2,1)} custom-call(s32[2]{0:T(128)} %pad_add_fusion.refs_0_, bf16[1024,1024]{1,0:T(8,128)(2,1)} %bitcast.27, bf16[1024,1024]{1,0:T(8,128)(2,1)} %bitcast.28, bf16[512,768]{1,0:T(8,128)(2,1)} %copy-done.2, bf16[512,768]{1,0:T(8,128)(2,1)} %collective-permute-done.refs_4_), custom_call_target="tpu_custom_call" | custom-call | flops 1024 | bytes 1024 | tf_op jit(solution)/shard_map/coded_sum/pallas_call | solution.py:137
  61.3 5.5 %all-to-all-start.1 = ((bf16[16,64,1024]{2,1,0:T(8,128)(2,1)}), bf16[16,64,1024]{2,1,0:T(8,128)(2,1)S(1)}, u32[]{:S(2)}, u32[]{:S(2)}) async-start(bf16[16,64,1024]{2,1,0:T(8,128)(2,1)} %bitcast.33), calls=%async_computation.1 | async-start | bytes 4194304 | tf_op jit(solution)/shard_map/all_to_all | solution.py:343
  69.5 4.4 %coded_sum.3 = s16[2,272,768]{2,1,0:T(8,128)(2,1)} custom-call(s32[2]{0:T(128)} %pad_add_fusion.refs_0_, bf16[1024,1024]{1,0:T(8,128)(2,1)} %bitcast.29, bf16[1024,1024]{1,0:T(8,128)(2,1)} %bitcast.30, bf16[512,768]{1,0:T(8,128)(2,1)} %copy-done.2, bf16[512,768]{1,0:T(8,128)(2,1)} %collective-permute-done.refs_4_), custom_call_target="tpu_custom_call" | custom-call | flops 1024 | bytes 1024 | tf_op jit(solution)/shard_map/coded_sum/pallas_call | solution.py:137
  78.6 41.1 %all-to-all-done.1 = bf16[16,64,1024]{2,1,0:T(8,128)(2,1)S(1)} async-done(((bf16[16,64,1024]{2,1,0:T(8,128)(2,1)}), bf16[16,64,1024]{2,1,0:T(8,128)(2,1)S(1)}, u32[]{:S(2)}, u32[]{:S(2)}) %all-to-all-start.1) | async-done | bytes 2097184 | tf_op jit(solution)/shard_map/all_to_all | solution.py:343
  121.0 6.3 %own_sum.1.refs_0_ = f32[1024,768]{1,0:T(8,128)} custom-call(s32[2]{0:T(128)} %pad_add_fusion.refs_0_, bf16[1024,1024]{1,0:T(8,128)(2,1)} %bitcast.31, bf16[1024,1024]{1,0:T(8,128)(2,1)} %bitcast.32, bf16[512,768]{1,0:T(8,128)(2,1)} %copy-done.2, bf16[512,768]{1,0:T(8,128)(2,1)} %collective-permute-done.refs_4_), custom_call_target="tpu_custom_call" | custom-call | flops 1024 | bytes 1024 | tf_op jit(solution)/shard_map/own_sum/pallas_call | solution.py:137
  127.4 4.8 %adam.2 = (f32[1024,768]{1,0:T(8,128)}, bf16[1024,768]{1,0:T(8,128)(2,1)}, bf16[1024,768]{1,0:T(8,128)(2,1)}, f32[1]{0:T(128)}) custom-call(f32[1024,768]{1,0:T(8,128)} %own_sum.1.refs_0_, s16[2,272,768]{2,1,0:T(8,128)(2,1)} %collective-permute-done.2.refs_1_, f32[1024,768]{1,0:T(8,128)} %refs_2_.3, bf16[1024,768]{1,0:T(8,128)(2,1)} %refs_3_.3, ...), custom_call_target="tpu_custom_call" | custom-call | flops 1024 | bytes 1024 | tf_op jit(solution)/shard_map/adam/pallas_call | solution.py:242
  132.2 10.4 %collective-permute-done.1.refs_1_ = s16[2,272,768]{2,1,0:T(8,128)(2,1)} collective-permute-done((s16[2,272,768]{2,1,0:T(8,128)(2,1)}, s16[2,272,768]{2,1,0:T(8,128)(2,1)}, u32[]{:S(2)}, u32[]{:S(2)}) %collective-permute-start.1) | collective-permute-done | bytes 835616 | tf_op jit(solution)/shard_map/ppermute | solution.py:333
  142.6 5.4 %adam.3 = (f32[1024,768]{1,0:T(8,128)}, bf16[1024,768]{1,0:T(8,128)(2,1)}, bf16[1024,768]{1,0:T(8,128)(2,1)}, f32[1]{0:T(128)}) custom-call(f32[1024,768]{1,0:T(8,128)} %own_sum.1.refs_0_, s16[2,272,768]{2,1,0:T(8,128)(2,1)} %collective-permute-done.1.refs_1_, f32[1024,768]{1,0:T(8,128)} %refs_2_.3, ...), custom_call_target="tpu_custom_call", output_to_operand_aliasing={{0}: (5, {}), {1}: (6, {}), {2}: (7, {})} | custom-call | flops 1024 | bytes 1024 | tf_op jit(solution)/shard_map/adam/pallas_call | solution.py:242
  149.0 2.9 %collective-permute-done.3 = f32[1]{0:T(128)} collective-permute-done((f32[1]{0:T(128)}, f32[1]{0:T(128)}, u32[]{:S(2)}, u32[]{:S(2)}) %collective-permute-start.3) | collective-permute-done | bytes 36 | tf_op jit(solution)/shard_map/ppermute | solution.py:333
  153.1 3.6 %collective-permute-start.4 = (f32[1]{0:T(128)}, f32[1]{0:T(128)}, u32[]{:S(2)}, u32[]{:S(2)}) collective-permute-start(f32[1]{0:T(128)} %max.19), channel_id=1, source_target_pairs={{0,2},{1,3},{2,0},{3,1},{4,6},{5,7},{6,4},{7,5},{8,10},{9,11},{10,... | collective-permute-start | bytes 20 | tf_op jit(solution)/shard_map/ppermute | solution.py:333
  161.8 4.6 %collective-permute-start.14 = (bf16[512,768]{1,0:T(8,128)(2,1)S(1)}, bf16[512,768]{1,0:T(8,128)(2,1)S(1)}, u32[]{:S(2)}, u32[]{:S(2)}) collective-permute-start(bf16[512,768]{1,0:T(8,128)(2,1)S(1)} %get-tuple-element.21.refs_0_), channel_id=1, source_target_pairs={{0,1},{1,2},{2,3},{4,5},{5,6},{6,7},{8,9},{9,10},{10,11},{12,13},{... | collective-permute-start | bytes 2359304 | tf_op jit(solution)/shard_map/ppermute | solution.py:377
  167.7 5.4 %collective-permute-start.8 = (bf16[512,768]{1,0:T(8,128)(2,1)S(1)}, bf16[512,768]{1,0:T(8,128)(2,1)}, u32[]{:S(2)}, u32[]{:S(2)}) collective-permute-start(bf16[512,768]{1,0:T(8,128)(2,1)S(1)} %get-tuple-element.22.refs_1_), channel_id=1, source_target_pairs={{0,1},{1,2},{2,3},{4,5},{5,6},{6,7},{8,9},{9,10},{10,11},{12,13},{... | collective-permute-start | bytes 2359304 | tf_op jit(solution)/shard_map/ppermute | solution.py:377
  173.1 3.0 %place.7.refs_2_ = bf16[4096,768]{1,0:T(8,128)(2,1)} custom-call(s32[4]{0:T(128)} %pad_add_fusion.1.table_ref, bf16[512,768]{1,0:T(8,128)(2,1)} %copy-done.5, bf16[512,768]{1,0:T(8,128)(2,1)} %copy-done.4), custom_call_target="tpu_custom_call" | custom-call | flops 68719476736 | bytes 68719476736 | tf_op jit(solution)/shard_map/place/pallas_call | solution.py:304
  176.1 6.9 %collective-permute-done.11.refs_0_ = bf16[512,768]{1,0:T(8,128)(2,1)} collective-permute-done((bf16[512,768]{1,0:T(8,128)(2,1)S(1)}, bf16[512,768]{1,0:T(8,128)(2,1)}, u32[]{:S(2)}, u32[]{:S(2)}) %collective-permute-start.11) | collective-permute-done | bytes 786464 | tf_op jit(solution)/shard_map/ppermute | solution.py:376
  184.3 4.5 %collective-permute-start.15 = (bf16[512,768]{1,0:T(8,128)(2,1)S(1)}, bf16[512,768]{1,0:T(8,128)(2,1)S(1)}, u32[]{:S(2)}, u32[]{:S(2)}) collective-permute-start(bf16[512,768]{1,0:T(8,128)(2,1)S(1)} %collective-permute-done.14.refs_1_), channel_id=1, source_target_pairs={{0,1},{1,2},{2,3},{4,5},{5,6},{6,7},{8,9},{9,10},{10,11},{12,13},{... | collective-permute-start | bytes 2359304 | tf_op jit(solution)/shard_map/ppermute | solution.py:377
  188.9 10.8 %collective-permute-done.5.refs_0_ = bf16[512,768]{1,0:T(8,128)(2,1)S(1)} collective-permute-done((bf16[512,768]{1,0:T(8,128)(2,1)S(1)}, bf16[512,768]{1,0:T(8,128)(2,1)S(1)}, u32[]{:S(2)}, u32[]{:S(2)}) %collective-permute-start.5) | collective-permute-done | bytes 786464 | tf_op jit(solution)/shard_map/ppermute | solution.py:376
  201.2 5.4 %collective-permute-start.9 = (bf16[512,768]{1,0:T(8,128)(2,1)}, bf16[512,768]{1,0:T(8,128)(2,1)}, u32[]{:S(2)}, u32[]{:S(2)}) collective-permute-start(bf16[512,768]{1,0:T(8,128)(2,1)} %collective-permute-done.8.refs_1_), channel_id=1, source_target_pairs={{0,1},{1,2},{2,3},{4,5},{5,6},{6,7},{8,9},{9,10},{10,11},{12,13},{... | collective-permute-start | bytes 2359304 | tf_op jit(solution)/shard_map/ppermute | solution.py:377
  206.6 2.7 %place.8.refs_2_ = bf16[4096,768]{1,0:T(8,128)(2,1)} custom-call(s32[4]{0:T(128)} %add_add_fusion.5.table_ref, bf16[512,768]{1,0:T(8,128)(2,1)} %collective-permute-done.11.refs_0_, bf16[512,768]{1,0:T(8,128)(2,1)} %copy-done.9, bf16[4096,768]{1,0:T(8,128)(2,1)} %place.7.refs_2_), custom_call_target="tpu_custom_call", output_to_operand_aliasing={{}: (3, {})} | custom-call | flops 68719476736 | bytes 68719476736 | tf_op jit(solution)/shard_map/place/pallas_call | solution.py:304
  209.3 2.7 %place.9.refs_2_ = bf16[4096,768]{1,0:T(8,128)(2,1)} custom-call(s32[4]{0:T(128)} %add_add_fusion.4.table_ref, bf16[512,768]{1,0:T(8,128)(2,1)} %copy-done.7, bf16[512,768]{1,0:T(8,128)(2,1)} %collective-permute-done.8.refs_1_, bf16[4096,768]{1,0:T(8,128)(2,1)} %place.8.refs_2_), custom_call_target="tpu_custom_call", output_to_operand_aliasing={{}: (3, {})} | custom-call | flops 68719476736 | bytes 68719476736 | tf_op jit(solution)/shard_map/place/pallas_call | solution.py:304
  212.0 4.6 %collective-permute-done.12.refs_0_ = bf16[512,768]{1,0:T(8,128)(2,1)S(1)} collective-permute-done((bf16[512,768]{1,0:T(8,128)(2,1)}, bf16[512,768]{1,0:T(8,128)(2,1)S(1)}, u32[]{:S(2)}, u32[]{:S(2)}) %collective-permute-start.12) | collective-permute-done | bytes 786464 | tf_op jit(solution)/shard_map/ppermute | solution.py:376
  218.0 4.4 %collective-permute-start.16 = (bf16[512,768]{1,0:T(8,128)(2,1)S(1)}, bf16[512,768]{1,0:T(8,128)(2,1)S(1)}, u32[]{:S(2)}, u32[]{:S(2)}) collective-permute-start(bf16[512,768]{1,0:T(8,128)(2,1)S(1)} %collective-permute-done.15.refs_1_), channel_id=1, source_target_pairs={{0,1},{1,2},{2,3},{4,5},{5,6},{6,7},{8,9},{9,10},{10,11},{12,13},{... | collective-permute-start | bytes 2359304 | tf_op jit(solution)/shard_map/ppermute | solution.py:377
  222.5 12.5 %collective-permute-done.9.refs_1_ = bf16[512,768]{1,0:T(8,128)(2,1)} collective-permute-done((bf16[512,768]{1,0:T(8,128)(2,1)}, bf16[512,768]{1,0:T(8,128)(2,1)}, u32[]{:S(2)}, u32[]{:S(2)}) %collective-permute-start.9) | collective-permute-done | bytes 786464 | tf_op jit(solution)/shard_map/ppermute | solution.py:377
  235.0 5.3 %collective-permute-start.10 = (bf16[512,768]{1,0:T(8,128)(2,1)}, bf16[512,768]{1,0:T(8,128)(2,1)}, u32[]{:S(2)}, u32[]{:S(2)}) collective-permute-start(bf16[512,768]{1,0:T(8,128)(2,1)} %collective-permute-done.9.refs_1_), channel_id=1, source_target_pairs={{0,1},{1,2},{2,3},{4,5},{5,6},{6,7},{8,9},{9,10},{10,11},{12,13},{... | collective-permute-start | bytes 2359304 | tf_op jit(solution)/shard_map/ppermute | solution.py:377
  241.6 2.7 %place.10.refs_2_ = bf16[4096,768]{1,0:T(8,128)(2,1)} custom-call(s32[4]{0:T(128)} %add_add_fusion.3.table_ref, bf16[512,768]{1,0:T(8,128)(2,1)} %copy-done.6, bf16[512,768]{1,0:T(8,128)(2,1)} %copy-done.8, bf16[4096,768]{1,0:T(8,128)(2,1)} %place.9.refs_2_), custom_call_target="tpu_custom_call", output_to_operand_aliasing={{}: (3, {})} | custom-call | flops 68719476736 | bytes 68719476736 | tf_op jit(solution)/shard_map/place/pallas_call | solution.py:304
  244.3 2.7 %place.11.refs_2_ = bf16[4096,768]{1,0:T(8,128)(2,1)} custom-call(s32[4]{0:T(128)} %add_add_fusion.2.table_ref, bf16[512,768]{1,0:T(8,128)(2,1)} %collective-permute-done.6.refs_0_, bf16[512,768]{1,0:T(8,128)(2,1)} %collective-permute-done.9.refs_1_, bf16[4096,768]{1,0:T(8,128)(2,1)} %place.10.refs_2_), custom_call_target="tpu_custom_call", output_to_operand_aliasing={{}: (3, {})} | custom-call | flops 68719476736 | bytes 68719476736 | tf_op jit(solution)/shard_map/place/pallas_call | solution.py:304
  247.0 3.3 %collective-permute-done.13.refs_0_ = bf16[512,768]{1,0:T(8,128)(2,1)S(1)} collective-permute-done((bf16[512,768]{1,0:T(8,128)(2,1)S(1)}, bf16[512,768]{1,0:T(8,128)(2,1)S(1)}, u32[]{:S(2)}, u32[]{:S(2)}) %collective-permute-start.13) | collective-permute-done | bytes 786464 | tf_op jit(solution)/shard_map/ppermute | solution.py:376
  255.3 9.2 %collective-permute-done.10.refs_1_ = bf16[512,768]{1,0:T(8,128)(2,1)} collective-permute-done((bf16[512,768]{1,0:T(8,128)(2,1)}, bf16[512,768]{1,0:T(8,128)(2,1)}, u32[]{:S(2)}, u32[]{:S(2)}) %collective-permute-start.10) | collective-permute-done | bytes 786464 | tf_op jit(solution)/shard_map/ppermute | solution.py:377
  264.6 2.7 %place.13 = bf16[4096,768]{1,0:T(8,128)(2,1)} custom-call(s32[4]{0:T(128)} %add_add_fusion.table_ref, bf16[512,768]{1,0:T(8,128)(2,1)} %collective-permute-done.7.refs_0_, bf16[512,768]{1,0:T(8,128)(2,1)} %collective-permute-done.10.refs_1_, bf16[4096,768]{1,0:T(8,128)(2,1)} %place.12.refs_2_), custom_call_target="tpu_custom_call", output_to_operand_aliasing={{}: (3, {})} | custom-call | flops 68719476736 | bytes 68719476736 | tf_op jit(solution)/shard_map/place/pallas_call | solution.py:304
  (61 shorter events, 32.3 us)
Async XLA Ops:
  4.2 6.3 %copy-start.12 = (s32[8]{0:T(128)S(1)}, s32[8]{0:T(128)}, u32[]{:S(2)}) copy-start(s32[8]{0:T(128)} %param.8) | copy-start | bytes 100
  4.2 51.4 %all-to-all-start = ((bf16[16,64,1024]{2,1,0:T(8,128)(2,1)}), bf16[16,64,1024]{2,1,0:T(8,128)(2,1)S(1)}, u32[]{:S(2)}, u32[]{:S(2)}) async-start(bf16[16,64,1024]{2,1,0:T(8,128)(2,1)} %bitcast.34), calls=%async_computation | async-start | bytes 4194304 | tf_op jit(solution)/shard_map/all_to_all | solution.py:343
  12.0 5.6 %copy-start.2 = (bf16[512,768]{1,0:T(8,128)(2,1)}, bf16[512,768]{1,0:T(8,128)(2,1)S(1)}, u32[]{:S(2)}) copy-start(bf16[512,768]{1,0:T(8,128)(2,1)S(1)} %broadcast_select_fusion.refs_3_) | copy-start | bytes 2359300
  12.0 43.6 %collective-permute-start = (bf16[512,768]{1,0:T(8,128)(2,1)S(1)}, bf16[512,768]{1,0:T(8,128)(2,1)}, u32[]{:S(2)}, u32[]{:S(2)}) collective-permute-start(bf16[512,768]{1,0:T(8,128)(2,1)S(1)} %broadcast_select_fusion.refs_3_), channel_id=1, source_target_pairs={{0,1},{1,0},{2,3},{3,2},{4,5},{5,4},{6,7},{7,6},{8,9},{9,8},{10,11... | collective-permute-start | bytes 2359304 | tf_op jit(solution)/shard_map/ppermute | solution.py:333
  55.6 1.3 copy-start
  61.3 5.5 %copy-start.3 = (s16[2,272,768]{2,1,0:T(8,128)(2,1)S(1)}, s16[2,272,768]{2,1,0:T(8,128)(2,1)}, u32[]{:S(2)}) copy-start(s16[2,272,768]{2,1,0:T(8,128)(2,1)} %coded_sum.2.refs_1_) | copy-start | bytes 2506756
  61.3 58.4 %all-to-all-start.1 = ((bf16[16,64,1024]{2,1,0:T(8,128)(2,1)}), bf16[16,64,1024]{2,1,0:T(8,128)(2,1)S(1)}, u32[]{:S(2)}, u32[]{:S(2)}) async-start(bf16[16,64,1024]{2,1,0:T(8,128)(2,1)} %bitcast.33), calls=%async_computation.1 | async-start | bytes 4194304 | tf_op jit(solution)/shard_map/all_to_all | solution.py:343
  66.8 60.5 %collective-permute-start.2 = (s16[2,272,768]{2,1,0:T(8,128)(2,1)S(1)}, s16[2,272,768]{2,1,0:T(8,128)(2,1)}, u32[]{:S(2)}, u32[]{:S(2)}) collective-permute-start(s16[2,272,768]{2,1,0:T(8,128)(2,1)S(1)} %copy-done.3), channel_id=1, source_target_pairs={{0,2},{1,3},{2,0},{3,1},{4,6},{5,7},{6,4},{7,5},{8,10},{9,11},{10,... | collective-permute-start | bytes 2506760 | tf_op jit(solution)/shard_map/ppermute | solution.py:333
  73.9 68.7 %collective-permute-start.1 = (s16[2,272,768]{2,1,0:T(8,128)(2,1)}, s16[2,272,768]{2,1,0:T(8,128)(2,1)}, u32[]{:S(2)}, u32[]{:S(2)}) collective-permute-start(s16[2,272,768]{2,1,0:T(8,128)(2,1)} %coded_sum.3), channel_id=1, source_target_pairs={{0,2},{1,3},{2,0},{3,1},{4,6},{5,7},{6,4},{7,5},{8,10},{9,11},{10,... | collective-permute-start | bytes 2506760 | tf_op jit(solution)/shard_map/ppermute | solution.py:333
  119.7 1.3 copy-start.1
  148.0 3.8 %collective-permute-start.3 = (f32[1]{0:T(128)}, f32[1]{0:T(128)}, u32[]{:S(2)}, u32[]{:S(2)}) collective-permute-start(f32[1]{0:T(128)} %get-tuple-element.20), channel_id=1, source_target_pairs={{0,1},{1,0},{2,3},{3,2},{4,5},{5,4},{6,7},{7,6},{8,9},{9,8},{10,11... | collective-permute-start | bytes 20 | tf_op jit(solution)/shard_map/ppermute | solution.py:333
  153.1 4.6 %collective-permute-start.4 = (f32[1]{0:T(128)}, f32[1]{0:T(128)}, u32[]{:S(2)}, u32[]{:S(2)}) collective-permute-start(f32[1]{0:T(128)} %max.19), channel_id=1, source_target_pairs={{0,2},{1,3},{2,0},{3,1},{4,6},{5,7},{6,4},{7,5},{8,10},{9,11},{10,... | collective-permute-start | bytes 20 | tf_op jit(solution)/shard_map/ppermute | solution.py:333
  160.5 12.7 %copy-start.4 = (bf16[512,768]{1,0:T(8,128)(2,1)}, bf16[512,768]{1,0:T(8,128)(2,1)S(1)}, u32[]{:S(2)}) copy-start(bf16[512,768]{1,0:T(8,128)(2,1)S(1)} %get-tuple-element.22.refs_1_) | copy-start | bytes 2359300
  160.5 12.7 %copy-start.5 = (bf16[512,768]{1,0:T(8,128)(2,1)}, bf16[512,768]{1,0:T(8,128)(2,1)S(1)}, u32[]{:S(2)}) copy-start(bf16[512,768]{1,0:T(8,128)(2,1)S(1)} %get-tuple-element.21.refs_0_) | copy-start | bytes 2359300
  160.5 22.5 %collective-permute-start.11 = (bf16[512,768]{1,0:T(8,128)(2,1)S(1)}, bf16[512,768]{1,0:T(8,128)(2,1)}, u32[]{:S(2)}, u32[]{:S(2)}) collective-permute-start(bf16[512,768]{1,0:T(8,128)(2,1)S(1)} %get-tuple-element.21.refs_0_), channel_id=1, source_target_pairs={{1,0},{2,1},{3,2},{5,4},{6,5},{7,6},{9,8},{10,9},{11,10},{13,12},{... | collective-permute-start | bytes 2359304 | tf_op jit(solution)/shard_map/ppermute | solution.py:376
  161.8 22.5 %collective-permute-start.14 = (bf16[512,768]{1,0:T(8,128)(2,1)S(1)}, bf16[512,768]{1,0:T(8,128)(2,1)S(1)}, u32[]{:S(2)}, u32[]{:S(2)}) collective-permute-start(bf16[512,768]{1,0:T(8,128)(2,1)S(1)} %get-tuple-element.21.refs_0_), channel_id=1, source_target_pairs={{0,1},{1,2},{2,3},{4,5},{5,6},{6,7},{8,9},{9,10},{10,11},{12,13},{... | collective-permute-start | bytes 2359304 | tf_op jit(solution)/shard_map/ppermute | solution.py:377
  166.4 33.3 %collective-permute-start.5 = (bf16[512,768]{1,0:T(8,128)(2,1)S(1)}, bf16[512,768]{1,0:T(8,128)(2,1)S(1)}, u32[]{:S(2)}, u32[]{:S(2)}) collective-permute-start(bf16[512,768]{1,0:T(8,128)(2,1)S(1)} %get-tuple-element.22.refs_1_), channel_id=1, source_target_pairs={{1,0},{2,1},{3,2},{5,4},{6,5},{7,6},{9,8},{10,9},{11,10},{13,12},{... | collective-permute-start | bytes 2359304 | tf_op jit(solution)/shard_map/ppermute | solution.py:376
  167.7 33.5 %collective-permute-start.8 = (bf16[512,768]{1,0:T(8,128)(2,1)S(1)}, bf16[512,768]{1,0:T(8,128)(2,1)}, u32[]{:S(2)}, u32[]{:S(2)}) collective-permute-start(bf16[512,768]{1,0:T(8,128)(2,1)S(1)} %get-tuple-element.22.refs_1_), channel_id=1, source_target_pairs={{0,1},{1,2},{2,3},{4,5},{5,6},{6,7},{8,9},{9,10},{10,11},{12,13},{... | collective-permute-start | bytes 2359304 | tf_op jit(solution)/shard_map/ppermute | solution.py:377
  183.0 33.6 %collective-permute-start.12 = (bf16[512,768]{1,0:T(8,128)(2,1)}, bf16[512,768]{1,0:T(8,128)(2,1)S(1)}, u32[]{:S(2)}, u32[]{:S(2)}) collective-permute-start(bf16[512,768]{1,0:T(8,128)(2,1)} %collective-permute-done.11.refs_0_), channel_id=1, source_target_pairs={{1,0},{2,1},{3,2},{5,4},{6,5},{7,6},{9,8},{10,9},{11,10},{13,12},{... | collective-permute-start | bytes 2359304 | tf_op jit(solution)/shard_map/ppermute | solution.py:376
  184.3 22.2 %copy-start.9 = (bf16[512,768]{1,0:T(8,128)(2,1)}, bf16[512,768]{1,0:T(8,128)(2,1)S(1)}, u32[]{:S(2)}) copy-start(bf16[512,768]{1,0:T(8,128)(2,1)S(1)} %collective-permute-done.14.refs_1_) | copy-start | bytes 2359300
  184.3 33.7 %collective-permute-start.15 = (bf16[512,768]{1,0:T(8,128)(2,1)S(1)}, bf16[512,768]{1,0:T(8,128)(2,1)S(1)}, u32[]{:S(2)}, u32[]{:S(2)}) collective-permute-start(bf16[512,768]{1,0:T(8,128)(2,1)S(1)} %collective-permute-done.14.refs_1_), channel_id=1, source_target_pairs={{0,1},{1,2},{2,3},{4,5},{5,6},{6,7},{8,9},{9,10},{10,11},{12,13},{... | collective-permute-start | bytes 2359304 | tf_op jit(solution)/shard_map/ppermute | solution.py:377
  199.7 9.6 %copy-start.7 = (bf16[512,768]{1,0:T(8,128)(2,1)}, bf16[512,768]{1,0:T(8,128)(2,1)S(1)}, u32[]{:S(2)}) copy-start(bf16[512,768]{1,0:T(8,128)(2,1)S(1)} %collective-permute-done.5.refs_0_) | copy-start | bytes 2359300
  199.7 40.5 %collective-permute-start.6 = (bf16[512,768]{1,0:T(8,128)(2,1)S(1)}, bf16[512,768]{1,0:T(8,128)(2,1)}, u32[]{:S(2)}, u32[]{:S(2)}) collective-permute-start(bf16[512,768]{1,0:T(8,128)(2,1)S(1)} %collective-permute-done.5.refs_0_), channel_id=1, source_target_pairs={{1,0},{2,1},{3,2},{5,4},{6,5},{7,6},{9,8},{10,9},{11,10},{13,12},{... | collective-permute-start | bytes 2359304 | tf_op jit(solution)/shard_map/ppermute | solution.py:376
  201.2 33.8 %collective-permute-start.9 = (bf16[512,768]{1,0:T(8,128)(2,1)}, bf16[512,768]{1,0:T(8,128)(2,1)}, u32[]{:S(2)}, u32[]{:S(2)}) collective-permute-start(bf16[512,768]{1,0:T(8,128)(2,1)} %collective-permute-done.8.refs_1_), channel_id=1, source_target_pairs={{0,1},{1,2},{2,3},{4,5},{5,6},{6,7},{8,9},{9,10},{10,11},{12,13},{... | collective-permute-start | bytes 2359304 | tf_op jit(solution)/shard_map/ppermute | solution.py:377
  216.6 25.0 %copy-start.6 = (bf16[512,768]{1,0:T(8,128)(2,1)}, bf16[512,768]{1,0:T(8,128)(2,1)S(1)}, u32[]{:S(2)}) copy-start(bf16[512,768]{1,0:T(8,128)(2,1)S(1)} %collective-permute-done.12.refs_0_) | copy-start | bytes 2359300
  216.6 33.7 %collective-permute-start.13 = (bf16[512,768]{1,0:T(8,128)(2,1)S(1)}, bf16[512,768]{1,0:T(8,128)(2,1)S(1)}, u32[]{:S(2)}, u32[]{:S(2)}) collective-permute-start(bf16[512,768]{1,0:T(8,128)(2,1)S(1)} %collective-permute-done.12.refs_0_), channel_id=1, source_target_pairs={{1,0},{2,1},{3,2},{5,4},{6,5},{7,6},{9,8},{10,9},{11,10},{13,12},{... | collective-permute-start | bytes 2359304 | tf_op jit(solution)/shard_map/ppermute | solution.py:376
  218.0 23.5 %copy-start.8 = (bf16[512,768]{1,0:T(8,128)(2,1)}, bf16[512,768]{1,0:T(8,128)(2,1)S(1)}, u32[]{:S(2)}) copy-start(bf16[512,768]{1,0:T(8,128)(2,1)S(1)} %collective-permute-done.15.refs_1_) | copy-start | bytes 2359300
  218.0 33.7 %collective-permute-start.16 = (bf16[512,768]{1,0:T(8,128)(2,1)S(1)}, bf16[512,768]{1,0:T(8,128)(2,1)S(1)}, u32[]{:S(2)}, u32[]{:S(2)}) collective-permute-start(bf16[512,768]{1,0:T(8,128)(2,1)S(1)} %collective-permute-done.15.refs_1_), channel_id=1, source_target_pairs={{0,1},{1,2},{2,3},{4,5},{5,6},{6,7},{8,9},{9,10},{10,11},{12,13},{... | collective-permute-start | bytes 2359304 | tf_op jit(solution)/shard_map/ppermute | solution.py:377
  235.0 29.6 %collective-permute-start.10 = (bf16[512,768]{1,0:T(8,128)(2,1)}, bf16[512,768]{1,0:T(8,128)(2,1)}, u32[]{:S(2)}, u32[]{:S(2)}) collective-permute-start(bf16[512,768]{1,0:T(8,128)(2,1)} %collective-permute-done.9.refs_1_), channel_id=1, source_target_pairs={{0,1},{1,2},{2,3},{4,5},{5,6},{6,7},{8,9},{9,10},{10,11},{12,13},{... | collective-permute-start | bytes 2359304 | tf_op jit(solution)/shard_map/ppermute | solution.py:377
  240.3 24.3 %collective-permute-start.7 = (bf16[512,768]{1,0:T(8,128)(2,1)}, bf16[512,768]{1,0:T(8,128)(2,1)}, u32[]{:S(2)}, u32[]{:S(2)}) collective-permute-start(bf16[512,768]{1,0:T(8,128)(2,1)} %collective-permute-done.6.refs_0_), channel_id=1, source_target_pairs={{1,0},{2,1},{3,2},{5,4},{6,5},{7,6},{9,8},{10,9},{11,10},{13,12},{... | collective-permute-start | bytes 2359304 | tf_op jit(solution)/shard_map/ppermute | solution.py:376
  250.3 1.5 copy-start.10
  251.7 0.9 copy-start.11

commit v3 on v2

--- a/solution.py
+++ b/solution.py
@@ -15,14 +15,14 @@
 weight_decay = 1.0
 peak_eps = 1e-06
 
-VMEM_LIMIT = 60 * 1024 * 1024
+MIB = 1024 * 1024
 LEVELS = 32000.0
-PLACE_HINT = 1 << 36
+PLACE_HINT = 1 << 32
 TAIL = 16
 
 
-def params():
-    return pltpu.CompilerParams(vmem_limit_bytes=VMEM_LIMIT)
+def params(mib=24):
+    return pltpu.CompilerParams(vmem_limit_bytes=mib * MIB)
 
 
 def hint(amount):
@@ -70,7 +70,7 @@
             pltpu.SemaphoreType.DMA((strips * count,)),
             pltpu.SemaphoreType.DMA((strips * count,)),
         ],
-        compiler_params=params(),
+        compiler_params=params(60),
         cost_estimate=hint(1024),
         name="pick_columns",
     )(chunks, x)
@@ -112,18 +112,26 @@
     return total
 
 
+def encode(values, out):
+    block = values.shape[0]
+    top = jnp.maximum(jnp.max(jnp.abs(values), axis=0, keepdims=True), 1e-30)
+    exponent = jnp.floor(jnp.log2(top)) + 1.0
+    codes = jnp.round(values * (1.0 / (jnp.exp2(exponent) * (1.0 / LEVELS))))
+    out[:block, :] = codes.astype(jnp.int32).astype(jnp.int16)
+    out[block:, :] = jnp.broadcast_to(
+        exponent.astype(jnp.int32), (TAIL, values.shape[1])
+    ).astype(jnp.int16)
+
+
+def decode(coded, rows):
+    block = coded.shape[0] - TAIL
+    exponent = coded[block : block + 1, :].astype(jnp.int32).astype(jnp.float32)
+    codes = coded[rows, :].astype(jnp.int32).astype(jnp.float32)
+    return codes * (jnp.exp2(exponent) * (1.0 / LEVELS))
+
+
 def code_kernel(count, *refs):
-    out = refs[-1]
-    total = group_sum(count, refs)
-    block = total.shape[0]
-    top = jnp.maximum(jnp.max(jnp.abs(total), axis=0, keepdims=True), 1e-30)
-    exponent = jnp.floor(jnp.log2(top)) + 1.0
-    step = jnp.exp2(exponent) * (1.0 / LEVELS)
-    codes = jnp.round(total * (1.0 / step))
-    out[0, :block, :] = codes.astype(jnp.int32).astype(jnp.int16)
-    out[0, block:, :] = jnp.broadcast_to(
-        exponent.astype(jnp.int32), (TAIL, total.shape[1])
-    ).astype(jnp.int16)
+    encode(group_sum(count, refs), refs[-1].at[0])
 
 
 def sum_kernel(count, *refs):
@@ -171,8 +179,9 @@
     return summed(sum_kernel, rows, order, hidden, 0, width, block, shape, spec, "own_sum")
 
 
-def adam_kernel(arrays, at, block, size, *refs):
+def adam_kernel(arrays, at, block, size, ahead, *refs):
     streams = refs[:5]
+    refs, (early,) = (refs[:-11] + refs[-10:], refs[-11:-10]) if ahead else (refs, (None,))
     outs, top_ref = refs[-14:-11], refs[-11]
     buffers, results = refs[-10:-5], refs[-5:-2]
     arrived, left = refs[-2:]
@@ -204,9 +213,7 @@
             copy.wait()
         here = pl.ds(i * size, size)
         b, off = i * size // block, i * size % block
-        exponent = coded[b, block : block + 1, :].astype(jnp.int32).astype(jnp.float32)
-        codes = coded[b, off : off + size, :].astype(jnp.int32).astype(jnp.float32)
-        grad = own[here, :] + codes * (jnp.exp2(exponent) * (1.0 / LEVELS))
+        grad = own[here, :] + decode(coded.at[b], pl.ds(off, size))
         first = beta_one * one[here, :].astype(jnp.float32) + (1.0 - beta_one) * grad
         second = beta_two * two[here, :].astype(jnp.float32) + (1.0 - beta_two) * grad * grad
         update = (first * (1.0 / correct_one)) / (
@@ -221,6 +228,8 @@
             copy.start()
         top = jnp.max(jnp.abs(new_master), axis=0, keepdims=True)
         highest = top if highest is None else jnp.maximum(highest, top)
+        if ahead and off + size == block:
+            encode(results[0][pl.ds(b * block, block), :], early.at[b])
     peak = jnp.max(highest)
     if arrays:
         peak = jnp.maximum(peak, refs[5 + arrays][0])
@@ -230,7 +239,7 @@
             copy.wait()
 
 
-def adam(own, coded, master, one, two, at, block, earlier=()):
+def adam(own, coded, master, one, two, at, block, ahead, earlier=()):
     shard, ffn = master.shape
     size = min(128, block)
     width = coded.shape[0] * block
@@ -240,82 +249,110 @@
     arrays = max(len(earlier) - 1, 0)
     types = (jnp.float32, jnp.bfloat16, jnp.bfloat16)
     return pl.pallas_call(
-        functools.partial(adam_kernel, arrays, at, block, size),
+        functools.partial(adam_kernel, arrays, at, block, size, ahead),
         out_shape=tuple(jax.ShapeDtypeStruct((shard, ffn), t) for t in types)
-        + (jax.ShapeDtypeStruct((1,), jnp.float32),),
+        + (jax.ShapeDtypeStruct((1,), jnp.float32),)
+        + (jax.ShapeDtypeStruct(coded.shape, jnp.int16),) * ahead,
         in_specs=[anywhere] * (5 + arrays) + [scalar] * (arrays > 0),
-        out_specs=(anywhere, anywhere, anywhere, scalar),
+        out_specs=(anywhere, anywhere, anywhere, scalar)
+        + (pl.BlockSpec(memory_space=pltpu.VMEM),) * ahead,
         scratch_shapes=[pltpu.VMEM((width, ffn), jnp.float32), pltpu.VMEM(coded.shape, jnp.int16)]
         + [pltpu.VMEM((width, ffn), t) for t in types * 2]
         + [pltpu.SemaphoreType.DMA((steps, 5)), pltpu.SemaphoreType.DMA((steps, 3))],
         input_output_aliases={5 + k: k for k in range(arrays)},
-        compiler_params=params(),
+        compiler_params=params(60),
         cost_estimate=hint(1024),
         name="adam",
     )(own, coded, master, one, two, *earlier)
 
 
-def place_kernel(count, strips, table_ref, *refs):
-    pieces = refs[:count]
-    whole, buffer, sems_in, sems_out = refs[-4:]
-    rows = pieces[0].shape[0]
+def scale_kernel(peak_ref, weight_ref, *refs):
+    out_ref = refs[-1]
+    factor = 1.0 / (jnp.full((1, out_ref.shape[1]), peak_ref[0], jnp.float32) + peak_eps)
+    out_ref[...] = (weight_ref[...] * factor).astype(jnp.bfloat16)
+
+
+def scale(weight, peak, at, rows, after):
+    ffn = weight.shape[1]
+    block = rows // 2
+    return pl.pallas_call(
+        scale_kernel,
+        out_shape=jax.ShapeDtypeStruct((rows, ffn), jnp.bfloat16),
+        grid=(2,),
+        in_specs=[
+            pl.BlockSpec(memory_space=pltpu.SMEM),
+            pl.BlockSpec((block, ffn), lambda i: (at // block + i, 0)),
+        ]
+        + [pl.BlockSpec(memory_space=pl.ANY)] * len(after),
+        out_specs=pl.BlockSpec((block, ffn), lambda i: (i, 0)),
+        compiler_params=params(),
+        cost_estimate=hint(1024),
+        name="scale",
+    )(peak, weight, *after)
+
+
+def place_kernel(strips, coded, table_ref, factor_ref, piece, *refs):
+    whole, landed, scaled, sems_in, sems_out = refs[-5:]
+    rows = scaled.shape[0]
     size = rows // strips
-
-    def come(k, j):
-        strip = pl.ds(j * size, size)
-        return pltpu.make_async_copy(
-            pieces[k].at[strip, :], buffer.at[k, strip, :], sems_in.at[k, j]
-        )
-
-    def leave(k, j):
-        at = pl.multiple_of(table_ref[2 * k] * rows + j * size, size)
-        return pltpu.make_async_copy(
-            buffer.at[k, pl.ds(j * size, size), :], whole.at[pl.ds(at, size), :], sems_out.at[k, j]
-        )
-
-    for k in range(count):
-
-        @pl.when(table_ref[2 * k + 1] > 0)
-        def _():
-            for j in range(strips):
-                come(k, j).start()
-
-    for k in range(count):
-
-        @pl.when(table_ref[2 * k + 1] > 0)
-        def _():
-            for j in range(strips):
-                come(k, j).wait()
-                leave(k, j).start()
-
-    for k in range(count):
-
-        @pl.when(table_ref[2 * k + 1] > 0)
-        def _():
-            for j in range(strips):
-                leave(k, j).wait()
-
-
-def place(whole, shape, pieces, spots):
-    count, strips = len(pieces), 4
-    table = jnp.stack([jnp.asarray(v).astype(jnp.int32) for spot in spots for v in spot])
+    at = pl.multiple_of(table_ref[0] * rows, rows)
+    comes, leaves = [], []
+    for j in range(strips):
+        here = pl.ds(j * size, size)
+        comes.append(
+            pltpu.make_async_copy(piece.at[here, :], landed.at[here, :], sems_in.at[j])
+        )
+        leaves.append(
+            pltpu.make_async_copy(
+                (scaled if coded else landed).at[here, :],
+                whole.at[pl.ds(at + j * size, size), :],
+                sems_out.at[j],
+            )
+        )
+    if coded:
+        last = pl.ds(rows, TAIL)
+        comes.append(
+            pltpu.make_async_copy(piece.at[last, :], landed.at[last, :], sems_in.at[strips])
+        )
+    for copy in comes:
+        copy.start()
+    if coded:
+        comes[-1].wait()
+    for j in range(strips):
+        comes[j].wait()
+        if coded:
+            here = pl.ds(j * size, size)
+            values = decode(landed, here) * factor_ref[0]
+            scaled[here, :] = values.astype(jnp.bfloat16)
+        leaves[j].start()
+    for copy in leaves:
+        copy.wait()
+
+
+def place(whole, shape, piece, spot, factor):
+    coded = piece.dtype == jnp.int16
+    rows, ffn = piece.shape
+    rows -= TAIL * coded
+    strips = 4
     anywhere = pl.BlockSpec(memory_space=pl.ANY)
+    scalars = pl.BlockSpec(memory_space=pltpu.SMEM)
     earlier = () if whole is None else (whole,)
     return pl.pallas_call(
-        functools.partial(place_kernel, count, strips),
+        functools.partial(place_kernel, strips, coded),
         out_shape=jax.ShapeDtypeStruct(shape, jnp.bfloat16),
-        in_specs=[pl.BlockSpec(memory_space=pltpu.SMEM)] + [anywhere] * (count + len(earlier)),
+        in_specs=[scalars, scalars, anywhere] + [anywhere] * len(earlier),
         out_specs=anywhere,
         scratch_shapes=[
-            pltpu.VMEM((count,) + pieces[0].shape, jnp.bfloat16),
-            pltpu.SemaphoreType.DMA((count, strips)),
-            pltpu.SemaphoreType.DMA((count, strips)),
+            pltpu.VMEM(piece.shape, piece.dtype),
+            pltpu.VMEM((rows, ffn), jnp.bfloat16),
+            pltpu.SemaphoreType.DMA((strips + 1,)),
+            pltpu.SemaphoreType.DMA((strips,)),
         ],
-        input_output_aliases={1 + count: 0} if earlier else {},
+        input_output_aliases={3: 0} if earlier else {},
         compiler_params=params(),
         cost_estimate=hint(PLACE_HINT),
         name="place",
-    )(table, *pieces, *earlier)
+    )(spot.astype(jnp.int32).reshape(1), factor, piece, *earlier)
 
 
 def local(out_grad, hidden_saved, recv_counts, master_weight, moment_one, moment_two):
@@ -326,7 +363,7 @@
     me = far * half + near
     capacity = out_grad.shape[0] // experts
     shard, ffn = master_weight.shape
-    block = min(256, shard // 2)
+    block, part = min(256, shard // 2), shard // 2
     chain = ("far", "near")
 
     def swap(x, k):
@@ -337,54 +374,71 @@
     hiddens = [hidden] + [swap(hidden, k) for k in range(1, half)]
     order = jnp.stack([near ^ k for k in range(half)]).astype(jnp.int32)
 
-    def arrive(side, after):
-        chunks = (side * half + jnp.arange(half)).astype(jnp.int32)
-        picked = gate(pick_columns(out_grad, chunks, shard), after)
+    def arrive(side, at, width, after):
+        chunks = ((side * half + jnp.arange(half)) * shard + at) // width
+        picked = gate(pick_columns(out_grad, chunks.astype(jnp.int32), width), after)
         return lax.all_to_all(picked, ("near", "expert"), 0, 0, tiled=True)
 
-    part = shard // 2
-    got = arrive(1 - far, ())
-    partials = [coded_sum(got, order, hiddens, p * part, part, block) for p in range(2)]
+    got = arrive(1 - far, 0, shard, ())
+    partials = [
+        coded_sum(got, order, hiddens, at, block, block) for at in range(0, shard, block)
+    ]
     coded = [swap(partial, half) for partial in partials]
 
-    got = arrive(far, (partials[0],))
+    got = arrive(far, 0, shard, (partials[0],))
     own = own_sum(got, order, hiddens, block)
-    results = ()
-    for p in range(2):
+    results, ahead = (), []
+    for p, codes in enumerate(coded):
+        early = p * block < part
         results = adam(
-            own, coded[p], master_weight, moment_one, moment_two, p * part, block, tuple(results)
-        )
+            own,
+            codes,
+            master_weight,
+            moment_one,
+            moment_two,
+            p * block,
+            block,
+            early,
+            tuple(results),
+        )
+        if early:
+            *results, piece = results
+            ahead.append(piece[0])
     new_master, new_one, new_two, peak = results
 
-    step = 1
-    while step < replicas:
+    beside = [swap(piece, 1) for piece in ahead]
+    step = half
+    while step:
         peak = jnp.maximum(peak, swap(peak, step))
-        step *= 2
-
-    pieces = 2
-    size = shard // pieces
+        step //= 2
+    late = scale(new_master, peak, part, part, beside)
+    factor = 1.0 / (peak + peak_eps)
+
+    def spread(piece, next_to=None):
+        held, distance = [(piece, me)], half
+        while distance:
+            for x, source in list(held):
+                if next_to is not None and distance == 1 and x is piece:
+                    got = next_to
+                else:
+                    got = swap(x, distance)
+                held.append((got, source ^ distance))
+            distance //= 2
+        return held
+
+    last = spread(late)
+    flows = [(part, last)]
+    for p, piece in enumerate(ahead):
+        flows.append((p * block, spread(gate(piece, (last[1][0],)), beside[p])))
+    last[0] = (gate(late, (flows[1][1][1][0],)), me)
     whole_shape = (replicas * shard, ffn)
-    inverse = 1.0 / (peak + peak_eps)
-    down = [
-        (new_master[i * size : (i + 1) * size] * inverse).astype(jnp.bfloat16)
-        for i in range(pieces)
-    ]
-    up = list(down)
-    scaled = place(None, whole_shape, down, [(me * pieces + i, 1) for i in range(pieces)])
-    for s in range(1, replicas):
-        for i in range(pieces):
-            down[i] = lax.ppermute(down[i], chain, [(j, j - 1) for j in range(1, replicas)])
-            up[i] = lax.ppermute(up[i], chain, [(j, j + 1) for j in range(replicas - 1)])
-        for i in range(pieces):
-            scaled = place(
-                scaled,
-                whole_shape,
-                [down[i], up[i]],
-                [
-                    (jnp.minimum(me + s, replicas - 1) * pieces + i, me + s < replicas),
-                    (jnp.maximum(me - s, 0) * pieces + i, me >= s),
-                ],
-            )
+    scaled = None
+    for i in range(replicas):
+        for at, held in flows:
+            got, source = held[i]
+            rows = part if at == part else block
+            spot = (source * shard + at) // rows
+            scaled = place(scaled, whole_shape, got, spot, factor)
     return new_master, new_one, new_two, scaled, peak
 
 

time: 270 us -> 259 us (0.959)
  starting transfers between devices: 58.7 us -> 33.3 us
  Pallas kernels: 50.6 us -> 59.9 us
  waiting for transfers between devices: 142 us -> 150 us
  other arithmetic: 9.47 us -> 2.46 us
  local copies, waits for them, and re-layouts: 3.66 us -> 7.97 us
    ppermute x5 -> x16, waiting for transfers between devices: 51.7 us -> 112 us  [swap(): return lax.ppermute(x, chain, [(i, i ^ k) for i in range(replicas)])]
    ppermute x12 -> x0, waiting for transfers between devices: 49.2 us -> none  [the longest x6 25.6 us: local(): lax.ppermute(down[i], chain, [(j, j - 1) for j in range(1, replicas)])]
    ppermute x12 -> x0, starting transfers between devices: 37.4 us -> none  [the longest x6 29.7 us: local(): lax.ppermute(up[i], chain, [(j, j + 1) for j in range(replicas - 1)])]
    ppermute x5 -> x16, starting transfers between devices: 9.48 us -> 21.4 us  [swap(): return lax.ppermute(x, chain, [(i, i ^ k) for i in range(replicas)])]
    pallas_call x9 -> x17, Pallas kernels: 29.4 us -> 37.2 us  [the longest x12 19.5 us: place(): pl.pallas_call(functools.partial(place_kernel, strips, coded), out_shape=...]
    another operation x7 -> x0, other arithmetic: 4.33 us -> none  [place(): jnp.stack([jnp.asarray(v).astype(jnp.int32) for spot in spots for v in sp...]
    unnamed x26 -> x30, local copies, waits for them, and re-layouts: 3.57 us -> 7.88 us
    all_to_all x2, waiting for transfers between devices: 41.2 us -> 37.7 us  [arrive(): return lax.all_to_all(picked, ('near', 'expert'), 0, 0, tiled=True)]
  transfers between devices with their start and end apart: 19 -> 18, of which waited for: 15 -> 9; matrix products, arithmetic and copies ran while one was open for 3% -> 1% of each run, Pallas kernels for 13% -> 21%
where the time goes in v3:
time: 259 us; the launch traced here: 258 us
  waiting for transfers between devices  150 us (58%)
  Pallas kernels  59.9 us (23%)
  starting transfers between devices  33.3 us (13%)
  local copies, waits for them, and re-layouts  7.97 us (3%)
  between operations  3.92 us (2%)
    ppermute x16, waiting for transfers between devices, swap(): return lax.ppermute(x, chain, [(i, i ^ k) for i in range(replicas)])  112 us
    all_to_all x2, waiting for transfers between devices, arrive(): return lax.all_to_all(picked, ('near', 'expert'), 0, 0, tiled=True)  37.7 us
    ppermute x16, starting transfers between devices, swap(): return lax.ppermute(x, chain, [(i, i ^ k) for i in range(replicas)])  21.4 us
    pallas_call x12, Pallas kernels, place(): pl.pallas_call(functools.partial(place_kernel, strips, coded), out_shape=...  19.5 us
    pallas_call x4, Pallas kernels, adam(): pl.pallas_call(functools.partial(adam_kernel, arrays, at, block, size, ah...  17.6 us
    pallas_call x5, Pallas kernels, summed(): pl.pallas_call(functools.partial(kernel, count), out_shape=out_shape, gri...  16.5 us
    all_to_all x2, starting transfers between devices, arrive(): return lax.all_to_all(picked, ('near', 'expert'), 0, 0, tiled=True)  11.9 us
    unnamed x30, local copies, waits for them, and re-layouts  7.88 us
  transfers between devices with their start and end apart: 18, of which 9 were waited for; matrix products, arithmetic and copies ran while one was open for 1% of the time, Pallas kernels for 21%

profile of v3, /device:TPU:0, one launch (start us, length us, event | category | flops | bytes accessed | tf_op | source)
XLA Modules:
  0.0 257.6 jit_solution(14160938521855732538)
XLA Ops:
  1.2 3.1 %pick_columns.3 = bf16[1024,1024]{1,0:T(8,128)(2,1)} custom-call(s32[2]{0:T(128)} %and_select_fusion.table_ref, bf16[512,4096]{1,0:T(8,128)(2,1)} %x_ref.3), custom_call_target="tpu_custom_call" | custom-call | flops 1024 | bytes 1024 | tf_op jit(solution)/shard_map/pick_columns/pallas_call | solution.py:63
  4.2 6.3 %all-to-all-start = ((bf16[16,64,1024]{2,1,0:T(8,128)(2,1)}), bf16[16,64,1024]{2,1,0:T(8,128)(2,1)S(1)}, u32[]{:S(2)}, u32[]{:S(2)}) async-start(bf16[16,64,1024]{2,1,0:T(8,128)(2,1)} %bitcast.33), calls=%async_computation | async-start | bytes 4194304 | tf_op jit(solution)/shard_map/all_to_all | solution.py:380
  12.0 2.0 collective-permute-start
  14.5 3.1 %pick_columns.2.refs_0_ = bf16[1024,1024]{1,0:T(8,128)(2,1)} custom-call(s32[2]{0:T(128)} %and_select_fusion.1.table_ref, bf16[512,4096]{1,0:T(8,128)(2,1)} %x_ref.3), custom_call_target="tpu_custom_call" | custom-call | flops 1024 | bytes 1024 | tf_op jit(solution)/shard_map/pick_columns/pallas_call | solution.py:63
  17.7 37.9 %collective-permute-done.refs_4_ = bf16[512,768]{1,0:T(8,128)(2,1)} collective-permute-done((bf16[512,768]{1,0:T(8,128)(2,1)S(1)}, bf16[512,768]{1,0:T(8,128)(2,1)}, u32[]{:S(2)}, u32[]{:S(2)}) %collective-permute-start) | collective-permute-done | bytes 786464 | tf_op jit(solution)/shard_map/ppermute | solution.py:370
  55.6 2.4 coded_sum.4.refs_1_
  58.7 5.6 %all-to-all-start.1 = ((bf16[16,64,1024]{2,1,0:T(8,128)(2,1)}), bf16[16,64,1024]{2,1,0:T(8,128)(2,1)}, u32[]{:S(2)}, u32[]{:S(2)}) async-start(bf16[16,64,1024]{2,1,0:T(8,128)(2,1)} %bitcast.32), calls=%async_computation.1 | async-start | bytes 4194304 | tf_op jit(solution)/shard_map/all_to_all | solution.py:380
  64.3 2.7 %collective-permute-start.4 = (s16[1,272,768]{2,1,0:T(8,128)(2,1)S(1)}, s16[1,272,768]{2,1,0:T(8,128)(2,1)}, u32[]{:S(2)}, u32[]{:S(2)}) collective-permute-start(s16[1,272,768]{2,1,0:T(8,128)(2,1)S(1)} %copy-done.7), channel_id=1, source_target_pairs={{0,2},{1,3},{2,0},{3,1},{4,6},{5,7},{6,4},{7,5},{8,10},{9,11},{10,... | collective-permute-start | bytes 1253384 | tf_op jit(solution)/shard_map/ppermute | solution.py:370
  66.9 3.1 %coded_sum.7 = s16[1,272,768]{2,1,0:T(8,128)(2,1)} custom-call(s32[2]{0:T(128)S(1)} %pad_add_fusion.refs_0_, bf16[1024,1024]{1,0:T(8,128)(2,1)S(1)} %bitcast.22, bf16[1024,1024]{1,0:T(8,128)(2,1)S(1)} %bitcast.23, bf16[512,768]{1,0:T(8,128)(2,1)S(1)} %broadcast_select_fusion.refs_3_, bf16[512,768]{1,0:T(8,128)(2,1)} %collective-permute-done.refs_4_), custom_call_target="tpu_custom_call" | custom-call | flops 1024 | bytes 1024 | tf_op jit(solution)/shard_map/coded_sum/pallas_call | solution.py:145
  70.4 3.1 %coded_sum.6 = s16[1,272,768]{2,1,0:T(8,128)(2,1)} custom-call(s32[2]{0:T(128)S(1)} %pad_add_fusion.refs_0_, bf16[1024,1024]{1,0:T(8,128)(2,1)S(1)} %bitcast.24, bf16[1024,1024]{1,0:T(8,128)(2,1)S(1)} %bitcast.25, bf16[512,768]{1,0:T(8,128)(2,1)S(1)} %broadcast_select_fusion.refs_3_, bf16[512,768]{1,0:T(8,128)(2,1)} %collective-permute-done.refs_4_), custom_call_target="tpu_custom_call" | custom-call | flops 1024 | bytes 1024 | tf_op jit(solution)/shard_map/coded_sum/pallas_call | solution.py:145
  73.5 2.6 %collective-permute-start.2 = (s16[1,272,768]{2,1,0:T(8,128)(2,1)}, s16[1,272,768]{2,1,0:T(8,128)(2,1)}, u32[]{:S(2)}, u32[]{:S(2)}) collective-permute-start(s16[1,272,768]{2,1,0:T(8,128)(2,1)} %coded_sum.6), channel_id=1, source_target_pairs={{0,2},{1,3},{2,0},{3,1},{4,6},{5,7},{6,4},{7,5},{8,10},{9,11},{10,... | collective-permute-start | bytes 1253384 | tf_op jit(solution)/shard_map/ppermute | solution.py:370
  76.1 3.1 %coded_sum.5 = s16[1,272,768]{2,1,0:T(8,128)(2,1)} custom-call(s32[2]{0:T(128)S(1)} %pad_add_fusion.refs_0_, bf16[1024,1024]{1,0:T(8,128)(2,1)S(1)} %bitcast.26, bf16[1024,1024]{1,0:T(8,128)(2,1)S(1)} %bitcast.27, bf16[512,768]{1,0:T(8,128)(2,1)S(1)} %broadcast_select_fusion.refs_3_, bf16[512,768]{1,0:T(8,128)(2,1)} %collective-permute-done.refs_4_), custom_call_target="tpu_custom_call" | custom-call | flops 1024 | bytes 1024 | tf_op jit(solution)/shard_map/coded_sum/pallas_call | solution.py:145
  79.6 37.7 %all-to-all-done.1 = bf16[16,64,1024]{2,1,0:T(8,128)(2,1)} async-done(((bf16[16,64,1024]{2,1,0:T(8,128)(2,1)}), bf16[16,64,1024]{2,1,0:T(8,128)(2,1)}, u32[]{:S(2)}, u32[]{:S(2)}) %all-to-all-start.1) | async-done | bytes 2097184 | tf_op jit(solution)/shard_map/all_to_all | solution.py:380
  117.2 4.8 %own_sum.1.refs_0_ = f32[1024,768]{1,0:T(8,128)S(1)} custom-call(s32[2]{0:T(128)S(1)} %pad_add_fusion.refs_0_, bf16[1024,1024]{1,0:T(8,128)(2,1)} %bitcast.5.refs_1_.refs_2_, bf16[1024,1024]{1,0:T(8,128)(2,1)} %bitcast.5.refs_1_.refs_2_, bf16[512,768]{1,0:T(8,128)(2,1)S(1)} %broadcast_select_fusion.refs_3_, bf16[512,768]{1,0:T(8,128)(2,1)} %collective-permute-done.refs_4_), custom_call_target="tpu_custom_call" | custom-call | flops 1024 | bytes 1024 | tf_op jit(solution)/shard_map/own_sum/pallas_call | solution.py:145
  123.7 4.0 %adam.4 = (f32[1024,768]{1,0:T(8,128)}, bf16[1024,768]{1,0:T(8,128)(2,1)}, bf16[1024,768]{1,0:T(8,128)(2,1)}, f32[1]{0:T(128)}, s16[1,272,768]{2,1,0:T(8,128)(2,1)}) custom-call(f32[1024,768]{1,0:T(8,128)} %copy-done, s16[1,272,768]{2,1,0:T(8,128)(2,1)} %collective-permute-done.4.refs_1_, f32[1024,768]{1,0:T(8,128)} %refs_2_.7, bf16[1024,768]{1,0:T(8,128)(2,1)} %refs_3_.7, ...), custom_call_target="tpu_custom_call" | custom-call | flops 1024 | bytes 1024 | tf_op jit(solution)/shard_map/adam/pallas_call | solution.py:251
  127.8 4.7 %adam.5 = (f32[1024,768]{1,0:T(8,128)}, bf16[1024,768]{1,0:T(8,128)(2,1)}, bf16[1024,768]{1,0:T(8,128)(2,1)}, f32[1]{0:T(128)}, s16[1,272,768]{2,1,0:T(8,128)(2,1)}) custom-call(f32[1024,768]{1,0:T(8,128)} %copy-done, s16[1,272,768]{2,1,0:T(8,128)(2,1)} %collective-permute-done.3.refs_1_, ...), custom_call_target="tpu_custom_call", output_to_operand_aliasing={{0}: (5, {}), {1}: (6, {}), {2}: (7, {})} | custom-call | flops 1024 | bytes 1024 | tf_op jit(solution)/shard_map/adam/pallas_call | solution.py:251
  132.6 2.0 collective-permute-start.7
  134.6 4.5 %adam.6 = (f32[1024,768]{1,0:T(8,128)}, bf16[1024,768]{1,0:T(8,128)(2,1)}, bf16[1024,768]{1,0:T(8,128)(2,1)}, f32[1]{0:T(128)}) custom-call(f32[1024,768]{1,0:T(8,128)} %copy-done, s16[1,272,768]{2,1,0:T(8,128)(2,1)} %collective-permute-done.2.refs_1_, f32[1024,768]{1,0:T(8,128)} %refs_2_.7, ...), custom_call_target="tpu_custom_call", output_to_operand_aliasing={{0}: (5, {}), {1}: (6, {}), {2}: (7, {})} | custom-call | flops 1024 | bytes 1024 | tf_op jit(solution)/shard_map/adam/pallas_call | solution.py:251
  140.7 4.4 %adam.7 = (f32[1024,768]{1,0:T(8,128)}, bf16[1024,768]{1,0:T(8,128)(2,1)}, bf16[1024,768]{1,0:T(8,128)(2,1)}, f32[1]{0:T(128)}) custom-call(f32[1024,768]{1,0:T(8,128)} %copy-done, s16[1,272,768]{2,1,0:T(8,128)(2,1)} %copy-done.13, f32[1024,768]{1,0:T(8,128)} %refs_2_.7, ...), custom_call_target="tpu_custom_call", output_to_operand_aliasing={{0}: (5, {}), {1}: (6, {}), {2}: (7, {})} | custom-call | flops 1024 | bytes 1024 | tf_op jit(solution)/shard_map/adam/pallas_call | solution.py:251
  145.2 5.5 %collective-permute-done.5 = f32[1]{0:T(128)} collective-permute-done((f32[1]{0:T(128)}, f32[1]{0:T(128)}, u32[]{:S(2)}, u32[]{:S(2)}) %collective-permute-start.5) | collective-permute-done | bytes 36 | tf_op jit(solution)/shard_map/ppermute | solution.py:370
  151.9 2.5 collective-permute-start.6
  154.4 3.5 %collective-permute-done.6 = f32[1]{0:T(128)} collective-permute-done((f32[1]{0:T(128)}, f32[1]{0:T(128)}, u32[]{:S(2)}, u32[]{:S(2)}) %collective-permute-start.6) | collective-permute-done | bytes 36 | tf_op jit(solution)/shard_map/ppermute | solution.py:370
  158.6 1.9 copy-done.1
  162.3 2.6 %collective-permute-start.15 = (bf16[512,768]{1,0:T(8,128)(2,1)S(1)}, bf16[512,768]{1,0:T(8,128)(2,1)S(1)}, u32[]{:S(2)}, u32[]{:S(2)}) collective-permute-start(bf16[512,768]{1,0:T(8,128)(2,1)S(1)} %scale.1.refs_0_), channel_id=1, source_target_pairs={{0,1},{1,0},{2,3},{3,2},{4,5},{5,4},{6,7},{7,6},{8,9},{9,8},{10,11... | collective-permute-start | bytes 2359304 | tf_op jit(solution)/shard_map/ppermute | solution.py:370
  164.9 32.9 %collective-permute-done.9.refs_1_.piece = bf16[512,768]{1,0:T(8,128)(2,1)S(1)} collective-permute-done((bf16[512,768]{1,0:T(8,128)(2,1)S(1)}, bf16[512,768]{1,0:T(8,128)(2,1)S(1)}, u32[]{:S(2)}, u32[]{:S(2)}) %collective-permute-start.9) | collective-permute-done | bytes 786464 | tf_op jit(solution)/shard_map/ppermute | solution.py:370
  198.8 3.0 %collective-permute-start.10 = (s16[272,768]{1,0:T(8,128)(2,1)}, s16[272,768]{1,0:T(8,128)(2,1)}, u32[]{:S(2)}, u32[]{:S(2)}) collective-permute-start(s16[272,768]{1,0:T(8,128)(2,1)} %gate.5.piece), channel_id=1, source_target_pairs={{0,2},{1,3},{2,0},{3,1},{4,6},{5,7},{6,4},{7,5},{8,10},{9,11},{10,... | collective-permute-start | bytes 1253384 | tf_op jit(solution)/shard_map/ppermute | solution.py:370
  202.2 27.3 %collective-permute-done.12.refs_1_.piece = s16[272,768]{1,0:T(8,128)(2,1)S(1)} collective-permute-done((s16[272,768]{1,0:T(8,128)(2,1)}, s16[272,768]{1,0:T(8,128)(2,1)S(1)}, u32[]{:S(2)}, u32[]{:S(2)}) %collective-permute-start.12) | collective-permute-done | bytes 417824 | tf_op jit(solution)/shard_map/ppermute | solution.py:370
  231.4 1.9 place.12.refs_0_
  238.4 1.9 place.15.refs_0_
  243.5 2.0 place.18.refs_0_
  248.4 2.0 place.21.refs_0_
  251.8 3.2 %collective-permute-done.11.piece = s16[272,768]{1,0:T(8,128)(2,1)S(1)} collective-permute-done((s16[272,768]{1,0:T(8,128)(2,1)}, s16[272,768]{1,0:T(8,128)(2,1)S(1)}, u32[]{:S(2)}, u32[]{:S(2)}) %collective-permute-start.11) | collective-permute-done | bytes 417824 | tf_op jit(solution)/shard_map/ppermute | solution.py:370
  (68 shorter events, 26.4 us)
Async XLA Ops:
  4.2 6.3 %copy-start.14 = (s32[8]{0:T(128)S(1)}, s32[8]{0:T(128)}, u32[]{:S(2)}) copy-start(s32[8]{0:T(128)} %param.8) | copy-start | bytes 100
  4.2 51.4 %all-to-all-start = ((bf16[16,64,1024]{2,1,0:T(8,128)(2,1)}), bf16[16,64,1024]{2,1,0:T(8,128)(2,1)S(1)}, u32[]{:S(2)}, u32[]{:S(2)}) async-start(bf16[16,64,1024]{2,1,0:T(8,128)(2,1)} %bitcast.33), calls=%async_computation | async-start | bytes 4194304 | tf_op jit(solution)/shard_map/all_to_all | solution.py:380
  12.0 43.6 %collective-permute-start = (bf16[512,768]{1,0:T(8,128)(2,1)S(1)}, bf16[512,768]{1,0:T(8,128)(2,1)}, u32[]{:S(2)}, u32[]{:S(2)}) collective-permute-start(bf16[512,768]{1,0:T(8,128)(2,1)S(1)} %broadcast_select_fusion.refs_3_), channel_id=1, source_target_pairs={{0,1},{1,0},{2,3},{3,2},{4,5},{5,4},{6,7},{7,6},{8,9},{9,8},{10,11... | collective-permute-start | bytes 2359304 | tf_op jit(solution)/shard_map/ppermute | solution.py:370
  58.7 5.6 %copy-start.7 = (s16[1,272,768]{2,1,0:T(8,128)(2,1)S(1)}, s16[1,272,768]{2,1,0:T(8,128)(2,1)}, u32[]{:S(2)}) copy-start(s16[1,272,768]{2,1,0:T(8,128)(2,1)} %copy-done.6) | copy-start | bytes 1253380
  58.7 58.5 %all-to-all-start.1 = ((bf16[16,64,1024]{2,1,0:T(8,128)(2,1)}), bf16[16,64,1024]{2,1,0:T(8,128)(2,1)}, u32[]{:S(2)}, u32[]{:S(2)}) async-start(bf16[16,64,1024]{2,1,0:T(8,128)(2,1)} %bitcast.32), calls=%async_computation.1 | async-start | bytes 4194304 | tf_op jit(solution)/shard_map/all_to_all | solution.py:380
  64.3 59.4 %collective-permute-start.4 = (s16[1,272,768]{2,1,0:T(8,128)(2,1)S(1)}, s16[1,272,768]{2,1,0:T(8,128)(2,1)}, u32[]{:S(2)}, u32[]{:S(2)}) collective-permute-start(s16[1,272,768]{2,1,0:T(8,128)(2,1)S(1)} %copy-done.7), channel_id=1, source_target_pairs={{0,2},{1,3},{2,0},{3,1},{4,6},{5,7},{6,4},{7,5},{8,10},{9,11},{10,... | collective-permute-start | bytes 1253384 | tf_op jit(solution)/shard_map/ppermute | solution.py:370
  70.1 57.7 %collective-permute-start.3 = (s16[1,272,768]{2,1,0:T(8,128)(2,1)}, s16[1,272,768]{2,1,0:T(8,128)(2,1)}, u32[]{:S(2)}, u32[]{:S(2)}) collective-permute-start(s16[1,272,768]{2,1,0:T(8,128)(2,1)} %coded_sum.7), channel_id=1, source_target_pairs={{0,2},{1,3},{2,0},{3,1},{4,6},{5,7},{6,4},{7,5},{8,10},{9,11},{10,... | collective-permute-start | bytes 1253384 | tf_op jit(solution)/shard_map/ppermute | solution.py:370
  73.5 61.1 %collective-permute-start.2 = (s16[1,272,768]{2,1,0:T(8,128)(2,1)}, s16[1,272,768]{2,1,0:T(8,128)(2,1)}, u32[]{:S(2)}, u32[]{:S(2)}) collective-permute-start(s16[1,272,768]{2,1,0:T(8,128)(2,1)} %coded_sum.6), channel_id=1, source_target_pairs={{0,2},{1,3},{2,0},{3,1},{4,6},{5,7},{6,4},{7,5},{8,10},{9,11},{10,... | collective-permute-start | bytes 1253384 | tf_op jit(solution)/shard_map/ppermute | solution.py:370
  79.2 60.7 %collective-permute-start.1 = (s16[1,272,768]{2,1,0:T(8,128)(2,1)}, s16[1,272,768]{2,1,0:T(8,128)(2,1)S(1)}, u32[]{:S(2)}, u32[]{:S(2)}) collective-permute-start(s16[1,272,768]{2,1,0:T(8,128)(2,1)} %coded_sum.5), channel_id=1, source_target_pairs={{0,2},{1,3},{2,0},{3,1},{4,6},{5,7},{6,4},{7,5},{8,10},{9,11},{10,... | collective-permute-start | bytes 1253384 | tf_op jit(solution)/shard_map/ppermute | solution.py:370
  122.0 1.7 copy-start
  127.7 4.8 %copy-start.9 = (s16[1,272,768]{2,1,0:T(8,128)(2,1)S(1)}, s16[1,272,768]{2,1,0:T(8,128)(2,1)}, u32[]{:S(2)}) copy-start(s16[1,272,768]{2,1,0:T(8,128)(2,1)} %get-tuple-element.40) | copy-start | bytes 1253380
  132.5 26.1 %collective-permute-start.8 = (s16[272,768]{1,0:T(8,128)(2,1)}, s16[272,768]{1,0:T(8,128)(2,1)S(1)}, u32[]{:S(2)}, u32[]{:S(2)}) collective-permute-start(s16[272,768]{1,0:T(8,128)(2,1)} %bitcast.28), channel_id=1, source_target_pairs={{0,1},{1,0},{2,3},{3,2},{4,5},{5,4},{6,7},{7,6},{8,9},{9,8},{10,11... | collective-permute-start | bytes 1253384 | tf_op jit(solution)/shard_map/ppermute | solution.py:370
  132.6 26.0 %collective-permute-start.7 = (s16[272,768]{1,0:T(8,128)(2,1)S(1)}, s16[272,768]{1,0:T(8,128)(2,1)S(1)}, u32[]{:S(2)}, u32[]{:S(2)}) collective-permute-start(s16[272,768]{1,0:T(8,128)(2,1)S(1)} %bitcast.31), channel_id=1, source_target_pairs={{0,1},{1,0},{2,3},{3,2},{4,5},{5,4},{6,7},{7,6},{8,9},{9,8},{10,11... | collective-permute-start | bytes 1253384 | tf_op jit(solution)/shard_map/ppermute | solution.py:370
  140.0 0.8 copy-start.13
  145.2 5.6 %collective-permute-start.5 = (f32[1]{0:T(128)}, f32[1]{0:T(128)}, u32[]{:S(2)}, u32[]{:S(2)}) collective-permute-start(f32[1]{0:T(128)} %get-tuple-element.38), channel_id=1, source_target_pairs={{0,2},{1,3},{2,0},{3,1},{4,6},{5,7},{6,4},{7,5},{8,10},{9,11},{10,... | collective-permute-start | bytes 20 | tf_op jit(solution)/shard_map/ppermute | solution.py:370
  151.9 6.1 %collective-permute-start.6 = (f32[1]{0:T(128)}, f32[1]{0:T(128)}, u32[]{:S(2)}, u32[]{:S(2)}) collective-permute-start(f32[1]{0:T(128)} %max.6), channel_id=1, source_target_pairs={{0,1},{1,0},{2,3},{3,2},{4,5},{5,4},{6,7},{7,6},{8,9},{9,8},{10,11... | collective-permute-start | bytes 20 | tf_op jit(solution)/shard_map/ppermute | solution.py:370
  158.6 1.9 copy-start.1
  160.6 68.9 %copy-start.4 = (bf16[512,768]{1,0:T(8,128)(2,1)}, bf16[512,768]{1,0:T(8,128)(2,1)S(1)}, u32[]{:S(2)}) copy-start(bf16[512,768]{1,0:T(8,128)(2,1)S(1)} %scale.1.refs_0_) | copy-start | bytes 2359300
  160.6 37.2 %collective-permute-start.9 = (bf16[512,768]{1,0:T(8,128)(2,1)S(1)}, bf16[512,768]{1,0:T(8,128)(2,1)S(1)}, u32[]{:S(2)}, u32[]{:S(2)}) collective-permute-start(bf16[512,768]{1,0:T(8,128)(2,1)S(1)} %scale.1.refs_0_), channel_id=1, source_target_pairs={{0,2},{1,3},{2,0},{3,1},{4,6},{5,7},{6,4},{7,5},{8,10},{9,11},{10,... | collective-permute-start | bytes 2359304 | tf_op jit(solution)/shard_map/ppermute | solution.py:370
  162.3 39.9 %collective-permute-start.15 = (bf16[512,768]{1,0:T(8,128)(2,1)S(1)}, bf16[512,768]{1,0:T(8,128)(2,1)S(1)}, u32[]{:S(2)}, u32[]{:S(2)}) collective-permute-start(bf16[512,768]{1,0:T(8,128)(2,1)S(1)} %scale.1.refs_0_), channel_id=1, source_target_pairs={{0,1},{1,0},{2,3},{3,2},{4,5},{5,4},{6,7},{7,6},{8,9},{9,8},{10,11... | collective-permute-start | bytes 2359304 | tf_op jit(solution)/shard_map/ppermute | solution.py:370
  197.8 0.9 copy-start.2
  198.7 30.8 %collective-permute-start.12 = (s16[272,768]{1,0:T(8,128)(2,1)}, s16[272,768]{1,0:T(8,128)(2,1)S(1)}, u32[]{:S(2)}, u32[]{:S(2)}) collective-permute-start(s16[272,768]{1,0:T(8,128)(2,1)} %gate.6.piece), channel_id=1, source_target_pairs={{0,2},{1,3},{2,0},{3,1},{4,6},{5,7},{6,4},{7,5},{8,10},{9,11},{10,... | collective-permute-start | bytes 1253384 | tf_op jit(solution)/shard_map/ppermute | solution.py:370
  198.8 38.6 %collective-permute-start.10 = (s16[272,768]{1,0:T(8,128)(2,1)}, s16[272,768]{1,0:T(8,128)(2,1)}, u32[]{:S(2)}, u32[]{:S(2)}) collective-permute-start(s16[272,768]{1,0:T(8,128)(2,1)} %gate.5.piece), channel_id=1, source_target_pairs={{0,2},{1,3},{2,0},{3,1},{4,6},{5,7},{6,4},{7,5},{8,10},{9,11},{10,... | collective-permute-start | bytes 1253384 | tf_op jit(solution)/shard_map/ppermute | solution.py:370
  201.7 46.6 %collective-permute-start.14 = (bf16[512,768]{1,0:T(8,128)(2,1)}, bf16[512,768]{1,0:T(8,128)(2,1)}, u32[]{:S(2)}, u32[]{:S(2)}) collective-permute-start(bf16[512,768]{1,0:T(8,128)(2,1)} %copy-done.2), channel_id=1, source_target_pairs={{0,1},{1,0},{2,3},{3,2},{4,5},{5,4},{6,7},{7,6},{8,9},{9,8},{10,11... | collective-permute-start | bytes 2359304 | tf_op jit(solution)/shard_map/ppermute | solution.py:370
  229.5 0.8 copy-start.11
  230.2 1.1 copy-start.5
  231.4 1.9 copy-start.10
  233.3 1.4 copy-start.12
  233.3 1.5 copy-start.8
  234.8 15.6 %collective-permute-start.13 = (s16[272,768]{1,0:T(8,128)(2,1)S(1)}, s16[272,768]{1,0:T(8,128)(2,1)S(1)}, u32[]{:S(2)}, u32[]{:S(2)}) collective-permute-start(s16[272,768]{1,0:T(8,128)(2,1)S(1)} %copy-done.12), channel_id=1, source_target_pairs={{0,1},{1,0},{2,3},{3,2},{4,5},{5,4},{6,7},{7,6},{8,9},{9,8},{10,11... | collective-permute-start | bytes 1253384 | tf_op jit(solution)/shard_map/ppermute | solution.py:370
  234.9 3.5 %copy-start.3 = (bf16[512,768]{1,0:T(8,128)(2,1)S(1)}, bf16[512,768]{1,0:T(8,128)(2,1)}, u32[]{:S(2)}) copy-start(bf16[512,768]{1,0:T(8,128)(2,1)} %copy-done.2) | copy-start | bytes 2359300
  237.3 17.7 %collective-permute-start.11 = (s16[272,768]{1,0:T(8,128)(2,1)}, s16[272,768]{1,0:T(8,128)(2,1)S(1)}, u32[]{:S(2)}, u32[]{:S(2)}) collective-permute-start(s16[272,768]{1,0:T(8,128)(2,1)} %collective-permute-done.10.piece), channel_id=1, source_target_pairs={{0,1},{1,0},{2,3},{3,2},{4,5},{5,4},{6,7},{7,6},{8,9},{9,8},{10,11... | collective-permute-start | bytes 1253384 | tf_op jit(solution)/shard_map/ppermute | solution.py:370
  (1 other events, 0.8 us)

commit v4 on v3

--- a/solution.py
+++ b/solution.py
@@ -17,7 +17,7 @@
 
 MIB = 1024 * 1024
 LEVELS = 32000.0
-PLACE_HINT = 1 << 32
+PLACE_HINT = 1 << 30
 TAIL = 16
 
 
@@ -80,8 +80,8 @@
     pass
 
 
-def gate(x, after):
-    if not after:
+def gate(x, after, work=1024):
+    if not after and work == 1024:
         return x
     anywhere = pl.BlockSpec(memory_space=pl.ANY)
     return pl.pallas_call(
@@ -90,7 +90,7 @@
         in_specs=[anywhere] * (1 + len(after)),
         out_specs=anywhere,
         input_output_aliases={0: 0},
-        cost_estimate=hint(1024),
+        cost_estimate=hint(work),
         name="gate",
     )(x, *after)
 
@@ -371,7 +371,7 @@
 
     live = (jnp.arange(capacity)[None, :] < recv_counts[:, None]).reshape(-1)
     hidden = jnp.where(live[:, None], hidden_saved, jnp.zeros((), jnp.bfloat16))
-    hiddens = [hidden] + [swap(hidden, k) for k in range(1, half)]
+    hiddens = [hidden] + [gate(swap(hidden, k), (), 1 << 35) for k in range(1, half)]
     order = jnp.stack([near ^ k for k in range(half)]).astype(jnp.int32)
 
     def arrive(side, at, width, after):
@@ -384,6 +384,7 @@
         coded_sum(got, order, hiddens, at, block, block) for at in range(0, shard, block)
     ]
     coded = [swap(partial, half) for partial in partials]
+    coded[0] = gate(coded[0], (), 1 << 35)
 
     got = arrive(far, 0, shard, (partials[0],))
     own = own_sum(got, order, hiddens, block)

time: 259 us -> 253 us (0.977)
  starting transfers between devices: 33.3 us -> 26 us
    ppermute x16, starting transfers between devices: 21.4 us -> 17.6 us  [swap(): return lax.ppermute(x, chain, [(i, i ^ k) for i in range(replicas)])]
    all_to_all x2, starting transfers between devices: 11.9 us -> 8.4 us  [arrive(): return lax.all_to_all(picked, ('near', 'expert'), 0, 0, tiled=True)]
    ppermute x16, waiting for transfers between devices: 112 us -> 110 us  [swap(): return lax.ppermute(x, chain, [(i, i ^ k) for i in range(replicas)])]
    unnamed x30 -> x32, local copies, waits for them, and re-layouts: 7.88 us -> 9.34 us
  transfers between devices with their start and end apart: 18 -> 18, of which waited for: 9 -> 12; matrix products, arithmetic and copies ran while one was open for 1% -> 0% of each run, Pallas kernels for 21% -> 22%
where the time goes in v4:
time: 253 us; the launch traced here: 252 us
  waiting for transfers between devices  149 us (59%)
  Pallas kernels  60.2 us (24%)
  starting transfers between devices  26 us (10%)
  local copies, waits for them, and re-layouts  9.42 us (4%)
  between operations  4.11 us (2%)
  other arithmetic  3.11 us (1%)
    ppermute x16, waiting for transfers between devices, swap(): return lax.ppermute(x, chain, [(i, i ^ k) for i in range(replicas)])  110 us
    all_to_all x2, waiting for transfers between devices, arrive(): return lax.all_to_all(picked, ('near', 'expert'), 0, 0, tiled=True)  39.8 us
    pallas_call x12, Pallas kernels, place(): pl.pallas_call(functools.partial(place_kernel, strips, coded), out_shape=...  19.9 us
    ppermute x16, starting transfers between devices, swap(): return lax.ppermute(x, chain, [(i, i ^ k) for i in range(replicas)])  17.6 us
    pallas_call x4, Pallas kernels, adam(): pl.pallas_call(functools.partial(adam_kernel, arrays, at, block, size, ah...  17.5 us
    pallas_call x5, Pallas kernels, summed(): pl.pallas_call(functools.partial(kernel, count), out_shape=out_shape, gri...  16.5 us
    unnamed x32, local copies, waits for them, and re-layouts  9.34 us
    all_to_all x2, starting transfers between devices, arrive(): return lax.all_to_all(picked, ('near', 'expert'), 0, 0, tiled=True)  8.4 us
  transfers between devices with their start and end apart: 18, of which 12 were waited for; matrix products, arithmetic and copies ran while one was open for 0% of the time, Pallas kernels for 22%

profile of v4, /device:TPU:0, one launch (start us, length us, event | category | flops | bytes accessed | tf_op | source)
XLA Modules:
  0.0 252.3 jit_solution(6248639871079769335)
XLA Ops:
  2.7 3.1 %collective-permute-start = (bf16[512,768]{1,0:T(8,128)(2,1)S(1)}, bf16[512,768]{1,0:T(8,128)(2,1)}, u32[]{:S(2)}, u32[]{:S(2)}) collective-permute-start(bf16[512,768]{1,0:T(8,128)(2,1)S(1)} %broadcast_select_fusion.refs_3_), channel_id=1, source_target_pairs={{0,1},{1,0},{2,3},{3,2},{4,5},{5,4},{6,7},{7,6},{8,9},{9,8},{10,11... | collective-permute-start | bytes 2359304 | tf_op jit(solution)/shard_map/ppermute | solution.py:370
  6.3 3.1 %pick_columns.3 = bf16[1024,1024]{1,0:T(8,128)(2,1)} custom-call(s32[2]{0:T(128)} %and_select_fusion.table_ref, bf16[512,4096]{1,0:T(8,128)(2,1)} %x_ref.3), custom_call_target="tpu_custom_call" | custom-call | flops 1024 | bytes 1024 | tf_op jit(solution)/shard_map/pick_columns/pallas_call | solution.py:63
  9.4 3.8 %all-to-all-start = ((bf16[16,64,1024]{2,1,0:T(8,128)(2,1)}), bf16[16,64,1024]{2,1,0:T(8,128)(2,1)S(1)}, u32[]{:S(2)}, u32[]{:S(2)}) async-start(bf16[16,64,1024]{2,1,0:T(8,128)(2,1)} %bitcast.33), calls=%async_computation | async-start | bytes 4194304 | tf_op jit(solution)/shard_map/all_to_all | solution.py:380
  13.8 3.1 %pick_columns.2.refs_0_ = bf16[1024,1024]{1,0:T(8,128)(2,1)} custom-call(s32[2]{0:T(128)} %and_select_fusion.1.table_ref, bf16[512,4096]{1,0:T(8,128)(2,1)} %x_ref.3), custom_call_target="tpu_custom_call" | custom-call | flops 1024 | bytes 1024 | tf_op jit(solution)/shard_map/pick_columns/pallas_call | solution.py:63
  16.9 7.4 %collective-permute-done.refs_0_ = bf16[512,768]{1,0:T(8,128)(2,1)} collective-permute-done((bf16[512,768]{1,0:T(8,128)(2,1)S(1)}, bf16[512,768]{1,0:T(8,128)(2,1)}, u32[]{:S(2)}, u32[]{:S(2)}) %collective-permute-start) | collective-permute-done | bytes 786464 | tf_op jit(solution)/shard_map/ppermute | solution.py:370
  24.3 23.7 %all-to-all-done = bf16[16,64,1024]{2,1,0:T(8,128)(2,1)S(1)} async-done(((bf16[16,64,1024]{2,1,0:T(8,128)(2,1)}), bf16[16,64,1024]{2,1,0:T(8,128)(2,1)S(1)}, u32[]{:S(2)}, u32[]{:S(2)}) %all-to-all-start) | async-done | bytes 2097184 | tf_op jit(solution)/shard_map/all_to_all | solution.py:380
  47.9 2.4 coded_sum.4.refs_1_
  51.1 4.6 %all-to-all-start.1 = ((bf16[16,64,1024]{2,1,0:T(8,128)(2,1)}), bf16[16,64,1024]{2,1,0:T(8,128)(2,1)}, u32[]{:S(2)}, u32[]{:S(2)}) async-start(bf16[16,64,1024]{2,1,0:T(8,128)(2,1)} %bitcast.32), calls=%async_computation.1 | async-start | bytes 4194304 | tf_op jit(solution)/shard_map/all_to_all | solution.py:380
  55.6 2.7 %collective-permute-start.4 = (s16[1,272,768]{2,1,0:T(8,128)(2,1)S(1)}, s16[1,272,768]{2,1,0:T(8,128)(2,1)}, u32[]{:S(2)}, u32[]{:S(2)}) collective-permute-start(s16[1,272,768]{2,1,0:T(8,128)(2,1)S(1)} %copy-done.7), channel_id=1, source_target_pairs={{0,2},{1,3},{2,0},{3,1},{4,6},{5,7},{6,4},{7,5},{8,10},{9,11},{10,... | collective-permute-start | bytes 1253384 | tf_op jit(solution)/shard_map/ppermute | solution.py:370
  58.3 3.1 %coded_sum.7 = s16[1,272,768]{2,1,0:T(8,128)(2,1)} custom-call(s32[2]{0:T(128)S(1)} %pad_add_fusion.refs_0_, bf16[1024,1024]{1,0:T(8,128)(2,1)S(1)} %bitcast.22, bf16[1024,1024]{1,0:T(8,128)(2,1)S(1)} %bitcast.23, bf16[512,768]{1,0:T(8,128)(2,1)S(1)} %broadcast_select_fusion.refs_3_, bf16[512,768]{1,0:T(8,128)(2,1)} %gate.6.refs_4_), custom_call_target="tpu_custom_call" | custom-call | flops 1024 | bytes 1024 | tf_op jit(solution)/shard_map/coded_sum/pallas_call | solution.py:145
  61.4 3.1 %coded_sum.6 = s16[1,272,768]{2,1,0:T(8,128)(2,1)} custom-call(s32[2]{0:T(128)S(1)} %pad_add_fusion.refs_0_, bf16[1024,1024]{1,0:T(8,128)(2,1)S(1)} %bitcast.24, bf16[1024,1024]{1,0:T(8,128)(2,1)S(1)} %bitcast.25, bf16[512,768]{1,0:T(8,128)(2,1)S(1)} %broadcast_select_fusion.refs_3_, bf16[512,768]{1,0:T(8,128)(2,1)} %gate.6.refs_4_), custom_call_target="tpu_custom_call" | custom-call | flops 1024 | bytes 1024 | tf_op jit(solution)/shard_map/coded_sum/pallas_call | solution.py:145
  64.6 3.1 %coded_sum.5 = s16[1,272,768]{2,1,0:T(8,128)(2,1)} custom-call(s32[2]{0:T(128)S(1)} %pad_add_fusion.refs_0_, bf16[1024,1024]{1,0:T(8,128)(2,1)S(1)} %bitcast.26, bf16[1024,1024]{1,0:T(8,128)(2,1)S(1)} %bitcast.27, bf16[512,768]{1,0:T(8,128)(2,1)S(1)} %broadcast_select_fusion.refs_3_, bf16[512,768]{1,0:T(8,128)(2,1)} %gate.6.refs_4_), custom_call_target="tpu_custom_call" | custom-call | flops 1024 | bytes 1024 | tf_op jit(solution)/shard_map/coded_sum/pallas_call | solution.py:145
  68.0 2.6 %collective-permute-start.2 = (s16[1,272,768]{2,1,0:T(8,128)(2,1)}, s16[1,272,768]{2,1,0:T(8,128)(2,1)S(1)}, u32[]{:S(2)}, u32[]{:S(2)}) collective-permute-start(s16[1,272,768]{2,1,0:T(8,128)(2,1)} %coded_sum.6), channel_id=1, source_target_pairs={{0,2},{1,3},{2,0},{3,1},{4,6},{5,7},{6,4},{7,5},{8,10},{9,11},{10,... | collective-permute-start | bytes 1253384 | tf_op jit(solution)/shard_map/ppermute | solution.py:370
  70.9 18.6 %collective-permute-done.4.refs_0_ = s16[1,272,768]{2,1,0:T(8,128)(2,1)} collective-permute-done((s16[1,272,768]{2,1,0:T(8,128)(2,1)S(1)}, s16[1,272,768]{2,1,0:T(8,128)(2,1)}, u32[]{:S(2)}, u32[]{:S(2)}) %collective-permute-start.4) | collective-permute-done | bytes 417824 | tf_op jit(solution)/shard_map/ppermute | solution.py:370
  89.5 16.1 %all-to-all-done.1 = bf16[16,64,1024]{2,1,0:T(8,128)(2,1)} async-done(((bf16[16,64,1024]{2,1,0:T(8,128)(2,1)}), bf16[16,64,1024]{2,1,0:T(8,128)(2,1)}, u32[]{:S(2)}, u32[]{:S(2)}) %all-to-all-start.1) | async-done | bytes 2097184 | tf_op jit(solution)/shard_map/all_to_all | solution.py:380
  105.6 4.8 %own_sum.1.refs_0_ = f32[1024,768]{1,0:T(8,128)S(1)} custom-call(s32[2]{0:T(128)S(1)} %pad_add_fusion.refs_0_, bf16[1024,1024]{1,0:T(8,128)(2,1)} %bitcast.5.refs_1_.refs_2_, bf16[1024,1024]{1,0:T(8,128)(2,1)} %bitcast.5.refs_1_.refs_2_, bf16[512,768]{1,0:T(8,128)(2,1)S(1)} %broadcast_select_fusion.refs_3_, bf16[512,768]{1,0:T(8,128)(2,1)} %gate.6.refs_4_), custom_call_target="tpu_custom_call" | custom-call | flops 1024 | bytes 1024 | tf_op jit(solution)/shard_map/own_sum/pallas_call | solution.py:145
  112.1 4.0 %adam.4 = (f32[1024,768]{1,0:T(8,128)}, bf16[1024,768]{1,0:T(8,128)(2,1)}, bf16[1024,768]{1,0:T(8,128)(2,1)}, f32[1]{0:T(128)}, s16[1,272,768]{2,1,0:T(8,128)(2,1)}) custom-call(f32[1024,768]{1,0:T(8,128)} %copy-done, s16[1,272,768]{2,1,0:T(8,128)(2,1)} %gate.8.refs_1_, f32[1024,768]{1,0:T(8,128)} %refs_2_.7, bf16[1024,768]{1,0:T(8,128)(2,1)} %refs_3_.7, ...), custom_call_target="tpu_custom_call" | custom-call | flops 1024 | bytes 1024 | tf_op jit(solution)/shard_map/adam/pallas_call | solution.py:251
  116.9 4.7 %adam.5 = (f32[1024,768]{1,0:T(8,128)}, bf16[1024,768]{1,0:T(8,128)(2,1)}, bf16[1024,768]{1,0:T(8,128)(2,1)}, f32[1]{0:T(128)}, s16[1,272,768]{2,1,0:T(8,128)(2,1)}) custom-call(f32[1024,768]{1,0:T(8,128)} %copy-done, s16[1,272,768]{2,1,0:T(8,128)(2,1)} %copy-done.15, ...), custom_call_target="tpu_custom_call", output_to_operand_aliasing={{0}: (5, {}), {1}: (6, {}), {2}: (7, {})} | custom-call | flops 1024 | bytes 1024 | tf_op jit(solution)/shard_map/adam/pallas_call | solution.py:251
  121.7 2.0 collective-permute-start.7
  123.7 2.5 collective-permute-done.2.refs_1_
  126.9 4.4 %adam.6 = (f32[1024,768]{1,0:T(8,128)}, bf16[1024,768]{1,0:T(8,128)(2,1)}, bf16[1024,768]{1,0:T(8,128)(2,1)}, f32[1]{0:T(128)}) custom-call(f32[1024,768]{1,0:T(8,128)} %copy-done, s16[1,272,768]{2,1,0:T(8,128)(2,1)} %copy-done.14, f32[1024,768]{1,0:T(8,128)} %refs_2_.7, ...), custom_call_target="tpu_custom_call", output_to_operand_aliasing={{0}: (5, {}), {1}: (6, {}), {2}: (7, {})} | custom-call | flops 1024 | bytes 1024 | tf_op jit(solution)/shard_map/adam/pallas_call | solution.py:251
  131.3 2.8 %collective-permute-done.1.refs_1_ = s16[1,272,768]{2,1,0:T(8,128)(2,1)S(1)} collective-permute-done((s16[1,272,768]{2,1,0:T(8,128)(2,1)}, s16[1,272,768]{2,1,0:T(8,128)(2,1)S(1)}, u32[]{:S(2)}, u32[]{:S(2)}) %collective-permute-start.1) | collective-permute-done | bytes 417824 | tf_op jit(solution)/shard_map/ppermute | solution.py:370
  134.9 4.4 %adam.7 = (f32[1024,768]{1,0:T(8,128)}, bf16[1024,768]{1,0:T(8,128)(2,1)}, bf16[1024,768]{1,0:T(8,128)(2,1)}, f32[1]{0:T(128)}) custom-call(f32[1024,768]{1,0:T(8,128)} %copy-done, s16[1,272,768]{2,1,0:T(8,128)(2,1)} %copy-done.13, f32[1024,768]{1,0:T(8,128)} %refs_2_.7, ...), custom_call_target="tpu_custom_call", output_to_operand_aliasing={{0}: (5, {}), {1}: (6, {}), {2}: (7, {})} | custom-call | flops 1024 | bytes 1024 | tf_op jit(solution)/shard_map/adam/pallas_call | solution.py:251
  139.4 4.7 %collective-permute-done.5 = f32[1]{0:T(128)} collective-permute-done((f32[1]{0:T(128)}, f32[1]{0:T(128)}, u32[]{:S(2)}, u32[]{:S(2)}) %collective-permute-start.5) | collective-permute-done | bytes 36 | tf_op jit(solution)/shard_map/ppermute | solution.py:370
  146.8 5.2 %collective-permute-done.6 = f32[1]{0:T(128)} collective-permute-done((f32[1]{0:T(128)}, f32[1]{0:T(128)}, u32[]{:S(2)}, u32[]{:S(2)}) %collective-permute-start.6) | collective-permute-done | bytes 36 | tf_op jit(solution)/shard_map/ppermute | solution.py:370
  154.7 2.0 collective-permute-start.15
  156.8 34.3 %collective-permute-done.9.refs_1_.piece = bf16[512,768]{1,0:T(8,128)(2,1)S(1)} collective-permute-done((bf16[512,768]{1,0:T(8,128)(2,1)S(1)}, bf16[512,768]{1,0:T(8,128)(2,1)S(1)}, u32[]{:S(2)}, u32[]{:S(2)}) %collective-permute-start.9) | collective-permute-done | bytes 786464 | tf_op jit(solution)/shard_map/ppermute | solution.py:370
  191.9 2.9 %collective-permute-start.10 = (s16[272,768]{1,0:T(8,128)(2,1)}, s16[272,768]{1,0:T(8,128)(2,1)}, u32[]{:S(2)}, u32[]{:S(2)}) collective-permute-start(s16[272,768]{1,0:T(8,128)(2,1)} %gate.9.piece), channel_id=1, source_target_pairs={{0,2},{1,3},{2,0},{3,1},{4,6},{5,7},{6,4},{7,5},{8,10},{9,11},{10,... | collective-permute-start | bytes 1253384 | tf_op jit(solution)/shard_map/ppermute | solution.py:370
  195.0 27.2 %collective-permute-done.12.refs_1_.piece = s16[272,768]{1,0:T(8,128)(2,1)S(1)} collective-permute-done((s16[272,768]{1,0:T(8,128)(2,1)}, s16[272,768]{1,0:T(8,128)(2,1)S(1)}, u32[]{:S(2)}, u32[]{:S(2)}) %collective-permute-start.12) | collective-permute-done | bytes 417824 | tf_op jit(solution)/shard_map/ppermute | solution.py:370
  226.0 5.1 %collective-permute-done.10.piece = s16[272,768]{1,0:T(8,128)(2,1)} collective-permute-done((s16[272,768]{1,0:T(8,128)(2,1)}, s16[272,768]{1,0:T(8,128)(2,1)}, u32[]{:S(2)}, u32[]{:S(2)}) %collective-permute-start.10) | collective-permute-done | bytes 417824 | tf_op jit(solution)/shard_map/ppermute | solution.py:370
  234.0 2.0 place.15.refs_0_
  244.1 2.0 place.21.refs_0_
  (72 shorter events, 32.8 us)
Async XLA Ops:
  2.7 21.6 %collective-permute-start = (bf16[512,768]{1,0:T(8,128)(2,1)S(1)}, bf16[512,768]{1,0:T(8,128)(2,1)}, u32[]{:S(2)}, u32[]{:S(2)}) collective-permute-start(bf16[512,768]{1,0:T(8,128)(2,1)S(1)} %broadcast_select_fusion.refs_3_), channel_id=1, source_target_pairs={{0,1},{1,0},{2,3},{3,2},{4,5},{5,4},{6,7},{7,6},{8,9},{9,8},{10,11... | collective-permute-start | bytes 2359304 | tf_op jit(solution)/shard_map/ppermute | solution.py:370
  9.4 38.5 %all-to-all-start = ((bf16[16,64,1024]{2,1,0:T(8,128)(2,1)}), bf16[16,64,1024]{2,1,0:T(8,128)(2,1)S(1)}, u32[]{:S(2)}, u32[]{:S(2)}) async-start(bf16[16,64,1024]{2,1,0:T(8,128)(2,1)} %bitcast.33), calls=%async_computation | async-start | bytes 4194304 | tf_op jit(solution)/shard_map/all_to_all | solution.py:380
  50.3 0.8 copy-start.6
  51.1 4.6 %copy-start.7 = (s16[1,272,768]{2,1,0:T(8,128)(2,1)S(1)}, s16[1,272,768]{2,1,0:T(8,128)(2,1)}, u32[]{:S(2)}) copy-start(s16[1,272,768]{2,1,0:T(8,128)(2,1)} %copy-done.6) | copy-start | bytes 1253380
  51.1 54.5 %all-to-all-start.1 = ((bf16[16,64,1024]{2,1,0:T(8,128)(2,1)}), bf16[16,64,1024]{2,1,0:T(8,128)(2,1)}, u32[]{:S(2)}, u32[]{:S(2)}) async-start(bf16[16,64,1024]{2,1,0:T(8,128)(2,1)} %bitcast.32), calls=%async_computation.1 | async-start | bytes 4194304 | tf_op jit(solution)/shard_map/all_to_all | solution.py:380
  55.6 33.9 %collective-permute-start.4 = (s16[1,272,768]{2,1,0:T(8,128)(2,1)S(1)}, s16[1,272,768]{2,1,0:T(8,128)(2,1)}, u32[]{:S(2)}, u32[]{:S(2)}) collective-permute-start(s16[1,272,768]{2,1,0:T(8,128)(2,1)S(1)} %copy-done.7), channel_id=1, source_target_pairs={{0,2},{1,3},{2,0},{3,1},{4,6},{5,7},{6,4},{7,5},{8,10},{9,11},{10,... | collective-permute-start | bytes 1253384 | tf_op jit(solution)/shard_map/ppermute | solution.py:370
  67.7 48.4 %collective-permute-start.3 = (s16[1,272,768]{2,1,0:T(8,128)(2,1)}, s16[1,272,768]{2,1,0:T(8,128)(2,1)S(1)}, u32[]{:S(2)}, u32[]{:S(2)}) collective-permute-start(s16[1,272,768]{2,1,0:T(8,128)(2,1)} %coded_sum.7), channel_id=1, source_target_pairs={{0,2},{1,3},{2,0},{3,1},{4,6},{5,7},{6,4},{7,5},{8,10},{9,11},{10,... | collective-permute-start | bytes 1253384 | tf_op jit(solution)/shard_map/ppermute | solution.py:370
  68.0 58.2 %collective-permute-start.2 = (s16[1,272,768]{2,1,0:T(8,128)(2,1)}, s16[1,272,768]{2,1,0:T(8,128)(2,1)S(1)}, u32[]{:S(2)}, u32[]{:S(2)}) collective-permute-start(s16[1,272,768]{2,1,0:T(8,128)(2,1)} %coded_sum.6), channel_id=1, source_target_pairs={{0,2},{1,3},{2,0},{3,1},{4,6},{5,7},{6,4},{7,5},{8,10},{9,11},{10,... | collective-permute-start | bytes 1253384 | tf_op jit(solution)/shard_map/ppermute | solution.py:370
  70.6 63.5 %collective-permute-start.1 = (s16[1,272,768]{2,1,0:T(8,128)(2,1)}, s16[1,272,768]{2,1,0:T(8,128)(2,1)S(1)}, u32[]{:S(2)}, u32[]{:S(2)}) collective-permute-start(s16[1,272,768]{2,1,0:T(8,128)(2,1)} %coded_sum.5), channel_id=1, source_target_pairs={{0,2},{1,3},{2,0},{3,1},{4,6},{5,7},{6,4},{7,5},{8,10},{9,11},{10,... | collective-permute-start | bytes 1253384 | tf_op jit(solution)/shard_map/ppermute | solution.py:370
  110.4 1.7 copy-start
  116.1 0.8 copy-start.15
  116.9 4.8 %copy-start.8 = (s16[1,272,768]{2,1,0:T(8,128)(2,1)S(1)}, s16[1,272,768]{2,1,0:T(8,128)(2,1)}, u32[]{:S(2)}) copy-start(s16[1,272,768]{2,1,0:T(8,128)(2,1)} %get-tuple-element.40) | copy-start | bytes 1253380
  121.6 31.0 %collective-permute-start.8 = (s16[272,768]{1,0:T(8,128)(2,1)}, s16[272,768]{1,0:T(8,128)(2,1)S(1)}, u32[]{:S(2)}, u32[]{:S(2)}) collective-permute-start(s16[272,768]{1,0:T(8,128)(2,1)} %bitcast.30), channel_id=1, source_target_pairs={{0,1},{1,0},{2,3},{3,2},{4,5},{5,4},{6,7},{7,6},{8,9},{9,8},{10,11... | collective-permute-start | bytes 1253384 | tf_op jit(solution)/shard_map/ppermute | solution.py:370
  121.7 30.9 %collective-permute-start.7 = (s16[272,768]{1,0:T(8,128)(2,1)S(1)}, s16[272,768]{1,0:T(8,128)(2,1)S(1)}, u32[]{:S(2)}, u32[]{:S(2)}) collective-permute-start(s16[272,768]{1,0:T(8,128)(2,1)S(1)} %bitcast.29), channel_id=1, source_target_pairs={{0,1},{1,0},{2,3},{3,2},{4,5},{5,4},{6,7},{7,6},{8,9},{9,8},{10,11... | collective-permute-start | bytes 1253384 | tf_op jit(solution)/shard_map/ppermute | solution.py:370
  139.3 4.8 %collective-permute-start.5 = (f32[1]{0:T(128)}, f32[1]{0:T(128)}, u32[]{:S(2)}, u32[]{:S(2)}) collective-permute-start(f32[1]{0:T(128)} %get-tuple-element.38), channel_id=1, source_target_pairs={{0,2},{1,3},{2,0},{3,1},{4,6},{5,7},{6,4},{7,5},{8,10},{9,11},{10,... | collective-permute-start | bytes 20 | tf_op jit(solution)/shard_map/ppermute | solution.py:370
  145.4 6.6 %collective-permute-start.6 = (f32[1]{0:T(128)}, f32[1]{0:T(128)}, u32[]{:S(2)}, u32[]{:S(2)}) collective-permute-start(f32[1]{0:T(128)} %max.6), channel_id=1, source_target_pairs={{0,1},{1,0},{2,3},{3,2},{4,5},{5,4},{6,7},{7,6},{8,9},{9,8},{10,11... | collective-permute-start | bytes 20 | tf_op jit(solution)/shard_map/ppermute | solution.py:370
  152.6 1.9 copy-start.1
  154.7 67.5 %copy-start.2 = (bf16[512,768]{1,0:T(8,128)(2,1)}, bf16[512,768]{1,0:T(8,128)(2,1)S(1)}, u32[]{:S(2)}) copy-start(bf16[512,768]{1,0:T(8,128)(2,1)S(1)} %scale.1.refs_0_) | copy-start | bytes 2359300
  154.7 36.4 %collective-permute-start.9 = (bf16[512,768]{1,0:T(8,128)(2,1)S(1)}, bf16[512,768]{1,0:T(8,128)(2,1)S(1)}, u32[]{:S(2)}, u32[]{:S(2)}) collective-permute-start(bf16[512,768]{1,0:T(8,128)(2,1)S(1)} %scale.1.refs_0_), channel_id=1, source_target_pairs={{0,2},{1,3},{2,0},{3,1},{4,6},{5,7},{6,4},{7,5},{8,10},{9,11},{10,... | collective-permute-start | bytes 2359304 | tf_op jit(solution)/shard_map/ppermute | solution.py:370
  154.7 67.4 %collective-permute-start.15 = (bf16[512,768]{1,0:T(8,128)(2,1)S(1)}, bf16[512,768]{1,0:T(8,128)(2,1)S(1)}, u32[]{:S(2)}, u32[]{:S(2)}) collective-permute-start(bf16[512,768]{1,0:T(8,128)(2,1)S(1)} %scale.1.refs_0_), channel_id=1, source_target_pairs={{0,1},{1,0},{2,3},{3,2},{4,5},{5,4},{6,7},{7,6},{8,9},{9,8},{10,11... | collective-permute-start | bytes 2359304 | tf_op jit(solution)/shard_map/ppermute | solution.py:370
  191.1 0.9 copy-start.4
  191.9 30.2 %collective-permute-start.12 = (s16[272,768]{1,0:T(8,128)(2,1)}, s16[272,768]{1,0:T(8,128)(2,1)S(1)}, u32[]{:S(2)}, u32[]{:S(2)}) collective-permute-start(s16[272,768]{1,0:T(8,128)(2,1)} %gate.10.piece), channel_id=1, source_target_pairs={{0,2},{1,3},{2,0},{3,1},{4,6},{5,7},{6,4},{7,5},{8,10},{9,11},{10,... | collective-permute-start | bytes 1253384 | tf_op jit(solution)/shard_map/ppermute | solution.py:370
  191.9 39.2 %collective-permute-start.10 = (s16[272,768]{1,0:T(8,128)(2,1)}, s16[272,768]{1,0:T(8,128)(2,1)}, u32[]{:S(2)}, u32[]{:S(2)}) collective-permute-start(s16[272,768]{1,0:T(8,128)(2,1)} %gate.9.piece), channel_id=1, source_target_pairs={{0,2},{1,3},{2,0},{3,1},{4,6},{5,7},{6,4},{7,5},{8,10},{9,11},{10,... | collective-permute-start | bytes 1253384 | tf_op jit(solution)/shard_map/ppermute | solution.py:370
  194.9 49.2 %collective-permute-start.14 = (bf16[512,768]{1,0:T(8,128)(2,1)}, bf16[512,768]{1,0:T(8,128)(2,1)}, u32[]{:S(2)}, u32[]{:S(2)}) collective-permute-start(bf16[512,768]{1,0:T(8,128)(2,1)} %copy-done.4), channel_id=1, source_target_pairs={{0,1},{1,0},{2,3},{3,2},{4,5},{5,4},{6,7},{7,6},{8,9},{9,8},{10,11... | collective-permute-start | bytes 2359304 | tf_op jit(solution)/shard_map/ppermute | solution.py:370
  222.2 0.8 copy-start.11
  222.2 23.9 %collective-permute-start.13 = (s16[272,768]{1,0:T(8,128)(2,1)S(1)}, s16[272,768]{1,0:T(8,128)(2,1)}, u32[]{:S(2)}, u32[]{:S(2)}) collective-permute-start(s16[272,768]{1,0:T(8,128)(2,1)S(1)} %collective-permute-done.12.refs_1_.piece), channel_id=1, source_target_pairs={{0,1},{1,0},{2,3},{3,2},{4,5},{5,4},{6,7},{7,6},{8,9},{9,8},{10,11... | collective-permute-start | bytes 1253384 | tf_op jit(solution)/shard_map/ppermute | solution.py:370
  222.9 1.1 copy-start.3
  224.1 7.1 %copy-start.9 = (s16[272,768]{1,0:T(8,128)(2,1)S(1)}, s16[272,768]{1,0:T(8,128)(2,1)}, u32[]{:S(2)}) copy-start(s16[272,768]{1,0:T(8,128)(2,1)} %gate.10.piece) | copy-start | bytes 1253380
  231.1 18.6 %collective-permute-start.11 = (s16[272,768]{1,0:T(8,128)(2,1)}, s16[272,768]{1,0:T(8,128)(2,1)S(1)}, u32[]{:S(2)}, u32[]{:S(2)}) collective-permute-start(s16[272,768]{1,0:T(8,128)(2,1)} %collective-permute-done.10.piece), channel_id=1, source_target_pairs={{0,1},{1,0},{2,3},{3,2},{4,5},{5,4},{6,7},{7,6},{8,9},{9,8},{10,11... | collective-permute-start | bytes 1253384 | tf_op jit(solution)/shard_map/ppermute | solution.py:370
  231.1 1.4 copy-start.10
  232.6 1.4 copy-start.5
  234.0 2.0 copy-start.12
  (2 other events, 1.5 us)

commit v5 on v4

--- a/solution.py
+++ b/solution.py
@@ -407,7 +407,7 @@
             ahead.append(piece[0])
     new_master, new_one, new_two, peak = results
 
-    beside = [swap(piece, 1) for piece in ahead]
+    beside = [gate(swap(piece, 1), (), work) for piece, work in zip(ahead, (1<<34, 1024))]
     step = half
     while step:
         peak = jnp.maximum(peak, swap(peak, step))

time: 253 us -> 252 us (level)
  waiting for transfers between devices: 149 us -> 141 us
  starting transfers between devices: 26 us -> 31.2 us
    ppermute x16, waiting for transfers between devices: 110 us -> 101 us  [swap(): return lax.ppermute(x, chain, [(i, i ^ k) for i in range(replicas)])]
    ppermute x16, starting transfers between devices: 17.6 us -> 22.8 us  [swap(): return lax.ppermute(x, chain, [(i, i ^ k) for i in range(replicas)])]
    unnamed x32 -> x24, local copies, waits for them, and re-layouts: 9.34 us -> 8.2 us
  transfers between devices with their start and end apart: 18 -> 18, of which waited for: 12 -> 12; matrix products, arithmetic and copies ran while one was open for 0% -> 0% of each run, Pallas kernels for 22% -> 23%
where the time goes in v5:
time: 252 us; the launch traced here: 249 us
  waiting for transfers between devices  141 us (56%)
  Pallas kernels  61.5 us (24%)
  starting transfers between devices  31.2 us (12%)
  local copies, waits for them, and re-layouts  8.28 us (3%)
  between operations  3.89 us (2%)
  other arithmetic  3.11 us (1%)
    ppermute x16, waiting for transfers between devices, swap(): return lax.ppermute(x, chain, [(i, i ^ k) for i in range(replicas)])  101 us
    all_to_all x2, waiting for transfers between devices, arrive(): return lax.all_to_all(picked, ('near', 'expert'), 0, 0, tiled=True)  39.8 us
    ppermute x16, starting transfers between devices, swap(): return lax.ppermute(x, chain, [(i, i ^ k) for i in range(replicas)])  22.8 us
    pallas_call x12, Pallas kernels, place(): pl.pallas_call(functools.partial(place_kernel, strips, coded), out_shape=...  20.4 us
    pallas_call x4, Pallas kernels, adam(): pl.pallas_call(functools.partial(adam_kernel, arrays, at, block, size, ah...  17.5 us
    pallas_call x5, Pallas kernels, summed(): pl.pallas_call(functools.partial(kernel, count), out_shape=out_shape, gri...  16.5 us
    all_to_all x2, starting transfers between devices, arrive(): return lax.all_to_all(picked, ('near', 'expert'), 0, 0, tiled=True)  8.41 us
    unnamed x24, local copies, waits for them, and re-layouts  8.2 us
  transfers between devices with their start and end apart: 18, of which 12 were waited for; matrix products, arithmetic and copies ran while one was open for 0% of the time, Pallas kernels for 23%

profile of v5, /device:TPU:0, one launch (start us, length us, event | category | flops | bytes accessed | tf_op | source)
XLA Modules:
  0.0 248.9 jit_solution(13585220839395026255)
XLA Ops:
  2.7 3.1 %collective-permute-start = (bf16[512,768]{1,0:T(8,128)(2,1)S(1)}, bf16[512,768]{1,0:T(8,128)(2,1)}, u32[]{:S(2)}, u32[]{:S(2)}) collective-permute-start(bf16[512,768]{1,0:T(8,128)(2,1)S(1)} %broadcast_select_fusion.refs_3_), channel_id=1, source_target_pairs={{0,1},{1,0},{2,3},{3,2},{4,5},{5,4},{6,7},{7,6},{8,9},{9,8},{10,11... | collective-permute-start | bytes 2359304 | tf_op jit(solution)/shard_map/ppermute | solution.py:370
  6.3 3.1 %pick_columns.3 = bf16[1024,1024]{1,0:T(8,128)(2,1)} custom-call(s32[2]{0:T(128)} %and_select_fusion.table_ref, bf16[512,4096]{1,0:T(8,128)(2,1)} %x_ref.3), custom_call_target="tpu_custom_call" | custom-call | flops 1024 | bytes 1024 | tf_op jit(solution)/shard_map/pick_columns/pallas_call | solution.py:63
  9.4 3.8 %all-to-all-start = ((bf16[16,64,1024]{2,1,0:T(8,128)(2,1)}), bf16[16,64,1024]{2,1,0:T(8,128)(2,1)S(1)}, u32[]{:S(2)}, u32[]{:S(2)}) async-start(bf16[16,64,1024]{2,1,0:T(8,128)(2,1)} %bitcast.31), calls=%async_computation | async-start | bytes 4194304 | tf_op jit(solution)/shard_map/all_to_all | solution.py:380
  13.8 3.1 %pick_columns.2.refs_0_ = bf16[1024,1024]{1,0:T(8,128)(2,1)} custom-call(s32[2]{0:T(128)} %and_select_fusion.1.table_ref, bf16[512,4096]{1,0:T(8,128)(2,1)} %x_ref.3), custom_call_target="tpu_custom_call" | custom-call | flops 1024 | bytes 1024 | tf_op jit(solution)/shard_map/pick_columns/pallas_call | solution.py:63
  16.9 7.4 %collective-permute-done.refs_0_ = bf16[512,768]{1,0:T(8,128)(2,1)} collective-permute-done((bf16[512,768]{1,0:T(8,128)(2,1)S(1)}, bf16[512,768]{1,0:T(8,128)(2,1)}, u32[]{:S(2)}, u32[]{:S(2)}) %collective-permute-start) | collective-permute-done | bytes 786464 | tf_op jit(solution)/shard_map/ppermute | solution.py:370
  24.3 23.7 %all-to-all-done = bf16[16,64,1024]{2,1,0:T(8,128)(2,1)S(1)} async-done(((bf16[16,64,1024]{2,1,0:T(8,128)(2,1)}), bf16[16,64,1024]{2,1,0:T(8,128)(2,1)S(1)}, u32[]{:S(2)}, u32[]{:S(2)}) %all-to-all-start) | async-done | bytes 2097184 | tf_op jit(solution)/shard_map/all_to_all | solution.py:380
  47.9 2.4 coded_sum.4.refs_1_
  51.1 4.6 %all-to-all-start.1 = ((bf16[16,64,1024]{2,1,0:T(8,128)(2,1)}), bf16[16,64,1024]{2,1,0:T(8,128)(2,1)}, u32[]{:S(2)}, u32[]{:S(2)}) async-start(bf16[16,64,1024]{2,1,0:T(8,128)(2,1)} %bitcast.30), calls=%async_computation.1 | async-start | bytes 4194304 | tf_op jit(solution)/shard_map/all_to_all | solution.py:380
  55.6 2.7 %collective-permute-start.4 = (s16[1,272,768]{2,1,0:T(8,128)(2,1)S(1)}, s16[1,272,768]{2,1,0:T(8,128)(2,1)}, u32[]{:S(2)}, u32[]{:S(2)}) collective-permute-start(s16[1,272,768]{2,1,0:T(8,128)(2,1)S(1)} %copy-done.5), channel_id=1, source_target_pairs={{0,2},{1,3},{2,0},{3,1},{4,6},{5,7},{6,4},{7,5},{8,10},{9,11},{10,... | collective-permute-start | bytes 1253384 | tf_op jit(solution)/shard_map/ppermute | solution.py:370
  58.3 3.1 %coded_sum.7 = s16[1,272,768]{2,1,0:T(8,128)(2,1)} custom-call(s32[2]{0:T(128)S(1)} %pad_add_fusion.refs_0_, bf16[1024,1024]{1,0:T(8,128)(2,1)S(1)} %bitcast.22, bf16[1024,1024]{1,0:T(8,128)(2,1)S(1)} %bitcast.23, bf16[512,768]{1,0:T(8,128)(2,1)S(1)} %broadcast_select_fusion.refs_3_, bf16[512,768]{1,0:T(8,128)(2,1)} %gate.7.refs_4_), custom_call_target="tpu_custom_call" | custom-call | flops 1024 | bytes 1024 | tf_op jit(solution)/shard_map/coded_sum/pallas_call | solution.py:145
  61.4 3.1 %coded_sum.6 = s16[1,272,768]{2,1,0:T(8,128)(2,1)} custom-call(s32[2]{0:T(128)S(1)} %pad_add_fusion.refs_0_, bf16[1024,1024]{1,0:T(8,128)(2,1)S(1)} %bitcast.24, bf16[1024,1024]{1,0:T(8,128)(2,1)S(1)} %bitcast.25, bf16[512,768]{1,0:T(8,128)(2,1)S(1)} %broadcast_select_fusion.refs_3_, bf16[512,768]{1,0:T(8,128)(2,1)} %gate.7.refs_4_), custom_call_target="tpu_custom_call" | custom-call | flops 1024 | bytes 1024 | tf_op jit(solution)/shard_map/coded_sum/pallas_call | solution.py:145
  64.5 3.1 %coded_sum.5 = s16[1,272,768]{2,1,0:T(8,128)(2,1)} custom-call(s32[2]{0:T(128)S(1)} %pad_add_fusion.refs_0_, bf16[1024,1024]{1,0:T(8,128)(2,1)S(1)} %bitcast.26, bf16[1024,1024]{1,0:T(8,128)(2,1)S(1)} %bitcast.27, bf16[512,768]{1,0:T(8,128)(2,1)S(1)} %broadcast_select_fusion.refs_3_, bf16[512,768]{1,0:T(8,128)(2,1)} %gate.7.refs_4_), custom_call_target="tpu_custom_call" | custom-call | flops 1024 | bytes 1024 | tf_op jit(solution)/shard_map/coded_sum/pallas_call | solution.py:145
  68.0 2.6 %collective-permute-start.2 = (s16[1,272,768]{2,1,0:T(8,128)(2,1)}, s16[1,272,768]{2,1,0:T(8,128)(2,1)S(1)}, u32[]{:S(2)}, u32[]{:S(2)}) collective-permute-start(s16[1,272,768]{2,1,0:T(8,128)(2,1)} %coded_sum.6), channel_id=1, source_target_pairs={{0,2},{1,3},{2,0},{3,1},{4,6},{5,7},{6,4},{7,5},{8,10},{9,11},{10,... | collective-permute-start | bytes 1253384 | tf_op jit(solution)/shard_map/ppermute | solution.py:370
  70.9 18.6 %collective-permute-done.4.refs_0_ = s16[1,272,768]{2,1,0:T(8,128)(2,1)} collective-permute-done((s16[1,272,768]{2,1,0:T(8,128)(2,1)S(1)}, s16[1,272,768]{2,1,0:T(8,128)(2,1)}, u32[]{:S(2)}, u32[]{:S(2)}) %collective-permute-start.4) | collective-permute-done | bytes 417824 | tf_op jit(solution)/shard_map/ppermute | solution.py:370
  89.5 16.1 %all-to-all-done.1 = bf16[16,64,1024]{2,1,0:T(8,128)(2,1)} async-done(((bf16[16,64,1024]{2,1,0:T(8,128)(2,1)}), bf16[16,64,1024]{2,1,0:T(8,128)(2,1)}, u32[]{:S(2)}, u32[]{:S(2)}) %all-to-all-start.1) | async-done | bytes 2097184 | tf_op jit(solution)/shard_map/all_to_all | solution.py:380
  105.6 4.8 %own_sum.1.refs_0_ = f32[1024,768]{1,0:T(8,128)S(1)} custom-call(s32[2]{0:T(128)S(1)} %pad_add_fusion.refs_0_, bf16[1024,1024]{1,0:T(8,128)(2,1)} %bitcast.5.refs_1_.refs_2_, bf16[1024,1024]{1,0:T(8,128)(2,1)} %bitcast.5.refs_1_.refs_2_, bf16[512,768]{1,0:T(8,128)(2,1)S(1)} %broadcast_select_fusion.refs_3_, bf16[512,768]{1,0:T(8,128)(2,1)} %gate.7.refs_4_), custom_call_target="tpu_custom_call" | custom-call | flops 1024 | bytes 1024 | tf_op jit(solution)/shard_map/own_sum/pallas_call | solution.py:145
  112.1 4.0 %adam.4 = (f32[1024,768]{1,0:T(8,128)}, bf16[1024,768]{1,0:T(8,128)(2,1)}, bf16[1024,768]{1,0:T(8,128)(2,1)}, f32[1]{0:T(128)}, s16[1,272,768]{2,1,0:T(8,128)(2,1)}) custom-call(f32[1024,768]{1,0:T(8,128)} %copy-done, s16[1,272,768]{2,1,0:T(8,128)(2,1)} %gate.9.refs_1_, f32[1024,768]{1,0:T(8,128)} %refs_2_.7, bf16[1024,768]{1,0:T(8,128)(2,1)} %refs_3_.7, ...), custom_call_target="tpu_custom_call" | custom-call | flops 1024 | bytes 1024 | tf_op jit(solution)/shard_map/adam/pallas_call | solution.py:251
  117.0 4.7 %adam.5 = (f32[1024,768]{1,0:T(8,128)}, bf16[1024,768]{1,0:T(8,128)(2,1)}, bf16[1024,768]{1,0:T(8,128)(2,1)}, f32[1]{0:T(128)}, s16[1,272,768]{2,1,0:T(8,128)(2,1)}) custom-call(f32[1024,768]{1,0:T(8,128)} %copy-done, s16[1,272,768]{2,1,0:T(8,128)(2,1)} %copy-done.11, ...), custom_call_target="tpu_custom_call", output_to_operand_aliasing={{0}: (5, {}), {1}: (6, {}), {2}: (7, {})} | custom-call | flops 1024 | bytes 1024 | tf_op jit(solution)/shard_map/adam/pallas_call | solution.py:251
  121.7 4.5 %collective-permute-done.2.refs_1_ = s16[1,272,768]{2,1,0:T(8,128)(2,1)S(1)} collective-permute-done((s16[1,272,768]{2,1,0:T(8,128)(2,1)}, s16[1,272,768]{2,1,0:T(8,128)(2,1)S(1)}, u32[]{:S(2)}, u32[]{:S(2)}) %collective-permute-start.2) | collective-permute-done | bytes 417824 | tf_op jit(solution)/shard_map/ppermute | solution.py:370
  126.9 4.5 %adam.6 = (f32[1024,768]{1,0:T(8,128)}, bf16[1024,768]{1,0:T(8,128)(2,1)}, bf16[1024,768]{1,0:T(8,128)(2,1)}, f32[1]{0:T(128)}) custom-call(f32[1024,768]{1,0:T(8,128)} %copy-done, s16[1,272,768]{2,1,0:T(8,128)(2,1)} %copy-done.10, f32[1024,768]{1,0:T(8,128)} %refs_2_.7, ...), custom_call_target="tpu_custom_call", output_to_operand_aliasing={{0}: (5, {}), {1}: (6, {}), {2}: (7, {})} | custom-call | flops 1024 | bytes 1024 | tf_op jit(solution)/shard_map/adam/pallas_call | solution.py:251
  131.4 2.8 %collective-permute-done.1.refs_1_ = s16[1,272,768]{2,1,0:T(8,128)(2,1)S(1)} collective-permute-done((s16[1,272,768]{2,1,0:T(8,128)(2,1)}, s16[1,272,768]{2,1,0:T(8,128)(2,1)S(1)}, u32[]{:S(2)}, u32[]{:S(2)}) %collective-permute-start.1) | collective-permute-done | bytes 417824 | tf_op jit(solution)/shard_map/ppermute | solution.py:370
  134.9 4.4 %adam.7 = (f32[1024,768]{1,0:T(8,128)}, bf16[1024,768]{1,0:T(8,128)(2,1)}, bf16[1024,768]{1,0:T(8,128)(2,1)}, f32[1]{0:T(128)}) custom-call(f32[1024,768]{1,0:T(8,128)} %copy-done, s16[1,272,768]{2,1,0:T(8,128)(2,1)} %copy-done.9, f32[1024,768]{1,0:T(8,128)} %refs_2_.7, ...), custom_call_target="tpu_custom_call", output_to_operand_aliasing={{0}: (5, {}), {1}: (6, {}), {2}: (7, {})} | custom-call | flops 1024 | bytes 1024 | tf_op jit(solution)/shard_map/adam/pallas_call | solution.py:251
  139.4 2.0 collective-permute-start.8
  141.4 2.7 %collective-permute-done.5 = f32[1]{0:T(128)} collective-permute-done((f32[1]{0:T(128)}, f32[1]{0:T(128)}, u32[]{:S(2)}, u32[]{:S(2)}) %collective-permute-start.5) | collective-permute-done | bytes 36 | tf_op jit(solution)/shard_map/ppermute | solution.py:370
  145.3 4.2 %collective-permute-start.6 = (f32[1]{0:T(128)}, f32[1]{0:T(128)}, u32[]{:S(2)}, u32[]{:S(2)}) collective-permute-start(f32[1]{0:T(128)} %max.6), channel_id=1, source_target_pairs={{0,1},{1,0},{2,3},{3,2},{4,5},{5,4},{6,7},{7,6},{8,9},{9,8},{10,11... | collective-permute-start | bytes 20 | tf_op jit(solution)/shard_map/ppermute | solution.py:370
  153.9 2.6 %collective-permute-start.9 = (bf16[512,768]{1,0:T(8,128)(2,1)}, bf16[512,768]{1,0:T(8,128)(2,1)S(1)}, u32[]{:S(2)}, u32[]{:S(2)}) collective-permute-start(bf16[512,768]{1,0:T(8,128)(2,1)} %scale.1.refs_0_), channel_id=1, source_target_pairs={{0,2},{1,3},{2,0},{3,1},{4,6},{5,7},{6,4},{7,5},{8,10},{9,11},{10,... | collective-permute-start | bytes 2359304 | tf_op jit(solution)/shard_map/ppermute | solution.py:370
  157.6 31.9 %collective-permute-done.9.refs_1_.piece = bf16[512,768]{1,0:T(8,128)(2,1)S(1)} collective-permute-done((bf16[512,768]{1,0:T(8,128)(2,1)}, bf16[512,768]{1,0:T(8,128)(2,1)S(1)}, u32[]{:S(2)}, u32[]{:S(2)}) %collective-permute-start.9) | collective-permute-done | bytes 786464 | tf_op jit(solution)/shard_map/ppermute | solution.py:370
  190.4 2.9 %collective-permute-start.10 = (s16[272,768]{1,0:T(8,128)(2,1)}, s16[272,768]{1,0:T(8,128)(2,1)S(1)}, u32[]{:S(2)}, u32[]{:S(2)}) collective-permute-start(s16[272,768]{1,0:T(8,128)(2,1)} %gate.11.piece), channel_id=1, source_target_pairs={{0,2},{1,3},{2,0},{3,1},{4,6},{5,7},{6,4},{7,5},{8,10},{9,11},{10,... | collective-permute-start | bytes 1253384 | tf_op jit(solution)/shard_map/ppermute | solution.py:370
  194.1 27.5 %collective-permute-done.12.refs_1_.piece = s16[272,768]{1,0:T(8,128)(2,1)S(1)} collective-permute-done((s16[272,768]{1,0:T(8,128)(2,1)}, s16[272,768]{1,0:T(8,128)(2,1)S(1)}, u32[]{:S(2)}, u32[]{:S(2)}) %collective-permute-start.12) | collective-permute-done | bytes 417824 | tf_op jit(solution)/shard_map/ppermute | solution.py:370
  222.4 2.0 place.12.refs_0_
  224.4 4.1 %collective-permute-done.10.piece = s16[272,768]{1,0:T(8,128)(2,1)S(1)} collective-permute-done((s16[272,768]{1,0:T(8,128)(2,1)}, s16[272,768]{1,0:T(8,128)(2,1)S(1)}, u32[]{:S(2)}, u32[]{:S(2)}) %collective-permute-start.10) | collective-permute-done | bytes 417824 | tf_op jit(solution)/shard_map/ppermute | solution.py:370
  231.9 2.0 place.15.refs_0_
  (65 shorter events, 33.1 us)
Async XLA Ops:
  2.7 21.6 %collective-permute-start = (bf16[512,768]{1,0:T(8,128)(2,1)S(1)}, bf16[512,768]{1,0:T(8,128)(2,1)}, u32[]{:S(2)}, u32[]{:S(2)}) collective-permute-start(bf16[512,768]{1,0:T(8,128)(2,1)S(1)} %broadcast_select_fusion.refs_3_), channel_id=1, source_target_pairs={{0,1},{1,0},{2,3},{3,2},{4,5},{5,4},{6,7},{7,6},{8,9},{9,8},{10,11... | collective-permute-start | bytes 2359304 | tf_op jit(solution)/shard_map/ppermute | solution.py:370
  9.4 38.5 %all-to-all-start = ((bf16[16,64,1024]{2,1,0:T(8,128)(2,1)}), bf16[16,64,1024]{2,1,0:T(8,128)(2,1)S(1)}, u32[]{:S(2)}, u32[]{:S(2)}) async-start(bf16[16,64,1024]{2,1,0:T(8,128)(2,1)} %bitcast.31), calls=%async_computation | async-start | bytes 4194304 | tf_op jit(solution)/shard_map/all_to_all | solution.py:380
  50.3 0.8 copy-start.4
  51.1 4.6 %copy-start.5 = (s16[1,272,768]{2,1,0:T(8,128)(2,1)S(1)}, s16[1,272,768]{2,1,0:T(8,128)(2,1)}, u32[]{:S(2)}) copy-start(s16[1,272,768]{2,1,0:T(8,128)(2,1)} %copy-done.4) | copy-start | bytes 1253380
  51.1 54.6 %all-to-all-start.1 = ((bf16[16,64,1024]{2,1,0:T(8,128)(2,1)}), bf16[16,64,1024]{2,1,0:T(8,128)(2,1)}, u32[]{:S(2)}, u32[]{:S(2)}) async-start(bf16[16,64,1024]{2,1,0:T(8,128)(2,1)} %bitcast.30), calls=%async_computation.1 | async-start | bytes 4194304 | tf_op jit(solution)/shard_map/all_to_all | solution.py:380
  55.6 33.9 %collective-permute-start.4 = (s16[1,272,768]{2,1,0:T(8,128)(2,1)S(1)}, s16[1,272,768]{2,1,0:T(8,128)(2,1)}, u32[]{:S(2)}, u32[]{:S(2)}) collective-permute-start(s16[1,272,768]{2,1,0:T(8,128)(2,1)S(1)} %copy-done.5), channel_id=1, source_target_pairs={{0,2},{1,3},{2,0},{3,1},{4,6},{5,7},{6,4},{7,5},{8,10},{9,11},{10,... | collective-permute-start | bytes 1253384 | tf_op jit(solution)/shard_map/ppermute | solution.py:370
  67.7 48.5 %collective-permute-start.3 = (s16[1,272,768]{2,1,0:T(8,128)(2,1)}, s16[1,272,768]{2,1,0:T(8,128)(2,1)S(1)}, u32[]{:S(2)}, u32[]{:S(2)}) collective-permute-start(s16[1,272,768]{2,1,0:T(8,128)(2,1)} %coded_sum.7), channel_id=1, source_target_pairs={{0,2},{1,3},{2,0},{3,1},{4,6},{5,7},{6,4},{7,5},{8,10},{9,11},{10,... | collective-permute-start | bytes 1253384 | tf_op jit(solution)/shard_map/ppermute | solution.py:370
  68.0 58.2 %collective-permute-start.2 = (s16[1,272,768]{2,1,0:T(8,128)(2,1)}, s16[1,272,768]{2,1,0:T(8,128)(2,1)S(1)}, u32[]{:S(2)}, u32[]{:S(2)}) collective-permute-start(s16[1,272,768]{2,1,0:T(8,128)(2,1)} %coded_sum.6), channel_id=1, source_target_pairs={{0,2},{1,3},{2,0},{3,1},{4,6},{5,7},{6,4},{7,5},{8,10},{9,11},{10,... | collective-permute-start | bytes 1253384 | tf_op jit(solution)/shard_map/ppermute | solution.py:370
  70.6 63.5 %collective-permute-start.1 = (s16[1,272,768]{2,1,0:T(8,128)(2,1)}, s16[1,272,768]{2,1,0:T(8,128)(2,1)S(1)}, u32[]{:S(2)}, u32[]{:S(2)}) collective-permute-start(s16[1,272,768]{2,1,0:T(8,128)(2,1)} %coded_sum.5), channel_id=1, source_target_pairs={{0,2},{1,3},{2,0},{3,1},{4,6},{5,7},{6,4},{7,5},{8,10},{9,11},{10,... | collective-permute-start | bytes 1253384 | tf_op jit(solution)/shard_map/ppermute | solution.py:370
  110.4 1.7 copy-start
  116.1 34.9 %collective-permute-start.7 = (s16[272,768]{1,0:T(8,128)(2,1)}, s16[272,768]{1,0:T(8,128)(2,1)}, u32[]{:S(2)}, u32[]{:S(2)}) collective-permute-start(s16[272,768]{1,0:T(8,128)(2,1)} %bitcast.28), channel_id=1, source_target_pairs={{0,1},{1,0},{2,3},{3,2},{4,5},{5,4},{6,7},{7,6},{8,9},{9,8},{10,11... | collective-permute-start | bytes 1253384 | tf_op jit(solution)/shard_map/ppermute | solution.py:370
  116.2 0.8 copy-start.11
  126.2 0.8 copy-start.10
  134.1 0.8 copy-start.9
  139.3 4.8 %collective-permute-start.5 = (f32[1]{0:T(128)}, f32[1]{0:T(128)}, u32[]{:S(2)}, u32[]{:S(2)}) collective-permute-start(f32[1]{0:T(128)} %get-tuple-element.38), channel_id=1, source_target_pairs={{0,2},{1,3},{2,0},{3,1},{4,6},{5,7},{6,4},{7,5},{8,10},{9,11},{10,... | collective-permute-start | bytes 20 | tf_op jit(solution)/shard_map/ppermute | solution.py:370
  139.4 11.7 %collective-permute-start.8 = (s16[272,768]{1,0:T(8,128)(2,1)}, s16[272,768]{1,0:T(8,128)(2,1)}, u32[]{:S(2)}, u32[]{:S(2)}) collective-permute-start(s16[272,768]{1,0:T(8,128)(2,1)} %bitcast.7.refs_0_), channel_id=1, source_target_pairs={{0,1},{1,0},{2,3},{3,2},{4,5},{5,4},{6,7},{7,6},{8,9},{9,8},{10,11... | collective-permute-start | bytes 1253384 | tf_op jit(solution)/shard_map/ppermute | solution.py:370
  145.3 5.1 %collective-permute-start.6 = (f32[1]{0:T(128)}, f32[1]{0:T(128)}, u32[]{:S(2)}, u32[]{:S(2)}) collective-permute-start(f32[1]{0:T(128)} %max.6), channel_id=1, source_target_pairs={{0,1},{1,0},{2,3},{3,2},{4,5},{5,4},{6,7},{7,6},{8,9},{9,8},{10,11... | collective-permute-start | bytes 20 | tf_op jit(solution)/shard_map/ppermute | solution.py:370
  151.0 1.9 copy-start.1
  153.9 35.6 %collective-permute-start.9 = (bf16[512,768]{1,0:T(8,128)(2,1)}, bf16[512,768]{1,0:T(8,128)(2,1)S(1)}, u32[]{:S(2)}, u32[]{:S(2)}) collective-permute-start(bf16[512,768]{1,0:T(8,128)(2,1)} %scale.1.refs_0_), channel_id=1, source_target_pairs={{0,2},{1,3},{2,0},{3,1},{4,6},{5,7},{6,4},{7,5},{8,10},{9,11},{10,... | collective-permute-start | bytes 2359304 | tf_op jit(solution)/shard_map/ppermute | solution.py:370
  156.4 65.2 %collective-permute-start.15 = (bf16[512,768]{1,0:T(8,128)(2,1)}, bf16[512,768]{1,0:T(8,128)(2,1)S(1)}, u32[]{:S(2)}, u32[]{:S(2)}) collective-permute-start(bf16[512,768]{1,0:T(8,128)(2,1)} %scale.1.refs_0_), channel_id=1, source_target_pairs={{0,1},{1,0},{2,3},{3,2},{4,5},{5,4},{6,7},{7,6},{8,9},{9,8},{10,11... | collective-permute-start | bytes 2359304 | tf_op jit(solution)/shard_map/ppermute | solution.py:370
  189.5 0.9 copy-start.2
  190.4 31.3 %collective-permute-start.12 = (s16[272,768]{1,0:T(8,128)(2,1)}, s16[272,768]{1,0:T(8,128)(2,1)S(1)}, u32[]{:S(2)}, u32[]{:S(2)}) collective-permute-start(s16[272,768]{1,0:T(8,128)(2,1)} %gate.12.piece), channel_id=1, source_target_pairs={{0,2},{1,3},{2,0},{3,1},{4,6},{5,7},{6,4},{7,5},{8,10},{9,11},{10,... | collective-permute-start | bytes 1253384 | tf_op jit(solution)/shard_map/ppermute | solution.py:370
  190.4 38.2 %collective-permute-start.10 = (s16[272,768]{1,0:T(8,128)(2,1)}, s16[272,768]{1,0:T(8,128)(2,1)S(1)}, u32[]{:S(2)}, u32[]{:S(2)}) collective-permute-start(s16[272,768]{1,0:T(8,128)(2,1)} %gate.11.piece), channel_id=1, source_target_pairs={{0,2},{1,3},{2,0},{3,1},{4,6},{5,7},{6,4},{7,5},{8,10},{9,11},{10,... | collective-permute-start | bytes 1253384 | tf_op jit(solution)/shard_map/ppermute | solution.py:370
  193.3 49.0 %collective-permute-start.14 = (bf16[512,768]{1,0:T(8,128)(2,1)}, bf16[512,768]{1,0:T(8,128)(2,1)S(1)}, u32[]{:S(2)}, u32[]{:S(2)}) collective-permute-start(bf16[512,768]{1,0:T(8,128)(2,1)} %copy-done.2), channel_id=1, source_target_pairs={{0,1},{1,0},{2,3},{3,2},{4,5},{5,4},{6,7},{7,6},{8,9},{9,8},{10,11... | collective-permute-start | bytes 2359304 | tf_op jit(solution)/shard_map/ppermute | solution.py:370
  221.6 0.8 copy-start.7
  221.6 22.7 %collective-permute-start.13 = (s16[272,768]{1,0:T(8,128)(2,1)S(1)}, s16[272,768]{1,0:T(8,128)(2,1)S(1)}, u32[]{:S(2)}, u32[]{:S(2)}) collective-permute-start(s16[272,768]{1,0:T(8,128)(2,1)S(1)} %collective-permute-done.12.refs_1_.piece), channel_id=1, source_target_pairs={{0,1},{1,0},{2,3},{3,2},{4,5},{5,4},{6,7},{7,6},{8,9},{9,8},{10,11... | collective-permute-start | bytes 1253384 | tf_op jit(solution)/shard_map/ppermute | solution.py:370
  222.4 6.2 %copy-start.6 = (s16[272,768]{1,0:T(8,128)(2,1)S(1)}, s16[272,768]{1,0:T(8,128)(2,1)}, u32[]{:S(2)}) copy-start(s16[272,768]{1,0:T(8,128)(2,1)} %gate.12.piece) | copy-start | bytes 1253380
  228.6 17.8 %collective-permute-start.11 = (s16[272,768]{1,0:T(8,128)(2,1)S(1)}, s16[272,768]{1,0:T(8,128)(2,1)S(1)}, u32[]{:S(2)}, u32[]{:S(2)}) collective-permute-start(s16[272,768]{1,0:T(8,128)(2,1)S(1)} %collective-permute-done.10.piece), channel_id=1, source_target_pairs={{0,1},{1,0},{2,3},{3,2},{4,5},{5,4},{6,7},{7,6},{8,9},{9,8},{10,11... | collective-permute-start | bytes 1253384 | tf_op jit(solution)/shard_map/ppermute | solution.py:370
  230.0 1.9 copy-start.3
  231.9 2.0 copy-start.8

commit v6 on v5

--- a/solution.py
+++ b/solution.py
@@ -408,10 +408,10 @@
     new_master, new_one, new_two, peak = results
 
     beside = [gate(swap(piece, 1), (), work) for piece, work in zip(ahead, (1<<34, 1024))]
-    step = half
-    while step:
+    step = 1
+    while step < replicas:
         peak = jnp.maximum(peak, swap(peak, step))
-        step //= 2
+        step *= 2
     late = scale(new_master, peak, part, part, beside)
     factor = 1.0 / (peak + peak_eps)
 

time: 252 us -> 250 us (level)
  no operation moved by 1% of the time
where the time goes in v6:
time: 250 us; the launch traced here: 248 us
  waiting for transfers between devices  140 us (56%)
  Pallas kernels  61.5 us (25%)
  starting transfers between devices  31.7 us (13%)
  local copies, waits for them, and re-layouts  8.06 us (3%)
  between operations  3.89 us (2%)
  other arithmetic  3.11 us (1%)
    ppermute x16, waiting for transfers between devices, swap(): return lax.ppermute(x, chain, [(i, i ^ k) for i in range(replicas)])  100 us
    all_to_all x2, waiting for transfers between devices, arrive(): return lax.all_to_all(picked, ('near', 'expert'), 0, 0, tiled=True)  39.8 us
    ppermute x16, starting transfers between devices, swap(): return lax.ppermute(x, chain, [(i, i ^ k) for i in range(replicas)])  23.3 us
    pallas_call x12, Pallas kernels, place(): pl.pallas_call(functools.partial(place_kernel, strips, coded), out_shape=...  20.4 us
    pallas_call x4, Pallas kernels, adam(): pl.pallas_call(functools.partial(adam_kernel, arrays, at, block, size, ah...  17.5 us
    pallas_call x5, Pallas kernels, summed(): pl.pallas_call(functools.partial(kernel, count), out_shape=out_shape, gri...  16.5 us
    all_to_all x2, starting transfers between devices, arrive(): return lax.all_to_all(picked, ('near', 'expert'), 0, 0, tiled=True)  8.41 us
    unnamed x24, local copies, waits for them, and re-layouts  7.98 us
  transfers between devices with their start and end apart: 18, of which 12 were waited for; matrix products, arithmetic and copies ran while one was open for 0% of the time, Pallas kernels for 23%

profile of v6, /device:TPU:0, one launch (start us, length us, event | category | flops | bytes accessed | tf_op | source)
XLA Modules:
  0.0 248.4 jit_solution(11582293422734673651)
XLA Ops:
  2.7 3.1 %collective-permute-start = (bf16[512,768]{1,0:T(8,128)(2,1)S(1)}, bf16[512,768]{1,0:T(8,128)(2,1)}, u32[]{:S(2)}, u32[]{:S(2)}) collective-permute-start(bf16[512,768]{1,0:T(8,128)(2,1)S(1)} %broadcast_select_fusion.refs_3_), channel_id=1, source_target_pairs={{0,1},{1,0},{2,3},{3,2},{4,5},{5,4},{6,7},{7,6},{8,9},{9,8},{10,11... | collective-permute-start | bytes 2359304 | tf_op jit(solution)/shard_map/ppermute | solution.py:370
  6.3 3.1 %pick_columns.3 = bf16[1024,1024]{1,0:T(8,128)(2,1)} custom-call(s32[2]{0:T(128)} %and_select_fusion.table_ref, bf16[512,4096]{1,0:T(8,128)(2,1)} %x_ref.3), custom_call_target="tpu_custom_call" | custom-call | flops 1024 | bytes 1024 | tf_op jit(solution)/shard_map/pick_columns/pallas_call | solution.py:63
  9.4 3.8 %all-to-all-start = ((bf16[16,64,1024]{2,1,0:T(8,128)(2,1)}), bf16[16,64,1024]{2,1,0:T(8,128)(2,1)S(1)}, u32[]{:S(2)}, u32[]{:S(2)}) async-start(bf16[16,64,1024]{2,1,0:T(8,128)(2,1)} %bitcast.31), calls=%async_computation | async-start | bytes 4194304 | tf_op jit(solution)/shard_map/all_to_all | solution.py:380
  13.8 3.1 %pick_columns.2.refs_0_ = bf16[1024,1024]{1,0:T(8,128)(2,1)} custom-call(s32[2]{0:T(128)} %and_select_fusion.1.table_ref, bf16[512,4096]{1,0:T(8,128)(2,1)} %x_ref.3), custom_call_target="tpu_custom_call" | custom-call | flops 1024 | bytes 1024 | tf_op jit(solution)/shard_map/pick_columns/pallas_call | solution.py:63
  16.9 7.4 %collective-permute-done.refs_0_ = bf16[512,768]{1,0:T(8,128)(2,1)} collective-permute-done((bf16[512,768]{1,0:T(8,128)(2,1)S(1)}, bf16[512,768]{1,0:T(8,128)(2,1)}, u32[]{:S(2)}, u32[]{:S(2)}) %collective-permute-start) | collective-permute-done | bytes 786464 | tf_op jit(solution)/shard_map/ppermute | solution.py:370
  24.3 23.7 %all-to-all-done = bf16[16,64,1024]{2,1,0:T(8,128)(2,1)S(1)} async-done(((bf16[16,64,1024]{2,1,0:T(8,128)(2,1)}), bf16[16,64,1024]{2,1,0:T(8,128)(2,1)S(1)}, u32[]{:S(2)}, u32[]{:S(2)}) %all-to-all-start) | async-done | bytes 2097184 | tf_op jit(solution)/shard_map/all_to_all | solution.py:380
  47.9 2.4 coded_sum.4.refs_1_
  51.1 4.6 %all-to-all-start.1 = ((bf16[16,64,1024]{2,1,0:T(8,128)(2,1)}), bf16[16,64,1024]{2,1,0:T(8,128)(2,1)}, u32[]{:S(2)}, u32[]{:S(2)}) async-start(bf16[16,64,1024]{2,1,0:T(8,128)(2,1)} %bitcast.30), calls=%async_computation.1 | async-start | bytes 4194304 | tf_op jit(solution)/shard_map/all_to_all | solution.py:380
  55.6 2.7 %collective-permute-start.4 = (s16[1,272,768]{2,1,0:T(8,128)(2,1)S(1)}, s16[1,272,768]{2,1,0:T(8,128)(2,1)}, u32[]{:S(2)}, u32[]{:S(2)}) collective-permute-start(s16[1,272,768]{2,1,0:T(8,128)(2,1)S(1)} %copy-done.5), channel_id=1, source_target_pairs={{0,2},{1,3},{2,0},{3,1},{4,6},{5,7},{6,4},{7,5},{8,10},{9,11},{10,... | collective-permute-start | bytes 1253384 | tf_op jit(solution)/shard_map/ppermute | solution.py:370
  58.3 3.1 %coded_sum.7 = s16[1,272,768]{2,1,0:T(8,128)(2,1)} custom-call(s32[2]{0:T(128)S(1)} %pad_add_fusion.refs_0_, bf16[1024,1024]{1,0:T(8,128)(2,1)S(1)} %bitcast.22, bf16[1024,1024]{1,0:T(8,128)(2,1)S(1)} %bitcast.23, bf16[512,768]{1,0:T(8,128)(2,1)S(1)} %broadcast_select_fusion.refs_3_, bf16[512,768]{1,0:T(8,128)(2,1)} %gate.7.refs_4_), custom_call_target="tpu_custom_call" | custom-call | flops 1024 | bytes 1024 | tf_op jit(solution)/shard_map/coded_sum/pallas_call | solution.py:145
  61.4 3.1 %coded_sum.6 = s16[1,272,768]{2,1,0:T(8,128)(2,1)} custom-call(s32[2]{0:T(128)S(1)} %pad_add_fusion.refs_0_, bf16[1024,1024]{1,0:T(8,128)(2,1)S(1)} %bitcast.24, bf16[1024,1024]{1,0:T(8,128)(2,1)S(1)} %bitcast.25, bf16[512,768]{1,0:T(8,128)(2,1)S(1)} %broadcast_select_fusion.refs_3_, bf16[512,768]{1,0:T(8,128)(2,1)} %gate.7.refs_4_), custom_call_target="tpu_custom_call" | custom-call | flops 1024 | bytes 1024 | tf_op jit(solution)/shard_map/coded_sum/pallas_call | solution.py:145
  64.5 3.1 %coded_sum.5 = s16[1,272,768]{2,1,0:T(8,128)(2,1)} custom-call(s32[2]{0:T(128)S(1)} %pad_add_fusion.refs_0_, bf16[1024,1024]{1,0:T(8,128)(2,1)S(1)} %bitcast.26, bf16[1024,1024]{1,0:T(8,128)(2,1)S(1)} %bitcast.27, bf16[512,768]{1,0:T(8,128)(2,1)S(1)} %broadcast_select_fusion.refs_3_, bf16[512,768]{1,0:T(8,128)(2,1)} %gate.7.refs_4_), custom_call_target="tpu_custom_call" | custom-call | flops 1024 | bytes 1024 | tf_op jit(solution)/shard_map/coded_sum/pallas_call | solution.py:145
  68.0 2.6 %collective-permute-start.2 = (s16[1,272,768]{2,1,0:T(8,128)(2,1)}, s16[1,272,768]{2,1,0:T(8,128)(2,1)S(1)}, u32[]{:S(2)}, u32[]{:S(2)}) collective-permute-start(s16[1,272,768]{2,1,0:T(8,128)(2,1)} %coded_sum.6), channel_id=1, source_target_pairs={{0,2},{1,3},{2,0},{3,1},{4,6},{5,7},{6,4},{7,5},{8,10},{9,11},{10,... | collective-permute-start | bytes 1253384 | tf_op jit(solution)/shard_map/ppermute | solution.py:370
  70.9 18.6 %collective-permute-done.4.refs_0_ = s16[1,272,768]{2,1,0:T(8,128)(2,1)} collective-permute-done((s16[1,272,768]{2,1,0:T(8,128)(2,1)S(1)}, s16[1,272,768]{2,1,0:T(8,128)(2,1)}, u32[]{:S(2)}, u32[]{:S(2)}) %collective-permute-start.4) | collective-permute-done | bytes 417824 | tf_op jit(solution)/shard_map/ppermute | solution.py:370
  89.5 16.1 %all-to-all-done.1 = bf16[16,64,1024]{2,1,0:T(8,128)(2,1)} async-done(((bf16[16,64,1024]{2,1,0:T(8,128)(2,1)}), bf16[16,64,1024]{2,1,0:T(8,128)(2,1)}, u32[]{:S(2)}, u32[]{:S(2)}) %all-to-all-start.1) | async-done | bytes 2097184 | tf_op jit(solution)/shard_map/all_to_all | solution.py:380
  105.6 4.8 %own_sum.1.refs_0_ = f32[1024,768]{1,0:T(8,128)S(1)} custom-call(s32[2]{0:T(128)S(1)} %pad_add_fusion.refs_0_, bf16[1024,1024]{1,0:T(8,128)(2,1)} %bitcast.5.refs_1_.refs_2_, bf16[1024,1024]{1,0:T(8,128)(2,1)} %bitcast.5.refs_1_.refs_2_, bf16[512,768]{1,0:T(8,128)(2,1)S(1)} %broadcast_select_fusion.refs_3_, bf16[512,768]{1,0:T(8,128)(2,1)} %gate.7.refs_4_), custom_call_target="tpu_custom_call" | custom-call | flops 1024 | bytes 1024 | tf_op jit(solution)/shard_map/own_sum/pallas_call | solution.py:145
  112.1 4.0 %adam.4 = (f32[1024,768]{1,0:T(8,128)}, bf16[1024,768]{1,0:T(8,128)(2,1)}, bf16[1024,768]{1,0:T(8,128)(2,1)}, f32[1]{0:T(128)}, s16[1,272,768]{2,1,0:T(8,128)(2,1)}) custom-call(f32[1024,768]{1,0:T(8,128)} %copy-done, s16[1,272,768]{2,1,0:T(8,128)(2,1)} %gate.9.refs_1_, f32[1024,768]{1,0:T(8,128)} %refs_2_.7, bf16[1024,768]{1,0:T(8,128)(2,1)} %refs_3_.7, ...), custom_call_target="tpu_custom_call" | custom-call | flops 1024 | bytes 1024 | tf_op jit(solution)/shard_map/adam/pallas_call | solution.py:251
  117.0 4.7 %adam.5 = (f32[1024,768]{1,0:T(8,128)}, bf16[1024,768]{1,0:T(8,128)(2,1)}, bf16[1024,768]{1,0:T(8,128)(2,1)}, f32[1]{0:T(128)}, s16[1,272,768]{2,1,0:T(8,128)(2,1)}) custom-call(f32[1024,768]{1,0:T(8,128)} %copy-done, s16[1,272,768]{2,1,0:T(8,128)(2,1)} %copy-done.11, ...), custom_call_target="tpu_custom_call", output_to_operand_aliasing={{0}: (5, {}), {1}: (6, {}), {2}: (7, {})} | custom-call | flops 1024 | bytes 1024 | tf_op jit(solution)/shard_map/adam/pallas_call | solution.py:251
  121.7 4.5 %collective-permute-done.2.refs_1_ = s16[1,272,768]{2,1,0:T(8,128)(2,1)S(1)} collective-permute-done((s16[1,272,768]{2,1,0:T(8,128)(2,1)}, s16[1,272,768]{2,1,0:T(8,128)(2,1)S(1)}, u32[]{:S(2)}, u32[]{:S(2)}) %collective-permute-start.2) | collective-permute-done | bytes 417824 | tf_op jit(solution)/shard_map/ppermute | solution.py:370
  126.9 4.5 %adam.6 = (f32[1024,768]{1,0:T(8,128)}, bf16[1024,768]{1,0:T(8,128)(2,1)}, bf16[1024,768]{1,0:T(8,128)(2,1)}, f32[1]{0:T(128)}) custom-call(f32[1024,768]{1,0:T(8,128)} %copy-done, s16[1,272,768]{2,1,0:T(8,128)(2,1)} %copy-done.10, f32[1024,768]{1,0:T(8,128)} %refs_2_.7, ...), custom_call_target="tpu_custom_call", output_to_operand_aliasing={{0}: (5, {}), {1}: (6, {}), {2}: (7, {})} | custom-call | flops 1024 | bytes 1024 | tf_op jit(solution)/shard_map/adam/pallas_call | solution.py:251
  131.4 2.8 %collective-permute-done.1.refs_1_ = s16[1,272,768]{2,1,0:T(8,128)(2,1)S(1)} collective-permute-done((s16[1,272,768]{2,1,0:T(8,128)(2,1)}, s16[1,272,768]{2,1,0:T(8,128)(2,1)S(1)}, u32[]{:S(2)}, u32[]{:S(2)}) %collective-permute-start.1) | collective-permute-done | bytes 417824 | tf_op jit(solution)/shard_map/ppermute | solution.py:370
  134.9 4.4 %adam.7 = (f32[1024,768]{1,0:T(8,128)}, bf16[1024,768]{1,0:T(8,128)(2,1)}, bf16[1024,768]{1,0:T(8,128)(2,1)}, f32[1]{0:T(128)}) custom-call(f32[1024,768]{1,0:T(8,128)} %copy-done, s16[1,272,768]{2,1,0:T(8,128)(2,1)} %copy-done.9, f32[1024,768]{1,0:T(8,128)} %refs_2_.7, ...), custom_call_target="tpu_custom_call", output_to_operand_aliasing={{0}: (5, {}), {1}: (6, {}), {2}: (7, {})} | custom-call | flops 1024 | bytes 1024 | tf_op jit(solution)/shard_map/adam/pallas_call | solution.py:251
  139.4 2.0 collective-permute-start.8
  144.5 5.1 %collective-permute-start.6 = (f32[1]{0:T(128)}, f32[1]{0:T(128)}, u32[]{:S(2)}, u32[]{:S(2)}) collective-permute-start(f32[1]{0:T(128)} %max.6), channel_id=1, source_target_pairs={{0,2},{1,3},{2,0},{3,1},{4,6},{5,7},{6,4},{7,5},{8,10},{9,11},{10,... | collective-permute-start | bytes 20 | tf_op jit(solution)/shard_map/ppermute | solution.py:370
  153.0 3.4 %collective-permute-start.9 = (bf16[512,768]{1,0:T(8,128)(2,1)}, bf16[512,768]{1,0:T(8,128)(2,1)S(1)}, u32[]{:S(2)}, u32[]{:S(2)}) collective-permute-start(bf16[512,768]{1,0:T(8,128)(2,1)} %scale.1.refs_0_), channel_id=1, source_target_pairs={{0,2},{1,3},{2,0},{3,1},{4,6},{5,7},{6,4},{7,5},{8,10},{9,11},{10,... | collective-permute-start | bytes 2359304 | tf_op jit(solution)/shard_map/ppermute | solution.py:370
  156.4 32.3 %collective-permute-done.9.refs_1_.piece = bf16[512,768]{1,0:T(8,128)(2,1)S(1)} collective-permute-done((bf16[512,768]{1,0:T(8,128)(2,1)}, bf16[512,768]{1,0:T(8,128)(2,1)S(1)}, u32[]{:S(2)}, u32[]{:S(2)}) %collective-permute-start.9) | collective-permute-done | bytes 786464 | tf_op jit(solution)/shard_map/ppermute | solution.py:370
  189.6 2.9 %collective-permute-start.10 = (s16[272,768]{1,0:T(8,128)(2,1)}, s16[272,768]{1,0:T(8,128)(2,1)S(1)}, u32[]{:S(2)}, u32[]{:S(2)}) collective-permute-start(s16[272,768]{1,0:T(8,128)(2,1)} %gate.11.piece), channel_id=1, source_target_pairs={{0,2},{1,3},{2,0},{3,1},{4,6},{5,7},{6,4},{7,5},{8,10},{9,11},{10,... | collective-permute-start | bytes 1253384 | tf_op jit(solution)/shard_map/ppermute | solution.py:370
  193.3 26.9 %collective-permute-done.12.refs_1_.piece = s16[272,768]{1,0:T(8,128)(2,1)S(1)} collective-permute-done((s16[272,768]{1,0:T(8,128)(2,1)}, s16[272,768]{1,0:T(8,128)(2,1)S(1)}, u32[]{:S(2)}, u32[]{:S(2)}) %collective-permute-start.12) | collective-permute-done | bytes 417824 | tf_op jit(solution)/shard_map/ppermute | solution.py:370
  221.0 2.0 place.12.refs_0_
  223.0 5.0 %collective-permute-done.10.piece = s16[272,768]{1,0:T(8,128)(2,1)S(1)} collective-permute-done((s16[272,768]{1,0:T(8,128)(2,1)}, s16[272,768]{1,0:T(8,128)(2,1)S(1)}, u32[]{:S(2)}, u32[]{:S(2)}) %collective-permute-start.10) | collective-permute-done | bytes 417824 | tf_op jit(solution)/shard_map/ppermute | solution.py:370
  231.4 2.0 place.15.refs_0_
  236.2 2.0 place.18.refs_0_
  (65 shorter events, 31.0 us)
Async XLA Ops:
  2.7 21.6 %collective-permute-start = (bf16[512,768]{1,0:T(8,128)(2,1)S(1)}, bf16[512,768]{1,0:T(8,128)(2,1)}, u32[]{:S(2)}, u32[]{:S(2)}) collective-permute-start(bf16[512,768]{1,0:T(8,128)(2,1)S(1)} %broadcast_select_fusion.refs_3_), channel_id=1, source_target_pairs={{0,1},{1,0},{2,3},{3,2},{4,5},{5,4},{6,7},{7,6},{8,9},{9,8},{10,11... | collective-permute-start | bytes 2359304 | tf_op jit(solution)/shard_map/ppermute | solution.py:370
  9.4 38.5 %all-to-all-start = ((bf16[16,64,1024]{2,1,0:T(8,128)(2,1)}), bf16[16,64,1024]{2,1,0:T(8,128)(2,1)S(1)}, u32[]{:S(2)}, u32[]{:S(2)}) async-start(bf16[16,64,1024]{2,1,0:T(8,128)(2,1)} %bitcast.31), calls=%async_computation | async-start | bytes 4194304 | tf_op jit(solution)/shard_map/all_to_all | solution.py:380
  50.3 0.8 copy-start.4
  51.1 4.6 %copy-start.5 = (s16[1,272,768]{2,1,0:T(8,128)(2,1)S(1)}, s16[1,272,768]{2,1,0:T(8,128)(2,1)}, u32[]{:S(2)}) copy-start(s16[1,272,768]{2,1,0:T(8,128)(2,1)} %copy-done.4) | copy-start | bytes 1253380
  51.1 54.6 %all-to-all-start.1 = ((bf16[16,64,1024]{2,1,0:T(8,128)(2,1)}), bf16[16,64,1024]{2,1,0:T(8,128)(2,1)}, u32[]{:S(2)}, u32[]{:S(2)}) async-start(bf16[16,64,1024]{2,1,0:T(8,128)(2,1)} %bitcast.30), calls=%async_computation.1 | async-start | bytes 4194304 | tf_op jit(solution)/shard_map/all_to_all | solution.py:380
  55.6 33.9 %collective-permute-start.4 = (s16[1,272,768]{2,1,0:T(8,128)(2,1)S(1)}, s16[1,272,768]{2,1,0:T(8,128)(2,1)}, u32[]{:S(2)}, u32[]{:S(2)}) collective-permute-start(s16[1,272,768]{2,1,0:T(8,128)(2,1)S(1)} %copy-done.5), channel_id=1, source_target_pairs={{0,2},{1,3},{2,0},{3,1},{4,6},{5,7},{6,4},{7,5},{8,10},{9,11},{10,... | collective-permute-start | bytes 1253384 | tf_op jit(solution)/shard_map/ppermute | solution.py:370
  67.7 48.5 %collective-permute-start.3 = (s16[1,272,768]{2,1,0:T(8,128)(2,1)}, s16[1,272,768]{2,1,0:T(8,128)(2,1)S(1)}, u32[]{:S(2)}, u32[]{:S(2)}) collective-permute-start(s16[1,272,768]{2,1,0:T(8,128)(2,1)} %coded_sum.7), channel_id=1, source_target_pairs={{0,2},{1,3},{2,0},{3,1},{4,6},{5,7},{6,4},{7,5},{8,10},{9,11},{10,... | collective-permute-start | bytes 1253384 | tf_op jit(solution)/shard_map/ppermute | solution.py:370
  68.0 58.2 %collective-permute-start.2 = (s16[1,272,768]{2,1,0:T(8,128)(2,1)}, s16[1,272,768]{2,1,0:T(8,128)(2,1)S(1)}, u32[]{:S(2)}, u32[]{:S(2)}) collective-permute-start(s16[1,272,768]{2,1,0:T(8,128)(2,1)} %coded_sum.6), channel_id=1, source_target_pairs={{0,2},{1,3},{2,0},{3,1},{4,6},{5,7},{6,4},{7,5},{8,10},{9,11},{10,... | collective-permute-start | bytes 1253384 | tf_op jit(solution)/shard_map/ppermute | solution.py:370
  70.6 63.5 %collective-permute-start.1 = (s16[1,272,768]{2,1,0:T(8,128)(2,1)}, s16[1,272,768]{2,1,0:T(8,128)(2,1)S(1)}, u32[]{:S(2)}, u32[]{:S(2)}) collective-permute-start(s16[1,272,768]{2,1,0:T(8,128)(2,1)} %coded_sum.5), channel_id=1, source_target_pairs={{0,2},{1,3},{2,0},{3,1},{4,6},{5,7},{6,4},{7,5},{8,10},{9,11},{10,... | collective-permute-start | bytes 1253384 | tf_op jit(solution)/shard_map/ppermute | solution.py:370
  110.4 1.7 copy-start
  116.1 34.1 %collective-permute-start.7 = (s16[272,768]{1,0:T(8,128)(2,1)}, s16[272,768]{1,0:T(8,128)(2,1)}, u32[]{:S(2)}, u32[]{:S(2)}) collective-permute-start(s16[272,768]{1,0:T(8,128)(2,1)} %bitcast.28), channel_id=1, source_target_pairs={{0,1},{1,0},{2,3},{3,2},{4,5},{5,4},{6,7},{7,6},{8,9},{9,8},{10,11... | collective-permute-start | bytes 1253384 | tf_op jit(solution)/shard_map/ppermute | solution.py:370
  116.2 0.8 copy-start.11
  126.2 0.8 copy-start.10
  134.1 0.8 copy-start.9
  139.3 4.0 %collective-permute-start.5 = (f32[1]{0:T(128)}, f32[1]{0:T(128)}, u32[]{:S(2)}, u32[]{:S(2)}) collective-permute-start(f32[1]{0:T(128)} %get-tuple-element.38), channel_id=1, source_target_pairs={{0,1},{1,0},{2,3},{3,2},{4,5},{5,4},{6,7},{7,6},{8,9},{9,8},{10,11... | collective-permute-start | bytes 20 | tf_op jit(solution)/shard_map/ppermute | solution.py:370
  139.4 11.0 %collective-permute-start.8 = (s16[272,768]{1,0:T(8,128)(2,1)}, s16[272,768]{1,0:T(8,128)(2,1)}, u32[]{:S(2)}, u32[]{:S(2)}) collective-permute-start(s16[272,768]{1,0:T(8,128)(2,1)} %bitcast.7.refs_0_), channel_id=1, source_target_pairs={{0,1},{1,0},{2,3},{3,2},{4,5},{5,4},{6,7},{7,6},{8,9},{9,8},{10,11... | collective-permute-start | bytes 1253384 | tf_op jit(solution)/shard_map/ppermute | solution.py:370
  144.5 5.1 %collective-permute-start.6 = (f32[1]{0:T(128)}, f32[1]{0:T(128)}, u32[]{:S(2)}, u32[]{:S(2)}) collective-permute-start(f32[1]{0:T(128)} %max.6), channel_id=1, source_target_pairs={{0,2},{1,3},{2,0},{3,1},{4,6},{5,7},{6,4},{7,5},{8,10},{9,11},{10,... | collective-permute-start | bytes 20 | tf_op jit(solution)/shard_map/ppermute | solution.py:370
  150.2 1.9 copy-start.1
  153.0 35.7 %collective-permute-start.9 = (bf16[512,768]{1,0:T(8,128)(2,1)}, bf16[512,768]{1,0:T(8,128)(2,1)S(1)}, u32[]{:S(2)}, u32[]{:S(2)}) collective-permute-start(bf16[512,768]{1,0:T(8,128)(2,1)} %scale.1.refs_0_), channel_id=1, source_target_pairs={{0,2},{1,3},{2,0},{3,1},{4,6},{5,7},{6,4},{7,5},{8,10},{9,11},{10,... | collective-permute-start | bytes 2359304 | tf_op jit(solution)/shard_map/ppermute | solution.py:370
  156.4 63.9 %collective-permute-start.15 = (bf16[512,768]{1,0:T(8,128)(2,1)}, bf16[512,768]{1,0:T(8,128)(2,1)S(1)}, u32[]{:S(2)}, u32[]{:S(2)}) collective-permute-start(bf16[512,768]{1,0:T(8,128)(2,1)} %scale.1.refs_0_), channel_id=1, source_target_pairs={{0,1},{1,0},{2,3},{3,2},{4,5},{5,4},{6,7},{7,6},{8,9},{9,8},{10,11... | collective-permute-start | bytes 2359304 | tf_op jit(solution)/shard_map/ppermute | solution.py:370
  188.7 0.9 copy-start.2
  189.6 30.7 %collective-permute-start.12 = (s16[272,768]{1,0:T(8,128)(2,1)}, s16[272,768]{1,0:T(8,128)(2,1)S(1)}, u32[]{:S(2)}, u32[]{:S(2)}) collective-permute-start(s16[272,768]{1,0:T(8,128)(2,1)} %gate.12.piece), channel_id=1, source_target_pairs={{0,2},{1,3},{2,0},{3,1},{4,6},{5,7},{6,4},{7,5},{8,10},{9,11},{10,... | collective-permute-start | bytes 1253384 | tf_op jit(solution)/shard_map/ppermute | solution.py:370
  189.6 38.5 %collective-permute-start.10 = (s16[272,768]{1,0:T(8,128)(2,1)}, s16[272,768]{1,0:T(8,128)(2,1)S(1)}, u32[]{:S(2)}, u32[]{:S(2)}) collective-permute-start(s16[272,768]{1,0:T(8,128)(2,1)} %gate.11.piece), channel_id=1, source_target_pairs={{0,2},{1,3},{2,0},{3,1},{4,6},{5,7},{6,4},{7,5},{8,10},{9,11},{10,... | collective-permute-start | bytes 1253384 | tf_op jit(solution)/shard_map/ppermute | solution.py:370
  192.5 49.3 %collective-permute-start.14 = (bf16[512,768]{1,0:T(8,128)(2,1)}, bf16[512,768]{1,0:T(8,128)(2,1)S(1)}, u32[]{:S(2)}, u32[]{:S(2)}) collective-permute-start(bf16[512,768]{1,0:T(8,128)(2,1)} %copy-done.2), channel_id=1, source_target_pairs={{0,1},{1,0},{2,3},{3,2},{4,5},{5,4},{6,7},{7,6},{8,9},{9,8},{10,11... | collective-permute-start | bytes 2359304 | tf_op jit(solution)/shard_map/ppermute | solution.py:370
  220.3 0.8 copy-start.7
  220.3 23.5 %collective-permute-start.13 = (s16[272,768]{1,0:T(8,128)(2,1)S(1)}, s16[272,768]{1,0:T(8,128)(2,1)S(1)}, u32[]{:S(2)}, u32[]{:S(2)}) collective-permute-start(s16[272,768]{1,0:T(8,128)(2,1)S(1)} %collective-permute-done.12.refs_1_.piece), channel_id=1, source_target_pairs={{0,1},{1,0},{2,3},{3,2},{4,5},{5,4},{6,7},{7,6},{8,9},{9,8},{10,11... | collective-permute-start | bytes 1253384 | tf_op jit(solution)/shard_map/ppermute | solution.py:370
  221.0 7.0 %copy-start.6 = (s16[272,768]{1,0:T(8,128)(2,1)S(1)}, s16[272,768]{1,0:T(8,128)(2,1)}, u32[]{:S(2)}) copy-start(s16[272,768]{1,0:T(8,128)(2,1)} %gate.12.piece) | copy-start | bytes 1253380
  228.0 17.8 %collective-permute-start.11 = (s16[272,768]{1,0:T(8,128)(2,1)S(1)}, s16[272,768]{1,0:T(8,128)(2,1)S(1)}, u32[]{:S(2)}, u32[]{:S(2)}) collective-permute-start(s16[272,768]{1,0:T(8,128)(2,1)S(1)} %collective-permute-done.10.piece), channel_id=1, source_target_pairs={{0,1},{1,0},{2,3},{3,2},{4,5},{5,4},{6,7},{7,6},{8,9},{9,8},{10,11... | collective-permute-start | bytes 1253384 | tf_op jit(solution)/shard_map/ppermute | solution.py:370
  229.5 1.9 copy-start.3
  231.4 2.0 copy-start.8

commit v7 on v6

--- a/solution.py
+++ b/solution.py
@@ -241,7 +241,7 @@
 
 def adam(own, coded, master, one, two, at, block, ahead, earlier=()):
     shard, ffn = master.shape
-    size = min(128, block)
+    size = min(64, block)
     width = coded.shape[0] * block
     steps = width // size
     anywhere = pl.BlockSpec(memory_space=pl.ANY)

time: 250 us -> 250 us (level)
  no operation moved by 1% of the time
where the time goes in v7:
time: 250 us; the launch traced here: 248 us
  waiting for transfers between devices  140 us (56%)
  Pallas kernels  61.4 us (25%)
  starting transfers between devices  31.8 us (13%)
  local copies, waits for them, and re-layouts  8.06 us (3%)
  between operations  3.89 us (2%)
  other arithmetic  3.11 us (1%)
    ppermute x16, waiting for transfers between devices, swap(): return lax.ppermute(x, chain, [(i, i ^ k) for i in range(replicas)])  100 us
    all_to_all x2, waiting for transfers between devices, arrive(): return lax.all_to_all(picked, ('near', 'expert'), 0, 0, tiled=True)  39.8 us
    ppermute x16, starting transfers between devices, swap(): return lax.ppermute(x, chain, [(i, i ^ k) for i in range(replicas)])  23.4 us
    pallas_call x12, Pallas kernels, place(): pl.pallas_call(functools.partial(place_kernel, strips, coded), out_shape=...  20.4 us
    pallas_call x4, Pallas kernels, adam(): pl.pallas_call(functools.partial(adam_kernel, arrays, at, block, size, ah...  17.4 us
    pallas_call x5, Pallas kernels, summed(): pl.pallas_call(functools.partial(kernel, count), out_shape=out_shape, gri...  16.5 us
    all_to_all x2, starting transfers between devices, arrive(): return lax.all_to_all(picked, ('near', 'expert'), 0, 0, tiled=True)  8.41 us
    unnamed x24, local copies, waits for them, and re-layouts  7.98 us
  transfers between devices with their start and end apart: 18, of which 12 were waited for; matrix products, arithmetic and copies ran while one was open for 0% of the time, Pallas kernels for 23%

profile of v7, /device:TPU:0, one launch (start us, length us, event | category | flops | bytes accessed | tf_op | source)
XLA Modules:
  0.0 248.3 jit_solution(17804392845748280603)
XLA Ops:
  2.7 3.1 %collective-permute-start = (bf16[512,768]{1,0:T(8,128)(2,1)S(1)}, bf16[512,768]{1,0:T(8,128)(2,1)}, u32[]{:S(2)}, u32[]{:S(2)}) collective-permute-start(bf16[512,768]{1,0:T(8,128)(2,1)S(1)} %broadcast_select_fusion.refs_3_), channel_id=1, source_target_pairs={{0,1},{1,0},{2,3},{3,2},{4,5},{5,4},{6,7},{7,6},{8,9},{9,8},{10,11... | collective-permute-start | bytes 2359304 | tf_op jit(solution)/shard_map/ppermute | solution.py:370
  6.3 3.1 %pick_columns.3 = bf16[1024,1024]{1,0:T(8,128)(2,1)} custom-call(s32[2]{0:T(128)} %and_select_fusion.table_ref, bf16[512,4096]{1,0:T(8,128)(2,1)} %x_ref.3), custom_call_target="tpu_custom_call" | custom-call | flops 1024 | bytes 1024 | tf_op jit(solution)/shard_map/pick_columns/pallas_call | solution.py:63
  9.4 3.8 %all-to-all-start = ((bf16[16,64,1024]{2,1,0:T(8,128)(2,1)}), bf16[16,64,1024]{2,1,0:T(8,128)(2,1)S(1)}, u32[]{:S(2)}, u32[]{:S(2)}) async-start(bf16[16,64,1024]{2,1,0:T(8,128)(2,1)} %bitcast.31), calls=%async_computation | async-start | bytes 4194304 | tf_op jit(solution)/shard_map/all_to_all | solution.py:380
  13.8 3.1 %pick_columns.2.refs_0_ = bf16[1024,1024]{1,0:T(8,128)(2,1)} custom-call(s32[2]{0:T(128)} %and_select_fusion.1.table_ref, bf16[512,4096]{1,0:T(8,128)(2,1)} %x_ref.3), custom_call_target="tpu_custom_call" | custom-call | flops 1024 | bytes 1024 | tf_op jit(solution)/shard_map/pick_columns/pallas_call | solution.py:63
  16.9 7.4 %collective-permute-done.refs_0_ = bf16[512,768]{1,0:T(8,128)(2,1)} collective-permute-done((bf16[512,768]{1,0:T(8,128)(2,1)S(1)}, bf16[512,768]{1,0:T(8,128)(2,1)}, u32[]{:S(2)}, u32[]{:S(2)}) %collective-permute-start) | collective-permute-done | bytes 786464 | tf_op jit(solution)/shard_map/ppermute | solution.py:370
  24.3 23.7 %all-to-all-done = bf16[16,64,1024]{2,1,0:T(8,128)(2,1)S(1)} async-done(((bf16[16,64,1024]{2,1,0:T(8,128)(2,1)}), bf16[16,64,1024]{2,1,0:T(8,128)(2,1)S(1)}, u32[]{:S(2)}, u32[]{:S(2)}) %all-to-all-start) | async-done | bytes 2097184 | tf_op jit(solution)/shard_map/all_to_all | solution.py:380
  47.9 2.4 coded_sum.4.refs_1_
  51.1 4.6 %all-to-all-start.1 = ((bf16[16,64,1024]{2,1,0:T(8,128)(2,1)}), bf16[16,64,1024]{2,1,0:T(8,128)(2,1)}, u32[]{:S(2)}, u32[]{:S(2)}) async-start(bf16[16,64,1024]{2,1,0:T(8,128)(2,1)} %bitcast.30), calls=%async_computation.1 | async-start | bytes 4194304 | tf_op jit(solution)/shard_map/all_to_all | solution.py:380
  55.6 2.7 %collective-permute-start.4 = (s16[1,272,768]{2,1,0:T(8,128)(2,1)S(1)}, s16[1,272,768]{2,1,0:T(8,128)(2,1)}, u32[]{:S(2)}, u32[]{:S(2)}) collective-permute-start(s16[1,272,768]{2,1,0:T(8,128)(2,1)S(1)} %copy-done.5), channel_id=1, source_target_pairs={{0,2},{1,3},{2,0},{3,1},{4,6},{5,7},{6,4},{7,5},{8,10},{9,11},{10,... | collective-permute-start | bytes 1253384 | tf_op jit(solution)/shard_map/ppermute | solution.py:370
  58.3 3.1 %coded_sum.7 = s16[1,272,768]{2,1,0:T(8,128)(2,1)} custom-call(s32[2]{0:T(128)S(1)} %pad_add_fusion.refs_0_, bf16[1024,1024]{1,0:T(8,128)(2,1)S(1)} %bitcast.22, bf16[1024,1024]{1,0:T(8,128)(2,1)S(1)} %bitcast.23, bf16[512,768]{1,0:T(8,128)(2,1)S(1)} %broadcast_select_fusion.refs_3_, bf16[512,768]{1,0:T(8,128)(2,1)} %gate.7.refs_4_), custom_call_target="tpu_custom_call" | custom-call | flops 1024 | bytes 1024 | tf_op jit(solution)/shard_map/coded_sum/pallas_call | solution.py:145
  61.4 3.1 %coded_sum.6 = s16[1,272,768]{2,1,0:T(8,128)(2,1)} custom-call(s32[2]{0:T(128)S(1)} %pad_add_fusion.refs_0_, bf16[1024,1024]{1,0:T(8,128)(2,1)S(1)} %bitcast.24, bf16[1024,1024]{1,0:T(8,128)(2,1)S(1)} %bitcast.25, bf16[512,768]{1,0:T(8,128)(2,1)S(1)} %broadcast_select_fusion.refs_3_, bf16[512,768]{1,0:T(8,128)(2,1)} %gate.7.refs_4_), custom_call_target="tpu_custom_call" | custom-call | flops 1024 | bytes 1024 | tf_op jit(solution)/shard_map/coded_sum/pallas_call | solution.py:145
  64.5 3.1 %coded_sum.5 = s16[1,272,768]{2,1,0:T(8,128)(2,1)} custom-call(s32[2]{0:T(128)S(1)} %pad_add_fusion.refs_0_, bf16[1024,1024]{1,0:T(8,128)(2,1)S(1)} %bitcast.26, bf16[1024,1024]{1,0:T(8,128)(2,1)S(1)} %bitcast.27, bf16[512,768]{1,0:T(8,128)(2,1)S(1)} %broadcast_select_fusion.refs_3_, bf16[512,768]{1,0:T(8,128)(2,1)} %gate.7.refs_4_), custom_call_target="tpu_custom_call" | custom-call | flops 1024 | bytes 1024 | tf_op jit(solution)/shard_map/coded_sum/pallas_call | solution.py:145
  68.0 2.6 %collective-permute-start.2 = (s16[1,272,768]{2,1,0:T(8,128)(2,1)}, s16[1,272,768]{2,1,0:T(8,128)(2,1)S(1)}, u32[]{:S(2)}, u32[]{:S(2)}) collective-permute-start(s16[1,272,768]{2,1,0:T(8,128)(2,1)} %coded_sum.6), channel_id=1, source_target_pairs={{0,2},{1,3},{2,0},{3,1},{4,6},{5,7},{6,4},{7,5},{8,10},{9,11},{10,... | collective-permute-start | bytes 1253384 | tf_op jit(solution)/shard_map/ppermute | solution.py:370
  70.9 18.6 %collective-permute-done.4.refs_0_ = s16[1,272,768]{2,1,0:T(8,128)(2,1)} collective-permute-done((s16[1,272,768]{2,1,0:T(8,128)(2,1)S(1)}, s16[1,272,768]{2,1,0:T(8,128)(2,1)}, u32[]{:S(2)}, u32[]{:S(2)}) %collective-permute-start.4) | collective-permute-done | bytes 417824 | tf_op jit(solution)/shard_map/ppermute | solution.py:370
  89.5 16.1 %all-to-all-done.1 = bf16[16,64,1024]{2,1,0:T(8,128)(2,1)} async-done(((bf16[16,64,1024]{2,1,0:T(8,128)(2,1)}), bf16[16,64,1024]{2,1,0:T(8,128)(2,1)}, u32[]{:S(2)}, u32[]{:S(2)}) %all-to-all-start.1) | async-done | bytes 2097184 | tf_op jit(solution)/shard_map/all_to_all | solution.py:380
  105.6 4.8 %own_sum.1.refs_0_ = f32[1024,768]{1,0:T(8,128)S(1)} custom-call(s32[2]{0:T(128)S(1)} %pad_add_fusion.refs_0_, bf16[1024,1024]{1,0:T(8,128)(2,1)} %bitcast.5.refs_1_.refs_2_, bf16[1024,1024]{1,0:T(8,128)(2,1)} %bitcast.5.refs_1_.refs_2_, bf16[512,768]{1,0:T(8,128)(2,1)S(1)} %broadcast_select_fusion.refs_3_, bf16[512,768]{1,0:T(8,128)(2,1)} %gate.7.refs_4_), custom_call_target="tpu_custom_call" | custom-call | flops 1024 | bytes 1024 | tf_op jit(solution)/shard_map/own_sum/pallas_call | solution.py:145
  112.1 4.0 %adam.4 = (f32[1024,768]{1,0:T(8,128)}, bf16[1024,768]{1,0:T(8,128)(2,1)}, bf16[1024,768]{1,0:T(8,128)(2,1)}, f32[1]{0:T(128)}, s16[1,272,768]{2,1,0:T(8,128)(2,1)}) custom-call(f32[1024,768]{1,0:T(8,128)} %copy-done, s16[1,272,768]{2,1,0:T(8,128)(2,1)} %gate.9.refs_1_, f32[1024,768]{1,0:T(8,128)} %refs_2_.7, bf16[1024,768]{1,0:T(8,128)(2,1)} %refs_3_.7, ...), custom_call_target="tpu_custom_call" | custom-call | flops 1024 | bytes 1024 | tf_op jit(solution)/shard_map/adam/pallas_call | solution.py:251
  116.9 4.6 %adam.5 = (f32[1024,768]{1,0:T(8,128)}, bf16[1024,768]{1,0:T(8,128)(2,1)}, bf16[1024,768]{1,0:T(8,128)(2,1)}, f32[1]{0:T(128)}, s16[1,272,768]{2,1,0:T(8,128)(2,1)}) custom-call(f32[1024,768]{1,0:T(8,128)} %copy-done, s16[1,272,768]{2,1,0:T(8,128)(2,1)} %copy-done.11, ...), custom_call_target="tpu_custom_call", output_to_operand_aliasing={{0}: (5, {}), {1}: (6, {}), {2}: (7, {})} | custom-call | flops 1024 | bytes 1024 | tf_op jit(solution)/shard_map/adam/pallas_call | solution.py:251
  121.6 4.6 %collective-permute-done.2.refs_1_ = s16[1,272,768]{2,1,0:T(8,128)(2,1)S(1)} collective-permute-done((s16[1,272,768]{2,1,0:T(8,128)(2,1)}, s16[1,272,768]{2,1,0:T(8,128)(2,1)S(1)}, u32[]{:S(2)}, u32[]{:S(2)}) %collective-permute-start.2) | collective-permute-done | bytes 417824 | tf_op jit(solution)/shard_map/ppermute | solution.py:370
  126.9 4.4 %adam.6 = (f32[1024,768]{1,0:T(8,128)}, bf16[1024,768]{1,0:T(8,128)(2,1)}, bf16[1024,768]{1,0:T(8,128)(2,1)}, f32[1]{0:T(128)}) custom-call(f32[1024,768]{1,0:T(8,128)} %copy-done, s16[1,272,768]{2,1,0:T(8,128)(2,1)} %copy-done.10, f32[1024,768]{1,0:T(8,128)} %refs_2_.7, ...), custom_call_target="tpu_custom_call", output_to_operand_aliasing={{0}: (5, {}), {1}: (6, {}), {2}: (7, {})} | custom-call | flops 1024 | bytes 1024 | tf_op jit(solution)/shard_map/adam/pallas_call | solution.py:251
  131.3 2.8 %collective-permute-done.1.refs_1_ = s16[1,272,768]{2,1,0:T(8,128)(2,1)S(1)} collective-permute-done((s16[1,272,768]{2,1,0:T(8,128)(2,1)}, s16[1,272,768]{2,1,0:T(8,128)(2,1)S(1)}, u32[]{:S(2)}, u32[]{:S(2)}) %collective-permute-start.1) | collective-permute-done | bytes 417824 | tf_op jit(solution)/shard_map/ppermute | solution.py:370
  134.9 4.4 %adam.7 = (f32[1024,768]{1,0:T(8,128)}, bf16[1024,768]{1,0:T(8,128)(2,1)}, bf16[1024,768]{1,0:T(8,128)(2,1)}, f32[1]{0:T(128)}) custom-call(f32[1024,768]{1,0:T(8,128)} %copy-done, s16[1,272,768]{2,1,0:T(8,128)(2,1)} %copy-done.9, f32[1024,768]{1,0:T(8,128)} %refs_2_.7, ...), custom_call_target="tpu_custom_call", output_to_operand_aliasing={{0}: (5, {}), {1}: (6, {}), {2}: (7, {})} | custom-call | flops 1024 | bytes 1024 | tf_op jit(solution)/shard_map/adam/pallas_call | solution.py:251
  139.4 2.0 collective-permute-start.8
  144.5 5.1 %collective-permute-start.6 = (f32[1]{0:T(128)}, f32[1]{0:T(128)}, u32[]{:S(2)}, u32[]{:S(2)}) collective-permute-start(f32[1]{0:T(128)} %max.6), channel_id=1, source_target_pairs={{0,2},{1,3},{2,0},{3,1},{4,6},{5,7},{6,4},{7,5},{8,10},{9,11},{10,... | collective-permute-start | bytes 20 | tf_op jit(solution)/shard_map/ppermute | solution.py:370
  153.0 3.4 %collective-permute-start.9 = (bf16[512,768]{1,0:T(8,128)(2,1)}, bf16[512,768]{1,0:T(8,128)(2,1)S(1)}, u32[]{:S(2)}, u32[]{:S(2)}) collective-permute-start(bf16[512,768]{1,0:T(8,128)(2,1)} %scale.1.refs_0_), channel_id=1, source_target_pairs={{0,2},{1,3},{2,0},{3,1},{4,6},{5,7},{6,4},{7,5},{8,10},{9,11},{10,... | collective-permute-start | bytes 2359304 | tf_op jit(solution)/shard_map/ppermute | solution.py:370
  156.3 32.3 %collective-permute-done.9.refs_1_.piece = bf16[512,768]{1,0:T(8,128)(2,1)S(1)} collective-permute-done((bf16[512,768]{1,0:T(8,128)(2,1)}, bf16[512,768]{1,0:T(8,128)(2,1)S(1)}, u32[]{:S(2)}, u32[]{:S(2)}) %collective-permute-start.9) | collective-permute-done | bytes 786464 | tf_op jit(solution)/shard_map/ppermute | solution.py:370
  189.5 2.9 %collective-permute-start.10 = (s16[272,768]{1,0:T(8,128)(2,1)}, s16[272,768]{1,0:T(8,128)(2,1)S(1)}, u32[]{:S(2)}, u32[]{:S(2)}) collective-permute-start(s16[272,768]{1,0:T(8,128)(2,1)} %gate.11.piece), channel_id=1, source_target_pairs={{0,2},{1,3},{2,0},{3,1},{4,6},{5,7},{6,4},{7,5},{8,10},{9,11},{10,... | collective-permute-start | bytes 1253384 | tf_op jit(solution)/shard_map/ppermute | solution.py:370
  193.4 27.0 %collective-permute-done.12.refs_1_.piece = s16[272,768]{1,0:T(8,128)(2,1)S(1)} collective-permute-done((s16[272,768]{1,0:T(8,128)(2,1)}, s16[272,768]{1,0:T(8,128)(2,1)S(1)}, u32[]{:S(2)}, u32[]{:S(2)}) %collective-permute-start.12) | collective-permute-done | bytes 417824 | tf_op jit(solution)/shard_map/ppermute | solution.py:370
  221.2 2.0 place.12.refs_0_
  223.2 4.8 %collective-permute-done.10.piece = s16[272,768]{1,0:T(8,128)(2,1)S(1)} collective-permute-done((s16[272,768]{1,0:T(8,128)(2,1)}, s16[272,768]{1,0:T(8,128)(2,1)S(1)}, u32[]{:S(2)}, u32[]{:S(2)}) %collective-permute-start.10) | collective-permute-done | bytes 417824 | tf_op jit(solution)/shard_map/ppermute | solution.py:370
  231.3 2.0 place.15.refs_0_
  236.2 2.0 place.18.refs_0_
  (65 shorter events, 31.1 us)
Async XLA Ops:
  2.7 21.6 %collective-permute-start = (bf16[512,768]{1,0:T(8,128)(2,1)S(1)}, bf16[512,768]{1,0:T(8,128)(2,1)}, u32[]{:S(2)}, u32[]{:S(2)}) collective-permute-start(bf16[512,768]{1,0:T(8,128)(2,1)S(1)} %broadcast_select_fusion.refs_3_), channel_id=1, source_target_pairs={{0,1},{1,0},{2,3},{3,2},{4,5},{5,4},{6,7},{7,6},{8,9},{9,8},{10,11... | collective-permute-start | bytes 2359304 | tf_op jit(solution)/shard_map/ppermute | solution.py:370
  9.4 38.5 %all-to-all-start = ((bf16[16,64,1024]{2,1,0:T(8,128)(2,1)}), bf16[16,64,1024]{2,1,0:T(8,128)(2,1)S(1)}, u32[]{:S(2)}, u32[]{:S(2)}) async-start(bf16[16,64,1024]{2,1,0:T(8,128)(2,1)} %bitcast.31), calls=%async_computation | async-start | bytes 4194304 | tf_op jit(solution)/shard_map/all_to_all | solution.py:380
  50.3 0.8 copy-start.4
  51.1 4.6 %copy-start.5 = (s16[1,272,768]{2,1,0:T(8,128)(2,1)S(1)}, s16[1,272,768]{2,1,0:T(8,128)(2,1)}, u32[]{:S(2)}) copy-start(s16[1,272,768]{2,1,0:T(8,128)(2,1)} %copy-done.4) | copy-start | bytes 1253380
  51.1 54.6 %all-to-all-start.1 = ((bf16[16,64,1024]{2,1,0:T(8,128)(2,1)}), bf16[16,64,1024]{2,1,0:T(8,128)(2,1)}, u32[]{:S(2)}, u32[]{:S(2)}) async-start(bf16[16,64,1024]{2,1,0:T(8,128)(2,1)} %bitcast.30), calls=%async_computation.1 | async-start | bytes 4194304 | tf_op jit(solution)/shard_map/all_to_all | solution.py:380
  55.6 33.9 %collective-permute-start.4 = (s16[1,272,768]{2,1,0:T(8,128)(2,1)S(1)}, s16[1,272,768]{2,1,0:T(8,128)(2,1)}, u32[]{:S(2)}, u32[]{:S(2)}) collective-permute-start(s16[1,272,768]{2,1,0:T(8,128)(2,1)S(1)} %copy-done.5), channel_id=1, source_target_pairs={{0,2},{1,3},{2,0},{3,1},{4,6},{5,7},{6,4},{7,5},{8,10},{9,11},{10,... | collective-permute-start | bytes 1253384 | tf_op jit(solution)/shard_map/ppermute | solution.py:370
  67.7 48.5 %collective-permute-start.3 = (s16[1,272,768]{2,1,0:T(8,128)(2,1)}, s16[1,272,768]{2,1,0:T(8,128)(2,1)S(1)}, u32[]{:S(2)}, u32[]{:S(2)}) collective-permute-start(s16[1,272,768]{2,1,0:T(8,128)(2,1)} %coded_sum.7), channel_id=1, source_target_pairs={{0,2},{1,3},{2,0},{3,1},{4,6},{5,7},{6,4},{7,5},{8,10},{9,11},{10,... | collective-permute-start | bytes 1253384 | tf_op jit(solution)/shard_map/ppermute | solution.py:370
  68.0 58.2 %collective-permute-start.2 = (s16[1,272,768]{2,1,0:T(8,128)(2,1)}, s16[1,272,768]{2,1,0:T(8,128)(2,1)S(1)}, u32[]{:S(2)}, u32[]{:S(2)}) collective-permute-start(s16[1,272,768]{2,1,0:T(8,128)(2,1)} %coded_sum.6), channel_id=1, source_target_pairs={{0,2},{1,3},{2,0},{3,1},{4,6},{5,7},{6,4},{7,5},{8,10},{9,11},{10,... | collective-permute-start | bytes 1253384 | tf_op jit(solution)/shard_map/ppermute | solution.py:370
  70.6 63.5 %collective-permute-start.1 = (s16[1,272,768]{2,1,0:T(8,128)(2,1)}, s16[1,272,768]{2,1,0:T(8,128)(2,1)S(1)}, u32[]{:S(2)}, u32[]{:S(2)}) collective-permute-start(s16[1,272,768]{2,1,0:T(8,128)(2,1)} %coded_sum.5), channel_id=1, source_target_pairs={{0,2},{1,3},{2,0},{3,1},{4,6},{5,7},{6,4},{7,5},{8,10},{9,11},{10,... | collective-permute-start | bytes 1253384 | tf_op jit(solution)/shard_map/ppermute | solution.py:370
  110.4 1.7 copy-start
  116.1 34.1 %collective-permute-start.7 = (s16[272,768]{1,0:T(8,128)(2,1)}, s16[272,768]{1,0:T(8,128)(2,1)}, u32[]{:S(2)}, u32[]{:S(2)}) collective-permute-start(s16[272,768]{1,0:T(8,128)(2,1)} %bitcast.28), channel_id=1, source_target_pairs={{0,1},{1,0},{2,3},{3,2},{4,5},{5,4},{6,7},{7,6},{8,9},{9,8},{10,11... | collective-permute-start | bytes 1253384 | tf_op jit(solution)/shard_map/ppermute | solution.py:370
  116.2 0.8 copy-start.11
  126.2 0.8 copy-start.10
  134.1 0.8 copy-start.9
  139.3 4.0 %collective-permute-start.5 = (f32[1]{0:T(128)}, f32[1]{0:T(128)}, u32[]{:S(2)}, u32[]{:S(2)}) collective-permute-start(f32[1]{0:T(128)} %get-tuple-element.38), channel_id=1, source_target_pairs={{0,1},{1,0},{2,3},{3,2},{4,5},{5,4},{6,7},{7,6},{8,9},{9,8},{10,11... | collective-permute-start | bytes 20 | tf_op jit(solution)/shard_map/ppermute | solution.py:370
  139.4 11.0 %collective-permute-start.8 = (s16[272,768]{1,0:T(8,128)(2,1)}, s16[272,768]{1,0:T(8,128)(2,1)}, u32[]{:S(2)}, u32[]{:S(2)}) collective-permute-start(s16[272,768]{1,0:T(8,128)(2,1)} %bitcast.7.refs_0_), channel_id=1, source_target_pairs={{0,1},{1,0},{2,3},{3,2},{4,5},{5,4},{6,7},{7,6},{8,9},{9,8},{10,11... | collective-permute-start | bytes 1253384 | tf_op jit(solution)/shard_map/ppermute | solution.py:370
  144.5 5.1 %collective-permute-start.6 = (f32[1]{0:T(128)}, f32[1]{0:T(128)}, u32[]{:S(2)}, u32[]{:S(2)}) collective-permute-start(f32[1]{0:T(128)} %max.6), channel_id=1, source_target_pairs={{0,2},{1,3},{2,0},{3,1},{4,6},{5,7},{6,4},{7,5},{8,10},{9,11},{10,... | collective-permute-start | bytes 20 | tf_op jit(solution)/shard_map/ppermute | solution.py:370
  150.1 1.9 copy-start.1
  153.0 35.7 %collective-permute-start.9 = (bf16[512,768]{1,0:T(8,128)(2,1)}, bf16[512,768]{1,0:T(8,128)(2,1)S(1)}, u32[]{:S(2)}, u32[]{:S(2)}) collective-permute-start(bf16[512,768]{1,0:T(8,128)(2,1)} %scale.1.refs_0_), channel_id=1, source_target_pairs={{0,2},{1,3},{2,0},{3,1},{4,6},{5,7},{6,4},{7,5},{8,10},{9,11},{10,... | collective-permute-start | bytes 2359304 | tf_op jit(solution)/shard_map/ppermute | solution.py:370
  156.3 64.1 %collective-permute-start.15 = (bf16[512,768]{1,0:T(8,128)(2,1)}, bf16[512,768]{1,0:T(8,128)(2,1)S(1)}, u32[]{:S(2)}, u32[]{:S(2)}) collective-permute-start(bf16[512,768]{1,0:T(8,128)(2,1)} %scale.1.refs_0_), channel_id=1, source_target_pairs={{0,1},{1,0},{2,3},{3,2},{4,5},{5,4},{6,7},{7,6},{8,9},{9,8},{10,11... | collective-permute-start | bytes 2359304 | tf_op jit(solution)/shard_map/ppermute | solution.py:370
  188.6 0.9 copy-start.2
  189.5 30.9 %collective-permute-start.12 = (s16[272,768]{1,0:T(8,128)(2,1)}, s16[272,768]{1,0:T(8,128)(2,1)S(1)}, u32[]{:S(2)}, u32[]{:S(2)}) collective-permute-start(s16[272,768]{1,0:T(8,128)(2,1)} %gate.12.piece), channel_id=1, source_target_pairs={{0,2},{1,3},{2,0},{3,1},{4,6},{5,7},{6,4},{7,5},{8,10},{9,11},{10,... | collective-permute-start | bytes 1253384 | tf_op jit(solution)/shard_map/ppermute | solution.py:370
  189.5 38.5 %collective-permute-start.10 = (s16[272,768]{1,0:T(8,128)(2,1)}, s16[272,768]{1,0:T(8,128)(2,1)S(1)}, u32[]{:S(2)}, u32[]{:S(2)}) collective-permute-start(s16[272,768]{1,0:T(8,128)(2,1)} %gate.11.piece), channel_id=1, source_target_pairs={{0,2},{1,3},{2,0},{3,1},{4,6},{5,7},{6,4},{7,5},{8,10},{9,11},{10,... | collective-permute-start | bytes 1253384 | tf_op jit(solution)/shard_map/ppermute | solution.py:370
  192.5 49.3 %collective-permute-start.14 = (bf16[512,768]{1,0:T(8,128)(2,1)}, bf16[512,768]{1,0:T(8,128)(2,1)S(1)}, u32[]{:S(2)}, u32[]{:S(2)}) collective-permute-start(bf16[512,768]{1,0:T(8,128)(2,1)} %copy-done.2), channel_id=1, source_target_pairs={{0,1},{1,0},{2,3},{3,2},{4,5},{5,4},{6,7},{7,6},{8,9},{9,8},{10,11... | collective-permute-start | bytes 2359304 | tf_op jit(solution)/shard_map/ppermute | solution.py:370
  220.4 0.8 copy-start.7
  220.4 23.3 %collective-permute-start.13 = (s16[272,768]{1,0:T(8,128)(2,1)S(1)}, s16[272,768]{1,0:T(8,128)(2,1)S(1)}, u32[]{:S(2)}, u32[]{:S(2)}) collective-permute-start(s16[272,768]{1,0:T(8,128)(2,1)S(1)} %collective-permute-done.12.refs_1_.piece), channel_id=1, source_target_pairs={{0,1},{1,0},{2,3},{3,2},{4,5},{5,4},{6,7},{7,6},{8,9},{9,8},{10,11... | collective-permute-start | bytes 1253384 | tf_op jit(solution)/shard_map/ppermute | solution.py:370
  221.2 6.8 %copy-start.6 = (s16[272,768]{1,0:T(8,128)(2,1)S(1)}, s16[272,768]{1,0:T(8,128)(2,1)}, u32[]{:S(2)}) copy-start(s16[272,768]{1,0:T(8,128)(2,1)} %gate.12.piece) | copy-start | bytes 1253380
  228.0 17.8 %collective-permute-start.11 = (s16[272,768]{1,0:T(8,128)(2,1)S(1)}, s16[272,768]{1,0:T(8,128)(2,1)S(1)}, u32[]{:S(2)}, u32[]{:S(2)}) collective-permute-start(s16[272,768]{1,0:T(8,128)(2,1)S(1)} %collective-permute-done.10.piece), channel_id=1, source_target_pairs={{0,1},{1,0},{2,3},{3,2},{4,5},{5,4},{6,7},{7,6},{8,9},{9,8},{10,11... | collective-permute-start | bytes 1253384 | tf_op jit(solution)/shard_map/ppermute | solution.py:370
  229.4 1.9 copy-start.3
  231.3 2.0 copy-start.8
